TPU v7x, 32 devices: a whole 2x2x4 slice. The times are simulated.
32 devices in a mesh: obj: 4 (over x, core), mem: 8 (over z, y).
Axes of the slice: x: 2, y: 2, z: 4, core: 2. Of those that a mesh axis runs over, the one named last changes fastest.
Arguments:
- features: bfloat16 [2048, 512], P(('obj', 'mem')), may hold values from -6 to 6
- labels: int32 [2048], P('obj'), may hold values from 0 to 127
- block_weight: float32 [512, 512], replicated, may hold values from -0.25 to 0.25
- block_first: float32 [512, 512], replicated, may hold values from -3 to 3
- block_second: float32 [512, 512], replicated, may hold values from 0.04 to 0.16
- member_vectors: float32 [3, 8, 512], replicated, may hold values from -0.5 to 3.5, as said below
- vectors_first: float32 [3, 8, 512], replicated, may hold values from -0.625 to 0.625
- vectors_second: float32 [3, 8, 512], replicated, may hold values from 0.0016 to 0.0064
- head_weight: float32 [8, 512, 128], P('mem'), may hold values from -0.5 to 0.5
- head_first: float32 [8, 512, 128], P('mem'), may hold values from -0.75 to 0.75
- head_second: float32 [8, 512, 128], P('mem'), may hold values from 0.0025 to 0.01
- head_bias: float32 [8, 128], P('mem'), may hold values from -4 to 4
- bias_first: float32 [8, 128], P('mem'), may hold values from -1.25 to 1.25
- bias_second: float32 [8, 128], P('mem'), may hold values from 0.008 to 0.032
Outputs:
- mean_logits: float32 [2048, 128], P(('obj', 'mem'))
- features_grad: float32 [2048, 512], P(('obj', 'mem'))
- grad_norm: float32 [], replicated
- block_new: float32 [512, 512], replicated
- block_first_new: float32 [512, 512], replicated
- block_second_new: float32 [512, 512], replicated
- block_copy: bfloat16 [512, 512], replicated
- vectors_new: float32 [3, 8, 512], replicated
- vectors_first_new: float32 [3, 8, 512], replicated
- vectors_second_new: float32 [3, 8, 512], replicated
- head_new: float32 [8, 512, 128], P('mem')
- head_first_new: float32 [8, 512, 128], P('mem')
- head_second_new: float32 [8, 512, 128], P('mem')
- head_copy: bfloat16 [8, 512, 128], P('mem')
- bias_new: float32 [8, 128], P('mem')
- bias_first_new: float32 [8, 128], P('mem')
- bias_second_new: float32 [8, 128], P('mem')
Inputs may be any that keep to these rules, and one draw needn't show every extreme that they name: `member_vectors`: entries of r and s are positive; b lies within -0.5 to 0.5.
All inputs are finite; a program needn't handle non-finite values.
Results may differ from a plain program's by a relative error of at most 0.012.
Values may be sent and summed in bfloat16 or wider, within the bound.
No kernel may reach another device: no remote copies, remote signals or barrier semaphores. Data moves between devices by JAX's collectives and lax.ppermute only.
A program may use at most 64 MiB of HBM per device.

v0:
```python
import jax
import jax.numpy as jnp
from jax import lax
from jax.sharding import PartitionSpec as P

STEP = 5


clip_limit = 100.0
beta_one = 0.5
beta_two = 0.5
epsilon = 1e-08


def adamw(weight, grad, first, second, rate, decay):
    first_new = beta_one * first + (1.0 - beta_one) * grad
    second_new = beta_two * second + (1.0 - beta_two) * grad * grad
    fix_one = 1.0 - beta_one**STEP
    fix_two = 1.0 - beta_two**STEP
    step_size = first_new / fix_one / (jnp.sqrt(second_new / fix_two) + epsilon)
    return (weight - rate * (step_size + decay * weight), first_new, second_new)


def loss_grad(logits, own_labels):
    classes = logits.shape[-1]
    onehot = (
        jnp.arange(classes, dtype=jnp.int32)[None, None, :] == own_labels[:, None, None]
    ).astype(jnp.float32)
    return jax.nn.softmax(logits, axis=-1) - onehot


def on_device(
    features,
    labels,
    block_weight,
    block_first,
    block_second,
    member_vectors,
    vectors_first,
    vectors_second,
    head_weight,
    head_first,
    head_second,
    head_bias,
    bias_first,
    bias_second,
):
    obj_dev, width = features.shape
    members = member_vectors.shape[1]
    scale_r = member_vectors[0]
    scale_s = member_vectors[1]
    shift_b = member_vectors[2]
    feat = features.astype(jnp.float32)
    lifted = (feat[:, None, :] * scale_r[None]).astype(jnp.bfloat16)
    flat_in = lifted.reshape(obj_dev * members, width)
    weight_low = block_weight.astype(jnp.bfloat16)
    mixed = jnp.dot(flat_in, weight_low, preferred_element_type=jnp.float32).reshape(
        obj_dev, members, width
    )
    pre = mixed * scale_s[None] + shift_b[None]
    active, gelu_back = jax.vjp(jax.nn.gelu, pre)
    hidden = active.astype(jnp.bfloat16)
    head_low = head_weight.astype(jnp.bfloat16)
    bias_low = head_bias.astype(jnp.bfloat16)
    moved = lax.all_to_all(hidden, "mem", split_axis=1, concat_axis=0, tiled=True)
    logits = (
        jnp.einsum("omd,mdc->omc", moved, head_low, preferred_element_type=jnp.float32)
        + bias_low.astype(jnp.float32)[None]
    )
    member_total = jnp.sum(logits, axis=1)
    mean_logits = (
        lax.psum_scatter(
            member_total.astype(jnp.bfloat16), "mem", scatter_dimension=0, tiled=True
        ).astype(jnp.float32)
        / members
    )
    dlogits = loss_grad(logits, labels)
    dlow = dlogits.astype(jnp.bfloat16)
    head_part = jnp.einsum("omd,omc->mdc", moved, dlow, preferred_element_type=jnp.float32)
    bias_part = jnp.sum(dlogits, axis=0)
    back_local = jnp.einsum(
        "omc,mdc->omd", dlow, head_low, preferred_element_type=jnp.float32
    ).astype(jnp.bfloat16)
    back_hidden = lax.all_to_all(back_local, "mem", split_axis=0, concat_axis=1, tiled=True)
    dpre = gelu_back(back_hidden.astype(jnp.float32))[0]
    dmixed = (dpre * scale_s[None]).astype(jnp.bfloat16).reshape(obj_dev * members, width)
    s_grad = jnp.sum(dpre * mixed, axis=0)
    b_grad = jnp.sum(dpre, axis=0)
    block_part = jnp.einsum("nd,ne->de", flat_in, dmixed, preferred_element_type=jnp.float32)
    dlifted = jnp.einsum(
        "ne,de->nd", dmixed, weight_low, preferred_element_type=jnp.float32
    ).reshape(obj_dev, members, width)
    features_grad = jnp.sum(dlifted * scale_r[None], axis=1)
    r_grad = jnp.sum(dlifted * feat[:, None, :], axis=0)
    vectors_part = jnp.stack([r_grad, s_grad, b_grad])
    head_grad, bias_grad = lax.psum((head_part, bias_part), "obj")
    head_squares = jnp.sum(head_grad * head_grad) + jnp.sum(bias_grad * bias_grad)
    block_grad, vectors_grad = lax.psum((block_part, vectors_part), ("obj", "mem"))
    head_total = lax.psum(head_squares, "mem")
    squares = jnp.sum(block_grad * block_grad) + jnp.sum(vectors_grad * vectors_grad) + head_total
    grad_norm = jnp.sqrt(squares)
    factor = clip_limit / jnp.maximum(grad_norm, clip_limit)
    block_new, block_m, block_v = adamw(
        block_weight, block_grad * factor, block_first, block_second, 0.02, 0.01
    )
    vectors_new, vectors_m, vectors_v = adamw(
        member_vectors, vectors_grad * factor, vectors_first, vectors_second, 0.5, 0.0
    )
    head_new, head_m, head_v = adamw(
        head_weight, head_grad * factor, head_first, head_second, 0.02, 0.01
    )
    bias_new, bias_m, bias_v = adamw(
        head_bias, bias_grad * factor, bias_first, bias_second, 0.1, 0.0
    )
    return (
        mean_logits,
        features_grad,
        grad_norm,
        block_new,
        block_m,
        block_v,
        block_new.astype(jnp.bfloat16),
        vectors_new,
        vectors_m,
        vectors_v,
        head_new,
        head_m,
        head_v,
        head_new.astype(jnp.bfloat16),
        bias_new,
        bias_m,
        bias_v,
    )


def solution(mesh):
    return jax.shard_map(
        on_device,
        mesh=mesh,
        in_specs=(
            P(("obj", "mem"), None),
            P("obj"),
            P(),
            P(),
            P(),
            P(),
            P(),
            P(),
            P("mem", None, None),
            P("mem", None, None),
            P("mem", None, None),
            P("mem", None),
            P("mem", None),
            P("mem", None),
        ),
        out_specs=(
            P(("obj", "mem"), None),
            P(("obj", "mem"), None),
            P(),
            P(),
            P(),
            P(),
            P(),
            P(),
            P(),
            P(),
            P("mem", None, None),
            P("mem", None, None),
            P("mem", None, None),
            P("mem", None, None),
            P("mem", None),
            P("mem", None),
            P("mem", None),
        ),
        check_vma=False,
    )
```

profile of v0, /device:TPU:0, one launch (start us, length us, event | category | flops | bytes accessed | tf_op | source)
XLA Modules:
  0.0 265.3 jit_solution(2164600707499557619)
XLA Ops:
  8.0 0.8 slice_bitcast_fusion.1
  8.8 0.0 copy-done.15
  8.9 0.6 copy-done.9
  9.5 0.0 copy-done.11
  9.5 1.9 multiply_convert_fusion.1
  11.4 0.9 copy.39
  12.4 7.4 %all-to-all-start = ((bf16[64,8,512]{2,0,1:T(8,128)(2,1)}), bf16[64,8,512]{2,0,1:T(8,128)(2,1)S(1)}, u32[]{:S(2)}, u32[]{:S(2)}) async-start(bf16[64,8,512]{2,0,1:T(8,128)(2,1)} %copy.39), calls=%async_computation | async-start | bytes 1048576 | tf_op jit(solution)/shard_map/all_to_all | solution.py:65
  19.8 0.0 copy-done.18
  19.8 14.5 %all-to-all-done = bf16[64,8,512]{2,0,1:T(8,128)(2,1)S(1)} async-done(((bf16[64,8,512]{2,0,1:T(8,128)(2,1)}), bf16[64,8,512]{2,0,1:T(8,128)(2,1)S(1)}, u32[]{:S(2)}, u32[]{:S(2)}) %all-to-all-start) | async-done | bytes 524320 | tf_op jit(solution)/shard_map/all_to_all | solution.py:65
  34.3 0.0 copy-done.4
  34.3 0.3 fusion.42
  34.6 0.0 copy-start.17
  34.6 0.1 fusion.23
  34.7 0.6 copy-done.17
  35.3 0.3 fusion
  35.6 0.5 broadcast.125
  36.1 1.0 reduce.5
  37.2 1.2 reshape.128
  38.3 3.6 %all-to-all-start.1 = ((bf16[8,2,16384]{2,1,0:T(2,128)(2,1)}), bf16[8,2,16384]{2,1,0:T(2,128)(2,1)S(1)}, u32[]{:S(2)}, u32[]{:S(2)}) async-start(bf16[8,2,16384]{2,1,0:T(2,128)(2,1)} %reshape.128), calls=%async_computation.1 | async-start | bytes 1048576 | tf_op jit(solution)/shard_map/all_to_all | solution.py:84
  42.0 0.0 all-reduce.5.cloned.1.call-start
  42.0 1.0 convolution_bitcast_fusion.1
  43.1 0.0 all-reduce.5.cloned.1.call-update
  43.1 0.0 reduce-scatter.4.cloned.1.call-start
  43.1 0.8 copy.44
  43.9 0.0 reduce-scatter.4.cloned.1.call-update
  43.9 0.0 all-reduce.3.cloned.1.call-start
  44.0 0.2 fusion.34
  44.1 6.8 %psum.38 = f32[1,128]{1,0:T(1,128)S(1)} all-reduce(f32[1,128]{1,0:T(1,128)S(1)} %bitcast.96), channel_id=1, replica_groups=mesh['obj'=4,'mem'=8] {'obj'}, use_global_device_ids=true, to_apply=%region_14.0 | all-reduce | flops 128 | bytes 1024 | tf_op jit(solution)/shard_map/psum | solution.py:96
  50.9 0.6 multiply_reduce_fusion.6
  51.5 0.0 copy-done.22
  51.5 27.7 %all-reduce.5.cloned.1.call-done = f32[1,512,128]{2,1,0:T(8,128)} async-done(((f32[1,512,128]{2,1,0:T(8,128)}), f32[1,512,128]{2,1,0:T(8,128)}) %all-reduce.5.cloned.1.call-update) | async-done | bytes 262160 | tf_op jit(solution)/shard_map/psum | solution.py:96
  79.2 1.6 multiply_reduce_fusion.4
  82.1 21.9 %psum.39 = f32[]{:T(128)} all-reduce(f32[]{:T(128)S(6)} %add.121), channel_id=1, replica_groups=mesh['obj'=4,'mem'=8] {'mem'}, use_global_device_ids=true, to_apply=%region_16.0 | all-reduce | flops 1 | bytes 8 | tf_op jit(solution)/shard_map/psum | solution.py:99
  104.0 6.4 %reduce-scatter.4.cloned.1.call-done = bf16[64,128]{1,0:T(8,128)(2,1)} async-done(((bf16[512,128]{1,0:T(8,128)(2,1)}), bf16[64,128]{1,0:T(8,128)(2,1)}) %reduce-scatter.4.cloned.1.call-update) | async-done | bytes 16400
  110.4 1.4 copy.45
  111.9 0.0 all-to-all-done.1
  111.9 0.5 reshape.129
  112.4 0.0 copy-start.12
  112.4 0.1 bitcast_convert_fusion.1
  112.5 0.6 copy-done.12
  113.1 1.7 multiply_reduce_fusion
  114.8 0.0 copy-done.10
  114.8 1.5 convolution_bitcast_fusion
  116.3 0.0 all-reduce.3.cloned.1.call-update
  116.3 0.7 copy.43
  117.0 0.5 copy-done
  117.5 2.2 multiply_reduce_fusion.1
  119.7 40.7 %psum.36 = f32[3,8,512]{2,1,0:T(8,128)S(1)} all-reduce(f32[3,8,512]{2,1,0:T(8,128)S(1)} %pad_maximum_fusion), channel_id=1, replica_groups=mesh['obj'=4,'mem'=8] {'obj','mem'}, use_global_device_ids=true, to_apply=%region_9.0 | all-reduce | flops 12288 | bytes 98304 | tf_op jit(solution)/shard_map/psum | solution.py:98
  160.4 0.6 multiply_reduce_fusion.5
  161.0 84.5 %all-reduce.3.cloned.1.call-done = f32[512,512]{1,0:T(8,128)} async-done(((f32[512,512]{1,0:T(8,128)}), f32[512,512]{1,0:T(8,128)}) %all-reduce.3.cloned.1.call-update) | async-done | bytes 1048592 | tf_op jit(solution)/shard_map/psum | solution.py:98
  245.5 2.2 multiply_reduce_fusion.2
  249.7 0.0 copy-done.7
  249.7 0.0 copy-done.16
  249.7 0.0 copy-start.19
  249.8 0.0 copy-start.20
  249.8 0.0 copy-start.21
  249.8 0.0 copy-start.23
  249.8 1.5 multiply_subtract_fusion.2
  251.3 0.0 copy-done.19
  251.3 0.5 multiply_subtract_fusion.3
  251.8 0.0 copy-done.1
  251.9 0.0 copy-start.6
  251.9 3.8 %fusion.39 = (bf16[512,512]{1,0:T(8,128)(2,1)}, f32[512,512]{1,0:T(8,128)}, f32[512,512]{1,0:T(8,128)}, f32[512,512]{1,0:T(8,128)}) fusion(f32[512,512]{1,0:T(8,128)S(1)} %copy-done, f32[512,512]{1,0:T(8,128)S(1)} %copy-done.1, f32[]{:T(128)S(6)} %div.61, f32[512,512]{1,0:T(8,128)S(1)} %copy-done.2, f32[512,512]{1,0:T(8,128)} %param.18), kind=kLoop, calls=%fused_computation.77 | loop fusion | flops 4194304 | bytes 7864324 | tf_op jit(solution)/shard_map/convert_element_type | solution.py:122
  255.6 1.1 fusion.36
  (31 shorter events, 0.1 us)
Async XLA Ops:
  8.0 0.8 copy-start.15
  8.9 0.6 copy-start.9
  8.9 0.6 copy-start.11
  12.4 7.4 %copy-start.18 = (f32[1,128]{1,0:T(1,128)S(1)}, f32[1,128]{1,0:T(1,128)}, u32[]{:S(2)}) copy-start(f32[1,128]{1,0:T(1,128)} %param.25) | copy-start | bytes 1540
  12.4 21.9 %copy-start.4 = (f32[1,512,128]{2,1,0:T(8,128)S(1)}, f32[1,512,128]{2,1,0:T(8,128)}, u32[]{:S(2)}) copy-start(f32[1,512,128]{2,1,0:T(8,128)} %param.22) | copy-start | bytes 786436
  12.4 21.9 %all-to-all-start = ((bf16[64,8,512]{2,0,1:T(8,128)(2,1)}), bf16[64,8,512]{2,0,1:T(8,128)(2,1)S(1)}, u32[]{:S(2)}, u32[]{:S(2)}) async-start(bf16[64,8,512]{2,0,1:T(8,128)(2,1)} %copy.39), calls=%async_computation | async-start | bytes 1048576 | tf_op jit(solution)/shard_map/all_to_all | solution.py:65
  34.6 0.7 copy-start.17
  38.3 73.5 %all-to-all-start.1 = ((bf16[8,2,16384]{2,1,0:T(2,128)(2,1)}), bf16[8,2,16384]{2,1,0:T(2,128)(2,1)S(1)}, u32[]{:S(2)}, u32[]{:S(2)}) async-start(bf16[8,2,16384]{2,1,0:T(2,128)(2,1)} %reshape.128), calls=%async_computation.1 | async-start | bytes 1048576 | tf_op jit(solution)/shard_map/all_to_all | solution.py:84
  42.0 37.3 %all-reduce.5.cloned.1.call-start = ((), (), s32[]{:S(2)}) async-start(), calls=%async_computation.4 | async-start | bytes 524288 | tf_op jit(solution)/shard_map/psum | solution.py:96
  43.1 67.3 %reduce-scatter.4.cloned.1.call-start = ((), (), s32[]{:S(2)}) async-start(), calls=%async_computation.5 | async-start | bytes 147456
  43.9 201.6 %all-reduce.3.cloned.1.call-start = ((), (), s32[]{:S(2)}) async-start(), calls=%async_computation.3 | async-start | bytes 2097152 | tf_op jit(solution)/shard_map/psum | solution.py:98
  50.9 0.6 copy-start.22
  112.4 0.7 copy-start.12
  113.1 1.7 copy-start.10
  114.8 1.5 copy-start.8
  116.3 1.2 copy-start
  117.5 2.2 copy-start.13
  117.5 2.2 copy-start.14
  117.5 134.3 %copy-start.2 = (f32[512,512]{1,0:T(8,128)S(1)}, f32[512,512]{1,0:T(8,128)}, u32[]{:S(2)}) copy-start(f32[512,512]{1,0:T(8,128)} %param.17) | copy-start | bytes 3145732
  161.0 88.7 %copy-start.7 = (f32[3,8,512]{2,1,0:T(8,128)S(1)}, f32[3,8,512]{2,1,0:T(8,128)}, u32[]{:S(2)}) copy-start(f32[3,8,512]{2,1,0:T(8,128)} %param.19) | copy-start | bytes 147460
  161.0 88.7 %copy-start.16 = (f32[3,8,512]{2,1,0:T(8,128)S(1)}, f32[3,8,512]{2,1,0:T(8,128)}, u32[]{:S(2)}) copy-start(f32[3,8,512]{2,1,0:T(8,128)} %param.20) | copy-start | bytes 147460
  245.5 6.3 %copy-start.1 = (f32[512,512]{1,0:T(8,128)S(1)}, f32[512,512]{1,0:T(8,128)}, u32[]{:S(2)}) copy-start(f32[512,512]{1,0:T(8,128)} %all-reduce.3.cloned.1.call-done) | copy-start | bytes 3145732
  249.7 1.5 copy-start.19
  249.8 1.5 copy-start.20
  249.8 1.5 copy-start.21
  249.8 1.5 copy-start.23
  251.8 3.8 %copy-start.3 = (f32[1,512,128]{2,1,0:T(8,128)S(1)}, f32[1,512,128]{2,1,0:T(8,128)}, u32[]{:S(2)}) copy-start(f32[1,512,128]{2,1,0:T(8,128)} %all-reduce.5.cloned.1.call-done) | copy-start | bytes 786436
  251.8 3.8 %copy-start.5 = (f32[1,512,128]{2,1,0:T(8,128)S(1)}, f32[1,512,128]{2,1,0:T(8,128)}, u32[]{:S(2)}) copy-start(f32[1,512,128]{2,1,0:T(8,128)} %param.23) | copy-start | bytes 786436
  251.9 3.8 %copy-start.6 = (f32[1,512,128]{2,1,0:T(8,128)S(1)}, f32[1,512,128]{2,1,0:T(8,128)}, u32[]{:S(2)}) copy-start(f32[1,512,128]{2,1,0:T(8,128)} %param.24) | copy-start | bytes 786436
Sparse Core Ops, SparseCore 0:
  45.7 33.4 all-reduce.4
  116.4 129.0 all-reduce.2
Sparse Core Ops, SparseCore 1:
  47.5 62.9 reduce-scatter.3
where the time goes:
time: 266 us; the launch traced here: 265 us
  waiting for transfers between devices  133 us (50%)
  blocking collectives  69.4 us (26%)
  between operations  20.2 us (8%)
  other arithmetic  15 us (6%)
  starting transfers between devices  11.2 us (4%)
  local copies, waits for them, and re-layouts  9.23 us (3%)
  matrix products  7.24 us (3%)
    psum x1, waiting for transfers between devices, on_device(): lax.psum((block_part, vectors_part), ('obj', 'mem'))  84.5 us
    psum x1, blocking collectives, on_device(): lax.psum((block_part, vectors_part), ('obj', 'mem'))  40.7 us
    psum x1, waiting for transfers between devices, on_device(): head_grad, bias_grad = lax.psum((head_part, bias_part), 'obj')  27.7 us
    psum x1, blocking collectives, on_device(): head_total = lax.psum(head_squares, 'mem')  21.9 us
    all_to_all x1, waiting for transfers between devices, on_device(): lax.all_to_all(hidden, 'mem', split_axis=1, concat_axis=0, tiled=True)  14.5 us
    all_to_all x1, starting transfers between devices, on_device(): lax.all_to_all(hidden, 'mem', split_axis=1, concat_axis=0, tiled=True)  7.42 us
    unnamed x53, local copies, waits for them, and re-layouts  6.98 us
    psum x1, blocking collectives, on_device(): head_grad, bias_grad = lax.psum((head_part, bias_part), 'obj')  6.77 us
  transfers between devices with their start and end apart: 5, of which 4 were waited for; matrix products, arithmetic and copies ran while one was open for 3% of the time, Pallas kernels for 0%

commit v1 on v0

v1 whole, which is shorter than its diff:
```python
import functools
import math

import jax
import jax.numpy as jnp
from jax import lax
from jax.experimental import pallas as pl
from jax.experimental.pallas import tpu as pltpu
from jax.sharding import PartitionSpec as P

STEP = 5
ALL = ("obj", "mem")
LANES = 128
PAD = 16
MIB = 1 << 20

clip_limit = 100.0
beta_one = 0.5
beta_two = 0.5
epsilon = 1e-08
gelu_in = math.sqrt(2.0 / math.pi)
gelu_cube = 0.044715

bf16 = jnp.bfloat16
f32 = jnp.float32
VMEM = pl.BlockSpec(memory_space=pltpu.VMEM)
SMEM = pl.BlockSpec(memory_space=pltpu.SMEM)


def adamw(weight, grad, first, second, rate, decay):
    first_new = beta_one * first + (1.0 - beta_one) * grad
    second_new = beta_two * second + (1.0 - beta_two) * grad * grad
    fix_one = 1.0 - beta_one**STEP
    fix_two = 1.0 - beta_two**STEP
    step_size = first_new / fix_one / (jnp.sqrt(second_new / fix_two) + epsilon)
    return (weight - rate * (step_size + decay * weight), first_new, second_new)


def dot(a, b, dims=((1,), (0,))):
    return lax.dot_general(a, b, (dims, ((), ())), preferred_element_type=f32)


def call(body, outs, args, scratch=(), name=None):
    specs = [SMEM] + [VMEM] * (len(args) - 1)
    return pl.pallas_call(
        body,
        out_shape=outs,
        in_specs=specs,
        out_specs=jax.tree.map(lambda _: VMEM, outs),
        scratch_shapes=list(scratch),
        compiler_params=pltpu.CompilerParams(vmem_limit_bytes=40 * MIB),
        name=name,
    )(*args)


class Plan:
    def __init__(self, mesh, width, classes, rows):
        self.n_obj, self.n_mem = mesh.shape["obj"], mesh.shape["mem"]
        self.outer = self.n_mem // 2
        self.quads = self.n_obj
        self.shards = 2 * self.quads
        self.width, self.classes, self.rows = width, classes, rows
        self.groups = width // LANES
        self.block_rows = width // self.shards
        self.stacked = self.block_rows * self.groups
        self.items = max(8, self.shards)

    def perm(self, move):
        pairs = []
        for obj in range(self.n_obj):
            for mem in range(self.n_mem):
                to_obj, to_mem = move(obj, mem)
                pairs.append((obj * self.n_mem + mem, to_obj * self.n_mem + to_mem))
        return pairs

    def over_core(self, v):
        return lax.ppermute(v, ALL, self.perm(lambda o, m: (o ^ 1, m)))

    def over_plane(self, v, k):
        return lax.ppermute(v, ALL, self.perm(lambda o, m: (o ^ (k >> 1 << 1), m ^ (k & 1))))

    def over_outer(self, v, k):
        return lax.ppermute(v, ALL, self.perm(lambda o, m: (o, m ^ (k << 1))))


def local_body(plan, place, *refs):
    n = plan.outer
    feats = refs[:n]
    onehot_ref, weight_ref, vec_ref, own_head, own_bias, far_head = refs[n : n + 6]
    send_ref, keep_ref = refs[n + 6 : n + 8]
    back_own = refs[n + 8]
    back_far = refs[n + 9 : n + 8 + n]
    lifted_ref, mixed_ref, hidden_ref, slope_ref, dmixed_ref, block_ref, heads_ref, items_ref = refs[
        n + 8 + n :
    ]
    rows, width, classes = plan.rows, plan.width, plan.classes
    objs = n * rows
    core, quad, outer, inner = place[0], place[1], place[2], place[3]
    tile = 16

    for j in range(2):
        scale_r = vec_ref[j : j + 1, :]
        for k in range(n):
            lifted_ref[j * objs + k * rows : j * objs + (k + 1) * rows, :] = (
                feats[k][...].astype(f32) * scale_r
            ).astype(bf16)
    mixed_ref[...] = dot(lifted_ref[...], weight_ref[...])

    items_ref[...] = jnp.zeros_like(items_ref)
    for j in range(2):
        scale_s = vec_ref[2 + j : 3 + j, :]
        shift_b = vec_ref[4 + j : 5 + j, :]

        def forward(t, carry):
            at = pl.ds(pl.multiple_of(j * objs + t * tile, tile), tile)
            pre = mixed_ref[at, :] * scale_s + shift_b
            square = pre * pre
            bend = jnp.tanh(gelu_in * (pre + gelu_cube * square * pre))
            hidden_ref[at, :] = (0.5 * pre * (1.0 + bend)).astype(bf16)
            slope_ref[at, :] = 0.5 * (1.0 + bend) + (0.5 * gelu_in) * pre * (1.0 - bend * bend) * (
                1.0 + (3.0 * gelu_cube) * square
            )
            return carry

        lax.fori_loop(0, objs // tile, forward, 0, unroll=2)

    logit_sum = None
    for j in range(2):
        mine = inner == j
        head = jnp.where(mine, own_head[...], far_head[0:width, :])
        bias = jnp.where(mine, own_bias[0:1, :], far_head[width : width + 1, :]).astype(f32)
        hidden = hidden_ref[j * objs : (j + 1) * objs, :]
        logits = dot(hidden, head) + bias
        logit_sum = logits if logit_sum is None else logit_sum + logits
        top = jnp.max(logits, axis=-1, keepdims=True)
        grown = jnp.exp(logits - top)
        soft = grown / jnp.sum(grown, axis=-1, keepdims=True)
        hot = jnp.concatenate(
            [
                onehot_ref[pl.ds(pl.multiple_of(((outer ^ k) * 2 + inner) * rows, rows), rows), :]
                for k in range(n)
            ],
            axis=0,
        )
        dlogits = soft - hot
        dlow = dlogits.astype(bf16)
        items_ref[6 + j, 0:1, :] = jnp.sum(dlogits, axis=0, keepdims=True)
        heads_ref[j] = dot(hidden, dlow, ((0,), (0,)))
        mixed_back = dot(dlow, head, ((1,), (1,)))
        block_ref[0:objs, :] = mixed_back
        scale_s = vec_ref[2 + j : 3 + j, :]

        def backward(t, carry):
            s_sum, b_sum = carry
            at = pl.ds(pl.multiple_of(j * objs + t * tile, tile), tile)
            near = pl.ds(pl.multiple_of(t * tile, tile), tile)
            dpre = block_ref[near, :].astype(bf16).astype(f32) * slope_ref[at, :]
            dmixed_ref[at, :] = (dpre * scale_s).astype(bf16)
            return s_sum + dpre * mixed_ref[at, :], b_sum + dpre

        zero = jnp.zeros((tile, width), f32)
        s_sum, b_sum = lax.fori_loop(0, objs // tile, backward, (zero, zero), unroll=2)
        s_grad = jnp.sum(s_sum, axis=0, keepdims=True)
        b_grad = jnp.sum(b_sum, axis=0, keepdims=True)
        for g in range(plan.groups):
            at = slice(g * LANES, (g + 1) * LANES)
            items_ref[2 + j, g : g + 1, :] = s_grad[:, at]
            items_ref[4 + j, g : g + 1, :] = b_grad[:, at]

    block_ref[0:width, :] = dot(lifted_ref[...], dmixed_ref[...], ((0,), (0,)))
    slope_ref[...] = dot(dmixed_ref[...], weight_ref[...], ((1,), (1,)))
    r_sums = [jnp.zeros((1, width), f32) for _ in range(2)]
    for k in range(n):
        feat = feats[k][...].astype(f32)
        back = None
        for j in range(2):
            lift_back = slope_ref[j * objs + k * rows : j * objs + (k + 1) * rows, :]
            r_sums[j] = r_sums[j] + jnp.sum(lift_back * feat, axis=0, keepdims=True)
            part = lift_back * vec_ref[j : j + 1, :]
            back = part if back is None else back + part
        out = back_own if k == 0 else back_far[k - 1]
        out[:, 0:width] = back.astype(out.dtype)
        out[:, width : width + classes] = logit_sum[k * rows : (k + 1) * rows, :].astype(out.dtype)
    for j in range(2):
        for g in range(plan.groups):
            items_ref[j, g : g + 1, :] = r_sums[j][:, g * LANES : (g + 1) * LANES]

    stride = plan.block_rows
    for out, side in ((keep_ref, core), (send_ref, 1 - core)):
        for k in range(plan.quads):
            shard = side * plan.quads + (quad ^ k)
            at = pl.ds(pl.multiple_of(shard * stride, stride), stride)
            for g in range(plan.groups):
                out[k, g * stride : (g + 1) * stride, :] = block_ref[
                    at, g * LANES : (g + 1) * LANES
                ].astype(out.dtype)
            base = plan.stacked
            for j in range(2):
                out[k, base : base + stride, :] = heads_ref[j, at, :].astype(out.dtype)
                base += stride
            out[k, base : base + PAD, :] = items_ref[shard].astype(out.dtype)


def core_body(plan, place, keep_ref, got_ref, own_ref, *send_refs):
    own_ref[...] = keep_ref[0] + got_ref[0].astype(f32)
    for k in range(1, plan.quads):
        send_refs[k - 1][...] = (keep_ref[k] + got_ref[k].astype(f32)).astype(bf16)


def two_parts(v):
    high = v.astype(bf16).astype(f32)
    return high, v - high


def plane_body(plan, place, own_ref, *refs):
    got, (send_ref, block_ref, head_ref) = refs[: plan.quads - 1], refs[plan.quads - 1 :]
    total = own_ref[...]
    for r in got:
        total = total + r[...].astype(f32)
    base = plan.stacked
    block_ref[0:base, :] = total[0:base, :]
    send_ref[0:base, :] = total[0:base, :].astype(bf16)
    heads = total[base : base + 2 * plan.block_rows, :]
    head_ref[...] = heads
    squares = jnp.sum(jnp.sum(heads * heads, axis=1, keepdims=True), axis=0, keepdims=True)
    high, low = two_parts(jnp.broadcast_to(squares, (PAD, LANES)))
    items = total[base + 2 * plan.block_rows :, :]
    row = lax.broadcasted_iota(jnp.int32, (PAD, LANES), 0)
    extra = jnp.where(row < plan.groups, items, jnp.where(row == plan.groups, high, low))
    block_ref[base : base + PAD, :] = extra
    send_ref[base : base + PAD, :] = extra.astype(bf16)


def outer_body(plan, place, block_ref, head_ref, *refs):
    n = plan.outer
    got, (same_ref, flip_ref) = refs[: n - 1], refs[n - 1 :]
    inner = place[3]
    base, stride, groups = plan.stacked, plan.block_rows, plan.groups
    total = block_ref[0:base, :]
    extras = [block_ref[base : base + PAD, :].astype(bf16).astype(f32)]
    for r in got:
        total = total + r[0:base, :].astype(f32)
        extras.append(r[base : base + PAD, :].astype(f32))
    row = lax.broadcasted_iota(jnp.int32, (PAD, LANES), 0)
    head_squares = jnp.zeros((1, LANES), f32)
    item_squares = jnp.zeros((PAD, LANES), f32)
    for extra in extras:
        head_squares = head_squares + extra[groups : groups + 1, :] + extra[groups + 1 : groups + 2, :]
        item_squares = item_squares + jnp.where(row < groups, extra * extra, 0.0)
    squares = (
        jnp.sum(jnp.sum(total * total, axis=1, keepdims=True), axis=0, keepdims=True)
        + jnp.sum(jnp.sum(item_squares, axis=1, keepdims=True), axis=0, keepdims=True)
        + head_squares
    )
    high, low = two_parts(jnp.broadcast_to(squares, (PAD, LANES)))
    items = jnp.concatenate([extra[0:groups, :] for extra in extras], axis=0).astype(bf16)
    sums = jnp.where(row == 0, high, low).astype(bf16)
    block = total.astype(bf16)
    for out, member in ((same_ref, inner), (flip_ref, 1 - inner)):
        at = pl.ds(pl.multiple_of(member * stride, stride), stride)
        out[0:base, :] = block
        out[base : base + groups * n, :] = items
        spot = base + groups * n
        out[spot : spot + stride, :] = head_ref[at, :].astype(bf16)
        out[spot + stride : spot + stride + PAD, :] = sums


def back_body(plan, place, own_ref, *refs):
    got, (feat_ref, mean_ref) = refs[: plan.outer - 1], refs[plan.outer - 1 :]
    total = own_ref[...]
    for r in got:
        total = total + r[...].astype(f32)
    feat_ref[...] = total[:, 0 : plan.width]
    mean_ref[...] = total[:, plan.width :] / plan.n_mem


def update_body(plan, place, *refs):
    chunks = refs[: plan.shards]
    (bw, bm, bv, vw, vm, vv, hw, hm, hv, cw, cm, cv) = refs[plan.shards : plan.shards + 12]
    (
        norm_ref,
        bw_out,
        bm_out,
        bv_out,
        bcopy_out,
        vw_out,
        vm_out,
        vv_out,
        hw_out,
        hm_out,
        hv_out,
        hcopy_out,
        cw_out,
        cm_out,
        cv_out,
        items_ref,
    ) = refs[plan.shards + 12 :]
    core, quad, outer, inner = place[0], place[1], place[2], place[3]
    n, groups, stride, base = plan.outer, plan.groups, plan.block_rows, plan.stacked
    spot = base + groups * n
    squares = jnp.zeros((1, LANES), f32)
    for chunk in chunks:
        sums = chunk[spot + stride : spot + stride + PAD, :].astype(f32)
        squares = squares + sums[0:1, :] + sums[1:2, :]
    norm = jnp.sqrt(squares)
    norm_ref[...] = norm
    factor = clip_limit / jnp.maximum(norm, clip_limit)

    for i, chunk in enumerate(chunks):
        side, k = divmod(i, plan.quads)
        shard = (core ^ side) * plan.quads + (quad ^ k)
        at = pl.ds(pl.multiple_of(shard * stride, stride), stride)
        for g in range(groups):
            lanes = slice(g * LANES, (g + 1) * LANES)
            grad = chunk[g * stride : (g + 1) * stride, :].astype(f32) * factor
            w, m, v = adamw(bw[at, lanes], grad, bm[at, lanes], bv[at, lanes], 0.02, 0.01)
            bw_out[at, lanes] = w
            bm_out[at, lanes] = m
            bv_out[at, lanes] = v
            bcopy_out[at, lanes] = w.astype(bf16)
        grad = chunk[spot : spot + stride, :].astype(f32) * factor
        w, m, v = adamw(hw[at, :], grad, hm[at, :], hv[at, :], 0.02, 0.01)
        hw_out[at, :] = w
        hm_out[at, :] = m
        hv_out[at, :] = v
        hcopy_out[at, :] = w.astype(bf16)
        items = chunk[base : base + groups * n, :].astype(f32)
        kind, member = shard // 2, shard % 2
        for z in range(n):
            items_ref[kind, (outer ^ z) * 2 + member] = items[z * groups : (z + 1) * groups, :]

    wide = jnp.concatenate([factor] * groups, axis=1)
    for t in range(3):
        grad = jnp.concatenate([items_ref[t, :, g, :] for g in range(groups)], axis=1) * wide
        w, m, v = adamw(vw[t], grad, vm[t], vv[t], 0.5, 0.0)
        vw_out[t] = w
        vm_out[t] = m
        vv_out[t] = v
    grad = items_ref[3, outer * 2 + inner, 0:1, :] * factor
    w, m, v = adamw(cw[...], grad, cm[...], cv[...], 0.1, 0.0)
    cw_out[...] = w
    cm_out[...] = m
    cv_out[...] = v


def on_device(
    mesh,
    features,
    labels,
    block_weight,
    block_first,
    block_second,
    member_vectors,
    vectors_first,
    vectors_second,
    head_weight,
    head_first,
    head_second,
    head_bias,
    bias_first,
    bias_second,
):
    rows, width = features.shape
    classes = head_weight.shape[-1]
    plan = Plan(mesh, width, classes, rows)
    n, quads, stride = plan.outer, plan.quads, plan.block_rows
    shape = jax.ShapeDtypeStruct
    obj, mem = lax.axis_index("obj"), lax.axis_index("mem")
    outer, inner = mem // 2, mem % 2
    place = jnp.stack([obj % 2, obj // 2 * 2 + inner, outer, inner]).astype(jnp.int32)

    far_feats = [plan.over_outer(features, k) for k in range(1, n)]
    head_low = head_weight[0].astype(bf16)
    bias_low = jnp.broadcast_to(head_bias.astype(bf16), (PAD, classes))
    far_head = plan.over_plane(jnp.concatenate([head_low, bias_low], axis=0), 1)
    onehot = (
        jnp.arange(classes, dtype=jnp.int32)[None, :] == labels[:, None]
    ).astype(f32)
    weight_low = block_weight.astype(bf16)
    pair = lax.dynamic_slice_in_dim(member_vectors, outer * 2, 2, axis=1).reshape(6, width)

    objs = n * rows
    total = plan.stacked + 2 * stride + PAD
    back = width + classes
    outs = call(
        functools.partial(local_body, plan),
        [
            shape((quads, total, LANES), bf16),
            shape((quads, total, LANES), f32),
            shape((rows, back), f32),
        ]
        + [shape((rows, back), bf16)] * (n - 1),
        [place, features, *far_feats, onehot, weight_low, pair, head_low, bias_low, far_head],
        [
            pltpu.VMEM((2 * objs, width), bf16),
            pltpu.VMEM((2 * objs, width), f32),
            pltpu.VMEM((2 * objs, width), bf16),
            pltpu.VMEM((2 * objs, width), f32),
            pltpu.VMEM((2 * objs, width), bf16),
            pltpu.VMEM((max(width, objs), width), f32),
            pltpu.VMEM((2, width, classes), f32),
            pltpu.VMEM((plan.items, PAD, LANES), f32),
        ],
        name="local",
    )
    send, keep, back_own, back_far = outs[0], outs[1], outs[2], outs[3:]

    got = plan.over_core(send)
    own, *sends = call(
        functools.partial(core_body, plan),
        [shape((total, LANES), f32)] + [shape((total, LANES), bf16)] * (quads - 1),
        [place, keep, got],
        name="core_sum",
    )
    got = [plan.over_plane(v, k + 1) for k, v in enumerate(sends)]
    send, block, heads = call(
        functools.partial(plane_body, plan),
        [
            shape((plan.stacked + PAD, LANES), bf16),
            shape((plan.stacked + PAD, LANES), f32),
            shape((2 * stride, LANES), f32),
        ],
        [place, own, *got],
        name="plane_sum",
    )
    got = [plan.over_outer(send, k) for k in range(1, n)]
    last = plan.stacked + plan.groups * n + stride + PAD
    same, flip = call(
        functools.partial(outer_body, plan),
        [shape((last, LANES), bf16)] * 2,
        [place, block, heads, *got],
        name="outer_sum",
    )
    near = [same] + [plan.over_plane(flip if k & 1 else same, k) for k in range(1, quads)]
    far = [plan.over_core(v) for v in near]

    back_got = [plan.over_outer(v, k + 1) for k, v in enumerate(back_far)]
    features_grad, mean_logits = call(
        functools.partial(back_body, plan),
        [shape((rows, width), f32), shape((rows, classes), f32)],
        [place, back_own, *back_got],
        name="back_sum",
    )

    like = lambda v, dtype=f32: shape(v.shape, dtype)
    head_w, head_m, head_v = head_weight[0], head_first[0], head_second[0]
    (norm, bw, bm, bv, bcopy, vw, vm, vv, hw, hm, hv, hcopy, cw, cm, cv) = call(
        functools.partial(update_body, plan),
        [shape((1, LANES), f32)]
        + [like(block_weight)] * 3
        + [like(block_weight, bf16)]
        + [like(member_vectors)] * 3
        + [like(head_w)] * 3
        + [like(head_w, bf16)]
        + [like(head_bias)] * 3,
        [
            place,
            *near,
            *far,
            block_weight,
            block_first,
            block_second,
            member_vectors,
            vectors_first,
            vectors_second,
            head_w,
            head_m,
            head_v,
            head_bias,
            bias_first,
            bias_second,
        ],
        [pltpu.VMEM((plan.items // 2, plan.n_mem, plan.groups, LANES), f32)],
        name="update",
    )
    return (
        mean_logits,
        features_grad,
        norm[0, 0],
        bw,
        bm,
        bv,
        bcopy,
        vw,
        vm,
        vv,
        hw[None],
        hm[None],
        hv[None],
        hcopy[None],
        cw,
        cm,
        cv,
    )


def solution(mesh):
    split, whole = P(ALL, None), P()
    heads, biases = P("mem", None, None), P("mem", None)
    return jax.shard_map(
        functools.partial(on_device, mesh),
        mesh=mesh,
        in_specs=(split, P("obj")) + (whole,) * 6 + (heads,) * 3 + (biases,) * 3,
        out_specs=(split, split) + (whole,) * 8 + (heads,) * 4 + (biases,) * 3,
        check_vma=False,
    )
```

time: 266 us -> 60.7 us (0.23)
  waiting for transfers between devices: 133 us -> 17.9 us
  blocking collectives: 69.4 us -> 0 us
  between operations: 20.2 us -> 0.89 us
  starting transfers between devices: 11.2 us -> 26.4 us
  other arithmetic: 15 us -> 2.59 us
  Pallas kernels: 0 us -> 11.3 us
  local copies, waits for them, and re-layouts: 9.23 us -> 1.46 us
  matrix products: 7.24 us -> 0 us
    psum x2 -> x0, waiting for transfers between devices: 112 us -> none  [the longest x1 84.5 us: on_device(): lax.psum((block_part, vectors_part), ('obj', 'mem'))]
    psum x3 -> x0, blocking collectives: 69.4 us -> none  [the longest x1 40.7 us: on_device(): lax.psum((block_part, vectors_part), ('obj', 'mem'))]
    ppermute x0 -> x21, starting transfers between devices: none -> 26.4 us  [the longest x9 16.3 us: over_outer(): return lax.ppermute(v, ALL, self.perm(lambda o, m: (o, m ^ k << 1)))]
    ppermute x0 -> x21, waiting for transfers between devices: none -> 17.9 us  [the longest x9 10.4 us: over_outer(): return lax.ppermute(v, ALL, self.perm(lambda o, m: (o, m ^ k << 1)))]
    all_to_all x2 -> x0, waiting for transfers between devices: 14.5 us -> none  [the longest x1 14.5 us: on_device(): lax.all_to_all(hidden, 'mem', split_axis=1, concat_axis=0, tiled=True)]
    pallas_call x0 -> x6, Pallas kernels: none -> 11.3 us  [call(): pl.pallas_call(body, out_shape=outs, in_specs=specs, out_specs=jax.tree.m...]
    all_to_all x2 -> x0, starting transfers between devices: 11.1 us -> none  [the longest x1 7.42 us: on_device(): lax.all_to_all(hidden, 'mem', split_axis=1, concat_axis=0, tiled=True)]
    dot_general x6 -> x0, matrix products: 7.24 us -> none  [the longest x1 2.16 us: on_device(): jnp.einsum('ne,de->nd', dmixed, weight_low, preferred_element_type=jnp.fl...]
  transfers between devices with their start and end apart: 5 -> 21, of which waited for: 4 -> 12; matrix products, arithmetic and copies ran while one was open for 3% -> 6% of each run, Pallas kernels for 0% -> 2%
where the time goes in v1:
time: 60.7 us; the launch traced here: 60.5 us
  starting transfers between devices  26.4 us (43%)
  waiting for transfers between devices  17.9 us (29%)
  Pallas kernels  11.3 us (19%)
  other arithmetic  2.59 us (4%)
  local copies, waits for them, and re-layouts  1.46 us (2%)
  between operations  0.89 us (1%)
    ppermute x9, starting transfers between devices, over_outer(): return lax.ppermute(v, ALL, self.perm(lambda o, m: (o, m ^ k << 1)))  16.3 us
    pallas_call x6, Pallas kernels, call(): pl.pallas_call(body, out_shape=outs, in_specs=specs, out_specs=jax.tree.m...  11.3 us
    ppermute x9, waiting for transfers between devices, over_outer(): return lax.ppermute(v, ALL, self.perm(lambda o, m: (o, m ^ k << 1)))  10.4 us
    ppermute x7, starting transfers between devices, over_plane(): lax.ppermute(v, ALL, self.perm(lambda o, m: (o ^ k >> 1 << 1, m ^ k & 1)))  8.91 us
    ppermute x7, waiting for transfers between devices, over_plane(): lax.ppermute(v, ALL, self.perm(lambda o, m: (o ^ k >> 1 << 1, m ^ k & 1)))  5.75 us
    ppermute x5, waiting for transfers between devices, over_core(): return lax.ppermute(v, ALL, self.perm(lambda o, m: (o ^ 1, m)))  1.74 us
  transfers between devices with their start and end apart: 21, of which 12 were waited for; matrix products, arithmetic and copies ran while one was open for 6% of the time, Pallas kernels for 2%

profile of v1, /device:TPU:0, one launch (start us, length us, event | category | flops | bytes accessed | tf_op | source)
XLA Modules:
  0.0 60.5 jit_solution(7869687187351748137)
XLA Ops:
  0.7 0.0 copy-start
  0.7 4.1 %collective-permute-start.1 = (bf16[64,512]{1,0:T(8,128)(2,1)}, bf16[64,512]{1,0:T(8,128)(2,1)S(1)}, u32[]{:S(2)}, u32[]{:S(2)}) collective-permute-start(bf16[64,512]{1,0:T(8,128)(2,1)} %refs_0_.1), channel_id=1, source_target_pairs={{0,4},{1,5},{2,6},{3,7},{4,0},{5,1},{6,2},{7,3},{8,12},{9,13},{10,... | collective-permute-start | bytes 196616 | tf_op jit(solution)/shard_map/ppermute | solution.py:83
  4.8 1.6 %collective-permute-start = (bf16[64,512]{1,0:T(8,128)(2,1)}, bf16[64,512]{1,0:T(8,128)(2,1)S(1)}, u32[]{:S(2)}, u32[]{:S(2)}) collective-permute-start(bf16[64,512]{1,0:T(8,128)(2,1)} %refs_0_.1), channel_id=1, source_target_pairs={{0,2},{1,3},{2,0},{3,1},{4,6},{5,7},{6,4},{7,5},{8,10},{9,11},{10,... | collective-permute-start | bytes 196616 | tf_op jit(solution)/shard_map/ppermute | solution.py:83
  6.3 0.0 collective-permute-start.2
  6.3 0.7 %convert_bitcast_fusion = bf16[128]{0:T(256)(128)(2,1)S(1)} fusion(f32[1,128]{1,0:T(1,128)} %refs_17_.1), kind=kLoop, calls=%fused_computation.4 | loop fusion | flops 128 | bytes 768 | tf_op jit(solution)/shard_map/broadcast_in_dim | solution.py:374
  7.0 1.0 %bitcast_convert_fusion.refs_7_ = bf16[512,128]{1,0:T(8,128)(2,1)S(1)} fusion(f32[1,512,128]{2,1,0:T(8,128)} %param.22), kind=kLoop, calls=%fused_computation.6 | loop fusion | flops 65536 | bytes 393216 | tf_op jit(solution)/shard_map/convert_element_type | solution.py:373
  8.0 1.8 %collective-permute-start.3 = (bf16[528,128]{1,0:T(8,128)(2,1)S(1)}, bf16[528,128]{1,0:T(8,128)(2,1)S(1)}, u32[]{:S(2)}, u32[]{:S(2)}) collective-permute-start(bf16[528,128]{1,0:T(8,128)(2,1)S(1)} %pad_maximum_fusion), channel_id=1, source_target_pairs={{0,1},{1,0},{2,3},{3,2},{4,5},{5,4},{6,7},{7,6},{8,9},{9,8},{10,11... | collective-permute-start | bytes 405512 | tf_op jit(solution)/shard_map/ppermute | solution.py:80
  9.8 0.8 %fusion.refs_4_ = f32[512,128]{1,0:T(8,128)S(1)} fusion(s32[512]{0:T(512)} %param.15), kind=kLoop, calls=%fused_computation.1 | loop fusion | flops 131072 | bytes 264192 | tf_op jit(solution)/shard_map/convert_element_type | solution.py:378
  10.6 0.8 %constant_dynamic-slice_fusion = f32[3,2,512]{2,1,0:T(2,128)S(1)} fusion(f32[3,8,512]{2,1,0:T(8,128)} %refs_11_.1, s32[]{:T(128)S(6)} %select_n.25), kind=kLoop, calls=%fused_computation.5 | loop fusion | bytes 24580 | tf_op jit(solution)/shard_map/dynamic_slice | solution.py:380
  11.5 0.0 copy-done
  11.5 0.0 copy-start.7
  11.5 0.1 convert_element_type.13.refs_5_
  11.6 0.1 pad_add_fusion.place
  11.6 0.0 collective-permute-done.1.refs_2_
  11.6 0.0 collective-permute-done.refs_1_
  11.7 1.0 %collective-permute-done.2.refs_3_ = bf16[64,512]{1,0:T(8,128)(2,1)S(1)} collective-permute-done((bf16[64,512]{1,0:T(8,128)(2,1)}, bf16[64,512]{1,0:T(8,128)(2,1)S(1)}, u32[]{:S(2)}, u32[]{:S(2)}) %collective-permute-start.2) | collective-permute-done | bytes 65568 | tf_op jit(solution)/shard_map/ppermute | solution.py:83
  12.6 0.5 collective-permute-done.3.refs_9_
  13.1 4.3 %local.1 = (bf16[4,400,128]{2,1,0:T(8,128)(2,1)S(1)}, f32[4,400,128]{2,1,0:T(8,128)S(1)}, f32[64,640]{1,0:T(8,128)S(1)}, bf16[64,640]{1,0:T(8,128)(2,1)S(1)}, bf...) custom-call(s32[4]{0:T(128)S(1)} %pad_add_fusion.place, bf16[64,512]{1,0:T(8,128)(2,1)S(1)} %copy-done.7, ...), custom_call_target="tpu_custom_call" | custom-call | tf_op jit(solution)/shard_map/local/pallas_call | solution.py:45
  17.4 0.1 collective-permute-start.7
  17.5 1.7 %collective-permute-done.7.got_ref = bf16[4,400,128]{2,1,0:T(8,128)(2,1)S(1)} collective-permute-done((bf16[4,400,128]{2,1,0:T(8,128)(2,1)S(1)}, bf16[4,400,128]{2,1,0:T(8,128)(2,1)S(1)}, u32[]{:S(2)}, u32[]{:S(2)}) %collective-permute-start.7) | collective-permute-done | bytes 409632 | tf_op jit(solution)/shard_map/ppermute | solution.py:77
  19.2 0.6 %core_sum.1 = (f32[400,128]{1,0:T(8,128)S(1)}, bf16[400,128]{1,0:T(8,128)(2,1)S(1)}, bf16[400,128]{1,0:T(8,128)(2,1)S(1)}, bf16[400,128]{1,0:T(8,128)(2,1)S(1)}) custom-call(s32[4]{0:T(128)S(1)} %pad_add_fusion.place, f32[4,400,128]{2,1,0:T(8,128)S(1)} %get-tuple-element.55.keep_ref, bf16[4,400,128]{2,1,0:T(8,128)(2,1)S(1)} %collective-permute-done.7.got_ref), custom_call_target="tpu_custom_call" | custom-call | tf_op jit(solution)/shard_map/core_sum/pallas_call | solution.py:45
  19.9 1.8 %collective-permute-start.8 = (bf16[400,128]{1,0:T(8,128)(2,1)S(1)}, bf16[400,128]{1,0:T(8,128)(2,1)S(1)}, u32[]{:S(2)}, u32[]{:S(2)}) collective-permute-start(bf16[400,128]{1,0:T(8,128)(2,1)S(1)} %get-tuple-element.58), channel_id=1, source_target_pairs={{0,1},{1,0},{2,3},{3,2},{4,5},{5,4},{6,7},{7,6},{8,9},{9,8},{10,11... | collective-permute-start | bytes 307208 | tf_op jit(solution)/shard_map/ppermute | solution.py:80
  21.7 1.5 %collective-permute-start.9 = (bf16[400,128]{1,0:T(8,128)(2,1)S(1)}, bf16[400,128]{1,0:T(8,128)(2,1)S(1)}, u32[]{:S(2)}, u32[]{:S(2)}) collective-permute-start(bf16[400,128]{1,0:T(8,128)(2,1)S(1)} %get-tuple-element.59), channel_id=1, source_target_pairs={{0,16},{1,17},{2,18},{3,19},{4,20},{5,21},{6,22},{7,23},{8,24},{9,... | collective-permute-start | bytes 307208 | tf_op jit(solution)/shard_map/ppermute | solution.py:80
  23.1 0.3 collective-permute-start.10
  23.4 1.4 %collective-permute-done.8.refs_0_ = bf16[400,128]{1,0:T(8,128)(2,1)S(1)} collective-permute-done((bf16[400,128]{1,0:T(8,128)(2,1)S(1)}, bf16[400,128]{1,0:T(8,128)(2,1)S(1)}, u32[]{:S(2)}, u32[]{:S(2)}) %collective-permute-start.8) | collective-permute-done | bytes 102432 | tf_op jit(solution)/shard_map/ppermute | solution.py:80
  24.8 2.5 %collective-permute-done.9.refs_1_ = bf16[400,128]{1,0:T(8,128)(2,1)S(1)} collective-permute-done((bf16[400,128]{1,0:T(8,128)(2,1)S(1)}, bf16[400,128]{1,0:T(8,128)(2,1)S(1)}, u32[]{:S(2)}, u32[]{:S(2)}) %collective-permute-start.9) | collective-permute-done | bytes 102432 | tf_op jit(solution)/shard_map/ppermute | solution.py:80
  27.4 1.3 %collective-permute-done.10.refs_2_ = bf16[400,128]{1,0:T(8,128)(2,1)S(1)} collective-permute-done((bf16[400,128]{1,0:T(8,128)(2,1)S(1)}, bf16[400,128]{1,0:T(8,128)(2,1)S(1)}, u32[]{:S(2)}, u32[]{:S(2)}) %collective-permute-start.10) | collective-permute-done | bytes 102432 | tf_op jit(solution)/shard_map/ppermute | solution.py:80
  28.7 0.7 %plane_sum.1 = (bf16[272,128]{1,0:T(8,128)(2,1)S(1)}, f32[272,128]{1,0:T(8,128)S(1)}, f32[128,128]{1,0:T(8,128)S(1)}) custom-call(s32[4]{0:T(128)S(1)} %pad_add_fusion.place, f32[400,128]{1,0:T(8,128)S(1)} %get-tuple-element.57.own_ref, bf16[400,128]{1,0:T(8,128)(2,1)S(1)} %collective-permute-done.8.refs_0_, ...), custom_call_target="tpu_custom_call" | custom-call | tf_op jit(solution)/shard_map/plane_sum/pallas_call | solution.py:45
  29.3 3.7 %collective-permute-start.13 = (bf16[272,128]{1,0:T(8,128)(2,1)S(1)}, bf16[272,128]{1,0:T(8,128)(2,1)S(1)}, u32[]{:S(2)}, u32[]{:S(2)}) collective-permute-start(bf16[272,128]{1,0:T(8,128)(2,1)S(1)} %get-tuple-element.63), channel_id=1, source_target_pairs={{0,6},{1,7},{2,4},{3,5},{4,2},{5,3},{6,0},{7,1},{8,14},{9,15},{10,... | collective-permute-start | bytes 208904 | tf_op jit(solution)/shard_map/ppermute | solution.py:83
  33.0 0.0 collective-permute-start.12
  33.0 0.8 %collective-permute-start.11 = (bf16[272,128]{1,0:T(8,128)(2,1)S(1)}, bf16[272,128]{1,0:T(8,128)(2,1)S(1)}, u32[]{:S(2)}, u32[]{:S(2)}) collective-permute-start(bf16[272,128]{1,0:T(8,128)(2,1)S(1)} %get-tuple-element.63), channel_id=1, source_target_pairs={{0,2},{1,3},{2,0},{3,1},{4,6},{5,7},{6,4},{7,5},{8,10},{9,11},{10,... | collective-permute-start | bytes 208904 | tf_op jit(solution)/shard_map/ppermute | solution.py:83
  33.8 1.8 %collective-permute-done.13.refs_2_ = bf16[272,128]{1,0:T(8,128)(2,1)S(1)} collective-permute-done((bf16[272,128]{1,0:T(8,128)(2,1)S(1)}, bf16[272,128]{1,0:T(8,128)(2,1)S(1)}, u32[]{:S(2)}, u32[]{:S(2)}) %collective-permute-start.13) | collective-permute-done | bytes 69664 | tf_op jit(solution)/shard_map/ppermute | solution.py:83
  35.6 2.7 %collective-permute-done.12.refs_1_ = bf16[272,128]{1,0:T(8,128)(2,1)S(1)} collective-permute-done((bf16[272,128]{1,0:T(8,128)(2,1)S(1)}, bf16[272,128]{1,0:T(8,128)(2,1)S(1)}, u32[]{:S(2)}, u32[]{:S(2)}) %collective-permute-start.12) | collective-permute-done | bytes 69664 | tf_op jit(solution)/shard_map/ppermute | solution.py:83
  38.3 0.1 collective-permute-done.11.refs_0_
  38.4 0.7 %outer_sum.1 = (bf16[352,128]{1,0:T(8,128)(2,1)S(1)}, bf16[352,128]{1,0:T(8,128)(2,1)S(1)}) custom-call(s32[4]{0:T(128)S(1)} %pad_add_fusion.place, f32[272,128]{1,0:T(8,128)S(1)} %get-tuple-element.61.block_ref, f32[128,128]{1,0:T(8,128)S(1)} %get-tuple-element.62.head_ref, bf16[272,128]{1,0:T(8,128)(2,1)S(1)} %collective-permute-done.11.refs_0_, ...), custom_call_target="tpu_custom_call" | custom-call | tf_op jit(solution)/shard_map/outer_sum/pallas_call | solution.py:45
  39.0 0.0 copy-start.1
  39.1 2.4 %collective-permute-start.16 = (bf16[352,128]{1,0:T(8,128)(2,1)S(1)}, bf16[352,128]{1,0:T(8,128)(2,1)S(1)}, u32[]{:S(2)}, u32[]{:S(2)}) collective-permute-start(bf16[352,128]{1,0:T(8,128)(2,1)S(1)} %get-tuple-element.65), channel_id=1, source_target_pairs={{0,17},{1,16},{2,19},{3,18},{4,21},{5,20},{6,23},{7,22},{8,25},{9,... | collective-permute-start | bytes 270344 | tf_op jit(solution)/shard_map/ppermute | solution.py:80
  41.5 0.7 %collective-permute-start.14 = (bf16[352,128]{1,0:T(8,128)(2,1)S(1)}, bf16[352,128]{1,0:T(8,128)(2,1)S(1)}, u32[]{:S(2)}, u32[]{:S(2)}) collective-permute-start(bf16[352,128]{1,0:T(8,128)(2,1)S(1)} %get-tuple-element.65), channel_id=1, source_target_pairs={{0,1},{1,0},{2,3},{3,2},{4,5},{5,4},{6,7},{7,6},{8,9},{9,8},{10,11... | collective-permute-start | bytes 270344 | tf_op jit(solution)/shard_map/ppermute | solution.py:80
  42.1 0.5 collective-permute-start.15
  42.6 0.5 collective-permute-start.4
  43.1 2.0 %collective-permute-start.5 = (bf16[64,640]{1,0:T(8,128)(2,1)S(1)}, bf16[64,640]{1,0:T(8,128)(2,1)S(1)}, u32[]{:S(2)}, u32[]{:S(2)}) collective-permute-start(bf16[64,640]{1,0:T(8,128)(2,1)S(1)} %get-tuple-element.51), channel_id=1, source_target_pairs={{0,4},{1,5},{2,6},{3,7},{4,0},{5,1},{6,2},{7,3},{8,12},{9,13},{10,... | collective-permute-start | bytes 245768 | tf_op jit(solution)/shard_map/ppermute | solution.py:83
  45.1 1.9 %collective-permute-done.4.refs_0_ = bf16[64,640]{1,0:T(8,128)(2,1)S(1)} collective-permute-done((bf16[64,640]{1,0:T(8,128)(2,1)S(1)}, bf16[64,640]{1,0:T(8,128)(2,1)S(1)}, u32[]{:S(2)}, u32[]{:S(2)}) %collective-permute-start.4) | collective-permute-done | bytes 81952 | tf_op jit(solution)/shard_map/ppermute | solution.py:83
  47.0 0.0 collective-permute-start.17
  47.1 0.0 collective-permute-done.16.refs_3_
  47.1 0.5 collective-permute-start.20
  47.6 0.0 collective-permute-done.14.refs_1_
  47.6 0.1 collective-permute-start.18
  47.6 0.0 collective-permute-done.15.refs_2_
  47.6 0.4 collective-permute-start.19
  48.1 0.4 collective-permute-done.5.refs_1_
  48.5 3.7 %collective-permute-start.6 = (bf16[64,640]{1,0:T(8,128)(2,1)S(1)}, bf16[64,640]{1,0:T(8,128)(2,1)S(1)}, u32[]{:S(2)}, u32[]{:S(2)}) collective-permute-start(bf16[64,640]{1,0:T(8,128)(2,1)S(1)} %get-tuple-element.52), channel_id=1, source_target_pairs={{0,6},{1,7},{2,4},{3,5},{4,2},{5,3},{6,0},{7,1},{8,14},{9,15},{10,... | collective-permute-start | bytes 245768 | tf_op jit(solution)/shard_map/ppermute | solution.py:83
  52.2 2.6 %collective-permute-done.6.refs_2_ = bf16[64,640]{1,0:T(8,128)(2,1)S(1)} collective-permute-done((bf16[64,640]{1,0:T(8,128)(2,1)S(1)}, bf16[64,640]{1,0:T(8,128)(2,1)S(1)}, u32[]{:S(2)}, u32[]{:S(2)}) %collective-permute-start.6) | collective-permute-done | bytes 81952 | tf_op jit(solution)/shard_map/ppermute | solution.py:83
  54.8 1.2 %back_sum.1 = (f32[64,512]{1,0:T(8,128)}, f32[64,128]{1,0:T(8,128)}) custom-call(s32[4]{0:T(128)S(1)} %pad_add_fusion.place, f32[64,640]{1,0:T(8,128)S(1)} %get-tuple-element.49.own_ref, bf16[64,640]{1,0:T(8,128)(2,1)S(1)} %collective-permute-done.4.refs_0_, bf16[64,640]{1,0:T(8,128)(2,1)S(1)} %collective-permute-done.5.refs_1_, ...), custom_call_target="tpu_custom_call" | custom-call | tf_op jit(solution)/shard_map/back_sum/pallas_call | solution.py:45
  56.0 0.0 collective-permute-done.17.refs_4_
  56.0 0.0 collective-permute-done.20.refs_7_
  56.0 0.0 collective-permute-done.18.refs_5_
  56.0 0.0 collective-permute-done.19.refs_6_
  56.0 0.0 copy-start.10
  56.0 0.0 copy-start.11
  56.1 0.0 copy-start.12
  56.1 0.5 copy-done.10
  56.7 0.0 copy-done.11
  56.7 0.0 copy-done.12
  56.7 3.8 %update.1 = (f32[1,128]{1,0:T(1,128)}, f32[512,512]{1,0:T(8,128)}, f32[512,512]{1,0:T(8,128)}, f32[512,512]{1,0:T(8,128)}, bf16[512,512]{1,0:T(8,128)(2,1)}, /*i...) custom-call(s32[4]{0:T(128)S(1)} %pad_add_fusion.place, ...), custom_call_target="tpu_custom_call" | custom-call | tf_op jit(solution)/shard_map/update/pallas_call | solution.py:45
  (19 shorter events, 0.1 us)
Async XLA Ops:
  0.7 10.8 %copy-start = (f32[512,512]{1,0:T(8,128)S(1)}, f32[512,512]{1,0:T(8,128)}, u32[]{:S(2)}) copy-start(f32[512,512]{1,0:T(8,128)} %refs_8_.1) | copy-start | bytes 3145732
  0.7 11.0 %collective-permute-start.1 = (bf16[64,512]{1,0:T(8,128)(2,1)}, bf16[64,512]{1,0:T(8,128)(2,1)S(1)}, u32[]{:S(2)}, u32[]{:S(2)}) collective-permute-start(bf16[64,512]{1,0:T(8,128)(2,1)} %refs_0_.1), channel_id=1, source_target_pairs={{0,4},{1,5},{2,6},{3,7},{4,0},{5,1},{6,2},{7,3},{8,12},{9,13},{10,... | collective-permute-start | bytes 196616 | tf_op jit(solution)/shard_map/ppermute | solution.py:83
  4.8 6.9 %collective-permute-start = (bf16[64,512]{1,0:T(8,128)(2,1)}, bf16[64,512]{1,0:T(8,128)(2,1)S(1)}, u32[]{:S(2)}, u32[]{:S(2)}) collective-permute-start(bf16[64,512]{1,0:T(8,128)(2,1)} %refs_0_.1), channel_id=1, source_target_pairs={{0,2},{1,3},{2,0},{3,1},{4,6},{5,7},{6,4},{7,5},{8,10},{9,11},{10,... | collective-permute-start | bytes 196616 | tf_op jit(solution)/shard_map/ppermute | solution.py:83
  6.3 6.3 %collective-permute-start.2 = (bf16[64,512]{1,0:T(8,128)(2,1)}, bf16[64,512]{1,0:T(8,128)(2,1)S(1)}, u32[]{:S(2)}, u32[]{:S(2)}) collective-permute-start(bf16[64,512]{1,0:T(8,128)(2,1)} %refs_0_.1), channel_id=1, source_target_pairs={{0,6},{1,7},{2,4},{3,5},{4,2},{5,3},{6,0},{7,1},{8,14},{9,15},{10,... | collective-permute-start | bytes 196616 | tf_op jit(solution)/shard_map/ppermute | solution.py:83
  8.0 5.1 %collective-permute-start.3 = (bf16[528,128]{1,0:T(8,128)(2,1)S(1)}, bf16[528,128]{1,0:T(8,128)(2,1)S(1)}, u32[]{:S(2)}, u32[]{:S(2)}) collective-permute-start(bf16[528,128]{1,0:T(8,128)(2,1)S(1)} %pad_maximum_fusion), channel_id=1, source_target_pairs={{0,1},{1,0},{2,3},{3,2},{4,5},{5,4},{6,7},{7,6},{8,9},{9,8},{10,11... | collective-permute-start | bytes 405512 | tf_op jit(solution)/shard_map/ppermute | solution.py:80
  11.5 1.6 %copy-start.7 = (bf16[64,512]{1,0:T(8,128)(2,1)S(1)}, bf16[64,512]{1,0:T(8,128)(2,1)}, u32[]{:S(2)}) copy-start(bf16[64,512]{1,0:T(8,128)(2,1)} %refs_0_.1) | copy-start | bytes 196612
  13.1 43.0 %copy-start.4 = (f32[1,512,128]{2,1,0:T(8,128)S(1)}, f32[1,512,128]{2,1,0:T(8,128)}, u32[]{:S(2)}) copy-start(f32[1,512,128]{2,1,0:T(8,128)} %param.23) | copy-start | bytes 786436
  13.1 43.0 %copy-start.5 = (f32[1,512,128]{2,1,0:T(8,128)S(1)}, f32[1,512,128]{2,1,0:T(8,128)}, u32[]{:S(2)}) copy-start(f32[1,512,128]{2,1,0:T(8,128)} %param.24) | copy-start | bytes 786436
  17.4 1.8 %collective-permute-start.7 = (bf16[4,400,128]{2,1,0:T(8,128)(2,1)S(1)}, bf16[4,400,128]{2,1,0:T(8,128)(2,1)S(1)}, u32[]{:S(2)}, u32[]{:S(2)}) collective-permute-start(bf16[4,400,128]{2,1,0:T(8,128)(2,1)S(1)} %get-tuple-element.56), channel_id=1, source_target_pairs={{0,8},{1,9},{2,10},{3,11},{4,12},{5,13},{6,14},{7,15},{8,0},{9,1},... | collective-permute-start | bytes 1228808 | tf_op jit(solution)/shard_map/ppermute | solution.py:77
  19.2 36.9 %copy-start.2 = (f32[512,512]{1,0:T(8,128)S(1)}, f32[512,512]{1,0:T(8,128)}, u32[]{:S(2)}) copy-start(f32[512,512]{1,0:T(8,128)} %refs_9_.1) | copy-start | bytes 3145732
  19.2 36.9 %copy-start.3 = (f32[512,512]{1,0:T(8,128)S(1)}, f32[512,512]{1,0:T(8,128)}, u32[]{:S(2)}) copy-start(f32[512,512]{1,0:T(8,128)} %refs_10_.1) | copy-start | bytes 3145732
  19.9 5.0 %collective-permute-start.8 = (bf16[400,128]{1,0:T(8,128)(2,1)S(1)}, bf16[400,128]{1,0:T(8,128)(2,1)S(1)}, u32[]{:S(2)}, u32[]{:S(2)}) collective-permute-start(bf16[400,128]{1,0:T(8,128)(2,1)S(1)} %get-tuple-element.58), channel_id=1, source_target_pairs={{0,1},{1,0},{2,3},{3,2},{4,5},{5,4},{6,7},{7,6},{8,9},{9,8},{10,11... | collective-permute-start | bytes 307208 | tf_op jit(solution)/shard_map/ppermute | solution.py:80
  21.7 5.7 %collective-permute-start.9 = (bf16[400,128]{1,0:T(8,128)(2,1)S(1)}, bf16[400,128]{1,0:T(8,128)(2,1)S(1)}, u32[]{:S(2)}, u32[]{:S(2)}) collective-permute-start(bf16[400,128]{1,0:T(8,128)(2,1)S(1)} %get-tuple-element.59), channel_id=1, source_target_pairs={{0,16},{1,17},{2,18},{3,19},{4,20},{5,21},{6,22},{7,23},{8,24},{9,... | collective-permute-start | bytes 307208 | tf_op jit(solution)/shard_map/ppermute | solution.py:80
  23.1 5.6 %collective-permute-start.10 = (bf16[400,128]{1,0:T(8,128)(2,1)S(1)}, bf16[400,128]{1,0:T(8,128)(2,1)S(1)}, u32[]{:S(2)}, u32[]{:S(2)}) collective-permute-start(bf16[400,128]{1,0:T(8,128)(2,1)S(1)} %get-tuple-element.60), channel_id=1, source_target_pairs={{0,17},{1,16},{2,19},{3,18},{4,21},{5,20},{6,23},{7,22},{8,25},{9,... | collective-permute-start | bytes 307208 | tf_op jit(solution)/shard_map/ppermute | solution.py:80
  29.3 6.3 %collective-permute-start.13 = (bf16[272,128]{1,0:T(8,128)(2,1)S(1)}, bf16[272,128]{1,0:T(8,128)(2,1)S(1)}, u32[]{:S(2)}, u32[]{:S(2)}) collective-permute-start(bf16[272,128]{1,0:T(8,128)(2,1)S(1)} %get-tuple-element.63), channel_id=1, source_target_pairs={{0,6},{1,7},{2,4},{3,5},{4,2},{5,3},{6,0},{7,1},{8,14},{9,15},{10,... | collective-permute-start | bytes 208904 | tf_op jit(solution)/shard_map/ppermute | solution.py:83
  33.0 5.3 %collective-permute-start.12 = (bf16[272,128]{1,0:T(8,128)(2,1)S(1)}, bf16[272,128]{1,0:T(8,128)(2,1)S(1)}, u32[]{:S(2)}, u32[]{:S(2)}) collective-permute-start(bf16[272,128]{1,0:T(8,128)(2,1)S(1)} %get-tuple-element.63), channel_id=1, source_target_pairs={{0,4},{1,5},{2,6},{3,7},{4,0},{5,1},{6,2},{7,3},{8,12},{9,13},{10,... | collective-permute-start | bytes 208904 | tf_op jit(solution)/shard_map/ppermute | solution.py:83
  33.0 5.3 %collective-permute-start.11 = (bf16[272,128]{1,0:T(8,128)(2,1)S(1)}, bf16[272,128]{1,0:T(8,128)(2,1)S(1)}, u32[]{:S(2)}, u32[]{:S(2)}) collective-permute-start(bf16[272,128]{1,0:T(8,128)(2,1)S(1)} %get-tuple-element.63), channel_id=1, source_target_pairs={{0,2},{1,3},{2,0},{3,1},{4,6},{5,7},{6,4},{7,5},{8,10},{9,11},{10,... | collective-permute-start | bytes 208904 | tf_op jit(solution)/shard_map/ppermute | solution.py:83
  39.0 17.1 %copy-start.1 = (f32[1,512,128]{2,1,0:T(8,128)S(1)}, f32[1,512,128]{2,1,0:T(8,128)}, u32[]{:S(2)}) copy-start(f32[1,512,128]{2,1,0:T(8,128)} %param.22) | copy-start | bytes 786436
  39.1 8.0 %collective-permute-start.16 = (bf16[352,128]{1,0:T(8,128)(2,1)S(1)}, bf16[352,128]{1,0:T(8,128)(2,1)S(1)}, u32[]{:S(2)}, u32[]{:S(2)}) collective-permute-start(bf16[352,128]{1,0:T(8,128)(2,1)S(1)} %get-tuple-element.65), channel_id=1, source_target_pairs={{0,17},{1,16},{2,19},{3,18},{4,21},{5,20},{6,23},{7,22},{8,25},{9,... | collective-permute-start | bytes 270344 | tf_op jit(solution)/shard_map/ppermute | solution.py:80
  41.5 6.1 %collective-permute-start.14 = (bf16[352,128]{1,0:T(8,128)(2,1)S(1)}, bf16[352,128]{1,0:T(8,128)(2,1)S(1)}, u32[]{:S(2)}, u32[]{:S(2)}) collective-permute-start(bf16[352,128]{1,0:T(8,128)(2,1)S(1)} %get-tuple-element.65), channel_id=1, source_target_pairs={{0,1},{1,0},{2,3},{3,2},{4,5},{5,4},{6,7},{7,6},{8,9},{9,8},{10,11... | collective-permute-start | bytes 270344 | tf_op jit(solution)/shard_map/ppermute | solution.py:80
  42.1 5.5 %collective-permute-start.15 = (bf16[352,128]{1,0:T(8,128)(2,1)S(1)}, bf16[352,128]{1,0:T(8,128)(2,1)S(1)}, u32[]{:S(2)}, u32[]{:S(2)}) collective-permute-start(bf16[352,128]{1,0:T(8,128)(2,1)S(1)} %get-tuple-element.64.refs_0_), channel_id=1, source_target_pairs={{0,16},{1,17},{2,18},{3,19},{4,20},{5,21},{6,22},{7,23},{8,24},{9,... | collective-permute-start | bytes 270344 | tf_op jit(solution)/shard_map/ppermute | solution.py:80
  42.6 4.4 %collective-permute-start.4 = (bf16[64,640]{1,0:T(8,128)(2,1)S(1)}, bf16[64,640]{1,0:T(8,128)(2,1)S(1)}, u32[]{:S(2)}, u32[]{:S(2)}) collective-permute-start(bf16[64,640]{1,0:T(8,128)(2,1)S(1)} %get-tuple-element.50), channel_id=1, source_target_pairs={{0,2},{1,3},{2,0},{3,1},{4,6},{5,7},{6,4},{7,5},{8,10},{9,11},{10,... | collective-permute-start | bytes 245768 | tf_op jit(solution)/shard_map/ppermute | solution.py:83
  43.1 5.3 %collective-permute-start.5 = (bf16[64,640]{1,0:T(8,128)(2,1)S(1)}, bf16[64,640]{1,0:T(8,128)(2,1)S(1)}, u32[]{:S(2)}, u32[]{:S(2)}) collective-permute-start(bf16[64,640]{1,0:T(8,128)(2,1)S(1)} %get-tuple-element.51), channel_id=1, source_target_pairs={{0,4},{1,5},{2,6},{3,7},{4,0},{5,1},{6,2},{7,3},{8,12},{9,13},{10,... | collective-permute-start | bytes 245768 | tf_op jit(solution)/shard_map/ppermute | solution.py:83
  47.0 9.0 %collective-permute-start.17 = (bf16[352,128]{1,0:T(8,128)(2,1)S(1)}, bf16[352,128]{1,0:T(8,128)(2,1)S(1)}, u32[]{:S(2)}, u32[]{:S(2)}) collective-permute-start(bf16[352,128]{1,0:T(8,128)(2,1)S(1)} %get-tuple-element.64.refs_0_), channel_id=1, source_target_pairs={{0,8},{1,9},{2,10},{3,11},{4,12},{5,13},{6,14},{7,15},{8,0},{9,1},... | collective-permute-start | bytes 270344 | tf_op jit(solution)/shard_map/ppermute | solution.py:77
  47.1 8.9 %collective-permute-start.20 = (bf16[352,128]{1,0:T(8,128)(2,1)S(1)}, bf16[352,128]{1,0:T(8,128)(2,1)S(1)}, u32[]{:S(2)}, u32[]{:S(2)}) collective-permute-start(bf16[352,128]{1,0:T(8,128)(2,1)S(1)} %collective-permute-done.16.refs_3_), channel_id=1, source_target_pairs={{0,8},{1,9},{2,10},{3,11},{4,12},{5,13},{6,14},{7,15},{8,0},{9,1},... | collective-permute-start | bytes 270344 | tf_op jit(solution)/shard_map/ppermute | solution.py:77
  47.6 8.4 %collective-permute-start.18 = (bf16[352,128]{1,0:T(8,128)(2,1)S(1)}, bf16[352,128]{1,0:T(8,128)(2,1)S(1)}, u32[]{:S(2)}, u32[]{:S(2)}) collective-permute-start(bf16[352,128]{1,0:T(8,128)(2,1)S(1)} %collective-permute-done.14.refs_1_), channel_id=1, source_target_pairs={{0,8},{1,9},{2,10},{3,11},{4,12},{5,13},{6,14},{7,15},{8,0},{9,1},... | collective-permute-start | bytes 270344 | tf_op jit(solution)/shard_map/ppermute | solution.py:77
  47.6 8.4 %collective-permute-start.19 = (bf16[352,128]{1,0:T(8,128)(2,1)S(1)}, bf16[352,128]{1,0:T(8,128)(2,1)S(1)}, u32[]{:S(2)}, u32[]{:S(2)}) collective-permute-start(bf16[352,128]{1,0:T(8,128)(2,1)S(1)} %collective-permute-done.15.refs_2_), channel_id=1, source_target_pairs={{0,8},{1,9},{2,10},{3,11},{4,12},{5,13},{6,14},{7,15},{8,0},{9,1},... | collective-permute-start | bytes 270344 | tf_op jit(solution)/shard_map/ppermute | solution.py:77
  48.5 6.3 %collective-permute-start.6 = (bf16[64,640]{1,0:T(8,128)(2,1)S(1)}, bf16[64,640]{1,0:T(8,128)(2,1)S(1)}, u32[]{:S(2)}, u32[]{:S(2)}) collective-permute-start(bf16[64,640]{1,0:T(8,128)(2,1)S(1)} %get-tuple-element.52), channel_id=1, source_target_pairs={{0,6},{1,7},{2,4},{3,5},{4,2},{5,3},{6,0},{7,1},{8,14},{9,15},{10,... | collective-permute-start | bytes 245768 | tf_op jit(solution)/shard_map/ppermute | solution.py:83
  54.8 1.4 %copy-start.6 = (f32[3,8,512]{2,1,0:T(8,128)S(1)}, f32[3,8,512]{2,1,0:T(8,128)}, u32[]{:S(2)}) copy-start(f32[3,8,512]{2,1,0:T(8,128)} %refs_11_.1) | copy-start | bytes 147460
  54.8 1.4 %copy-start.8 = (f32[3,8,512]{2,1,0:T(8,128)S(1)}, f32[3,8,512]{2,1,0:T(8,128)}, u32[]{:S(2)}) copy-start(f32[3,8,512]{2,1,0:T(8,128)} %refs_12_.1) | copy-start | bytes 147460
  54.8 1.4 %copy-start.9 = (f32[3,8,512]{2,1,0:T(8,128)S(1)}, f32[3,8,512]{2,1,0:T(8,128)}, u32[]{:S(2)}) copy-start(f32[3,8,512]{2,1,0:T(8,128)} %refs_13_.1) | copy-start | bytes 147460
  56.0 0.7 %copy-start.10 = (f32[1,128]{1,0:T(1,128)S(1)}, f32[1,128]{1,0:T(1,128)}, u32[]{:S(2)}) copy-start(f32[1,128]{1,0:T(1,128)} %refs_17_.1) | copy-start | bytes 1540
  56.0 0.7 %copy-start.11 = (f32[1,128]{1,0:T(1,128)S(1)}, f32[1,128]{1,0:T(1,128)}, u32[]{:S(2)}) copy-start(f32[1,128]{1,0:T(1,128)} %refs_18_.1) | copy-start | bytes 1540
  56.1 0.7 %copy-start.12 = (f32[1,128]{1,0:T(1,128)S(1)}, f32[1,128]{1,0:T(1,128)}, u32[]{:S(2)}) copy-start(f32[1,128]{1,0:T(1,128)} %refs_19_.1) | copy-start | bytes 1540

commit v2 on v1

--- a/solution.py
+++ b/solution.py
@@ -40,13 +40,13 @@
     return lax.dot_general(a, b, (dims, ((), ())), preferred_element_type=f32)
 
 
-def call(body, outs, args, scratch=(), name=None):
-    specs = [SMEM] + [VMEM] * (len(args) - 1)
+def call(body, outs, args, scratch=(), name=None, out_spec=VMEM):
+    specs = [VMEM] * len(args)
     return pl.pallas_call(
         body,
         out_shape=outs,
         in_specs=specs,
-        out_specs=jax.tree.map(lambda _: VMEM, outs),
+        out_specs=[out_spec] * len(outs),
         scratch_shapes=list(scratch),
         compiler_params=pltpu.CompilerParams(vmem_limit_bytes=40 * MIB),
         name=name,
@@ -64,6 +64,8 @@
         self.block_rows = width // self.shards
         self.stacked = self.block_rows * self.groups
         self.items = max(8, self.shards)
+        self.bits = [1 << i for i in range(self.outer.bit_length() - 1)]
+        self.halving = sorted(range(self.outer), key=lambda k: [k & bit for bit in self.bits])
 
     def perm(self, move):
         pairs = []
@@ -83,19 +85,18 @@
         return lax.ppermute(v, ALL, self.perm(lambda o, m: (o, m ^ (k << 1))))
 
 
-def local_body(plan, place, *refs):
+def local_body(plan, *refs):
     n = plan.outer
     feats = refs[:n]
     onehot_ref, weight_ref, vec_ref, own_head, own_bias, far_head = refs[n : n + 6]
     send_ref, keep_ref = refs[n + 6 : n + 8]
-    back_own = refs[n + 8]
-    back_far = refs[n + 9 : n + 8 + n]
+    back_keep, back_send = refs[n + 8 : n + 10]
     lifted_ref, mixed_ref, hidden_ref, slope_ref, dmixed_ref, block_ref, heads_ref, items_ref = refs[
-        n + 8 + n :
+        n + 10 :
     ]
     rows, width, classes = plan.rows, plan.width, plan.classes
     objs = n * rows
-    core, quad, outer, inner = place[0], place[1], place[2], place[3]
+    core, quad, outer, inner = place_of()
     tile = 16
 
     for j in range(2):
@@ -170,7 +171,7 @@
     block_ref[0:width, :] = dot(lifted_ref[...], dmixed_ref[...], ((0,), (0,)))
     slope_ref[...] = dot(dmixed_ref[...], weight_ref[...], ((1,), (1,)))
     r_sums = [jnp.zeros((1, width), f32) for _ in range(2)]
-    for k in range(n):
+    for spot, k in enumerate(plan.halving):
         feat = feats[k][...].astype(f32)
         back = None
         for j in range(2):
@@ -178,9 +179,10 @@
             r_sums[j] = r_sums[j] + jnp.sum(lift_back * feat, axis=0, keepdims=True)
             part = lift_back * vec_ref[j : j + 1, :]
             back = part if back is None else back + part
-        out = back_own if k == 0 else back_far[k - 1]
-        out[:, 0:width] = back.astype(out.dtype)
-        out[:, width : width + classes] = logit_sum[k * rows : (k + 1) * rows, :].astype(out.dtype)
+        out = back_keep if spot < n // 2 else back_send
+        at = slice(spot % (n // 2) * rows, (spot % (n // 2) + 1) * rows)
+        out[at, 0:width] = back.astype(out.dtype)
+        out[at, width : width + classes] = logit_sum[k * rows : (k + 1) * rows, :].astype(out.dtype)
     for j in range(2):
         for g in range(plan.groups):
             items_ref[j, g : g + 1, :] = r_sums[j][:, g * LANES : (g + 1) * LANES]
@@ -201,18 +203,23 @@
             out[k, base : base + PAD, :] = items_ref[shard].astype(out.dtype)
 
 
-def core_body(plan, place, keep_ref, got_ref, own_ref, *send_refs):
+def core_body(plan, keep_ref, got_ref, own_ref, *send_refs):
     own_ref[...] = keep_ref[0] + got_ref[0].astype(f32)
     for k in range(1, plan.quads):
         send_refs[k - 1][...] = (keep_ref[k] + got_ref[k].astype(f32)).astype(bf16)
 
 
+def place_of():
+    obj, mem = lax.axis_index("obj"), lax.axis_index("mem")
+    return obj % 2, obj // 2 * 2 + mem % 2, mem // 2, mem % 2
+
+
 def two_parts(v):
     high = v.astype(bf16).astype(f32)
     return high, v - high
 
 
-def plane_body(plan, place, own_ref, *refs):
+def plane_body(plan, own_ref, *refs):
     got, (send_ref, block_ref, head_ref) = refs[: plan.quads - 1], refs[plan.quads - 1 :]
     total = own_ref[...]
     for r in got:
@@ -231,10 +238,10 @@
     send_ref[base : base + PAD, :] = extra.astype(bf16)
 
 
-def outer_body(plan, place, block_ref, head_ref, *refs):
+def outer_body(plan, block_ref, head_ref, *refs):
     n = plan.outer
     got, (same_ref, flip_ref) = refs[: n - 1], refs[n - 1 :]
-    inner = place[3]
+    inner = place_of()[3]
     base, stride, groups = plan.stacked, plan.block_rows, plan.groups
     total = block_ref[0:base, :]
     extras = [block_ref[base : base + PAD, :].astype(bf16).astype(f32)]
@@ -265,39 +272,47 @@
         out[spot + stride : spot + stride + PAD, :] = sums
 
 
-def back_body(plan, place, own_ref, *refs):
-    got, (feat_ref, mean_ref) = refs[: plan.outer - 1], refs[plan.outer - 1 :]
-    total = own_ref[...]
-    for r in got:
-        total = total + r[...].astype(f32)
+def half_body(plan, had_ref, got_ref, keep_ref, send_ref):
+    half = keep_ref.shape[0]
+    keep_ref[...] = had_ref[0:half, :] + got_ref[0:half, :].astype(f32)
+    send_ref[...] = (had_ref[half : 2 * half, :] + got_ref[half : 2 * half, :].astype(f32)).astype(bf16)
+
+
+def back_body(plan, had_ref, got_ref, feat_ref, mean_ref):
+    total = had_ref[...] + got_ref[...].astype(f32)
     feat_ref[...] = total[:, 0 : plan.width]
     mean_ref[...] = total[:, plan.width :] / plan.n_mem
 
 
-def update_body(plan, place, *refs):
+def update_body(plan, *refs):
     chunks = refs[: plan.shards]
-    (bw, bm, bv, vw, vm, vv, hw, hm, hv, cw, cm, cv) = refs[plan.shards : plan.shards + 12]
-    (
-        norm_ref,
-        bw_out,
-        bm_out,
-        bv_out,
-        bcopy_out,
-        vw_out,
-        vm_out,
-        vv_out,
-        hw_out,
-        hm_out,
-        hv_out,
-        hcopy_out,
-        cw_out,
-        cm_out,
-        cv_out,
-        items_ref,
-    ) = refs[plan.shards + 12 :]
-    core, quad, outer, inner = place[0], place[1], place[2], place[3]
+    states = refs[plan.shards : plan.shards + 10]
+    outs = refs[plan.shards + 10 : plan.shards + 25]
+    held, items_ref, sems = refs[plan.shards + 25 : -2], refs[-2], refs[-1]
+    bw, bm, bv, vw, vm, vv, hw, hm, hv, cs = states
+    norm_out, vec_outs, bias_outs, block_outs, head_outs = (
+        outs[0],
+        outs[5:8],
+        outs[12:15],
+        outs[1:5],
+        outs[8:12],
+    )
+    norm_ref, vec_refs, bias_refs, block_refs, head_refs = (
+        held[0],
+        held[5:8],
+        held[12:15],
+        held[1:5],
+        held[8:12],
+    )
+    core, quad, outer, inner = place_of()
     n, groups, stride, base = plan.outer, plan.groups, plan.block_rows, plan.stacked
     spot = base + groups * n
+    copies = []
+
+    def send(source, target):
+        copies.append(pltpu.make_async_copy(source, target, sems.at[len(copies)]))
+        copies[-1].start()
+
     squares = jnp.zeros((1, LANES), f32)
     for chunk in chunks:
         sums = chunk[spot + stride : spot + stride + PAD, :].astype(f32)
@@ -305,42 +320,46 @@
     norm = jnp.sqrt(squares)
     norm_ref[...] = norm
     factor = clip_limit / jnp.maximum(norm, clip_limit)
+    send(norm_ref, norm_out)
+
+    def shard_of(i):
+        side, k = divmod(i, plan.quads)
+        return (core ^ side) * plan.quads + (quad ^ k)
 
     for i, chunk in enumerate(chunks):
-        side, k = divmod(i, plan.quads)
-        shard = (core ^ side) * plan.quads + (quad ^ k)
-        at = pl.ds(pl.multiple_of(shard * stride, stride), stride)
+        shard = shard_of(i)
+        items = chunk[base : base + groups * n, :].astype(f32)
+        for z in range(n):
+            items_ref[shard // 2, (outer ^ z) * 2 + shard % 2] = items[z * groups : (z + 1) * groups, :]
+    wide = jnp.concatenate([factor] * groups, axis=1)
+    for t in range(3):
+        grad = jnp.concatenate([items_ref[t, :, g, :] for g in range(groups)], axis=1) * wide
+        for ref, v in zip(vec_refs, adamw(vw[t], grad, vm[t], vv[t], 0.5, 0.0)):
+            ref[t] = v
+    grad = items_ref[3, outer * 2 + inner, 0:1, :] * factor
+    for ref, v in zip(bias_refs, adamw(cs[0:1, :], grad, cs[1:2, :], cs[2:3, :], 0.1, 0.0)):
+        ref[...] = v
+    for source, target in zip(vec_refs + bias_refs, vec_outs + bias_outs):
+        send(source, target)
+
+    for i, chunk in enumerate(chunks):
+        at = pl.ds(pl.multiple_of(shard_of(i) * stride, stride), stride)
         for g in range(groups):
             lanes = slice(g * LANES, (g + 1) * LANES)
             grad = chunk[g * stride : (g + 1) * stride, :].astype(f32) * factor
-            w, m, v = adamw(bw[at, lanes], grad, bm[at, lanes], bv[at, lanes], 0.02, 0.01)
-            bw_out[at, lanes] = w
-            bm_out[at, lanes] = m
-            bv_out[at, lanes] = v
-            bcopy_out[at, lanes] = w.astype(bf16)
+            new = adamw(bw[at, lanes], grad, bm[at, lanes], bv[at, lanes], 0.02, 0.01)
+            for ref, v in zip(block_refs, new + (new[0],)):
+                ref[at, lanes] = v.astype(ref.dtype)
         grad = chunk[spot : spot + stride, :].astype(f32) * factor
-        w, m, v = adamw(hw[at, :], grad, hm[at, :], hv[at, :], 0.02, 0.01)
-        hw_out[at, :] = w
-        hm_out[at, :] = m
-        hv_out[at, :] = v
-        hcopy_out[at, :] = w.astype(bf16)
-        items = chunk[base : base + groups * n, :].astype(f32)
-        kind, member = shard // 2, shard % 2
-        for z in range(n):
-            items_ref[kind, (outer ^ z) * 2 + member] = items[z * groups : (z + 1) * groups, :]
-
-    wide = jnp.concatenate([factor] * groups, axis=1)
-    for t in range(3):
-        grad = jnp.concatenate([items_ref[t, :, g, :] for g in range(groups)], axis=1) * wide
-        w, m, v = adamw(vw[t], grad, vm[t], vv[t], 0.5, 0.0)
-        vw_out[t] = w
-        vm_out[t] = m
-        vv_out[t] = v
-    grad = items_ref[3, outer * 2 + inner, 0:1, :] * factor
-    w, m, v = adamw(cw[...], grad, cm[...], cv[...], 0.1, 0.0)
-    cw_out[...] = w
-    cm_out[...] = m
-    cv_out[...] = v
+        new = adamw(hw[at, :], grad, hm[at, :], hv[at, :], 0.02, 0.01)
+        for ref, v in zip(head_refs, new + (new[0],)):
+            ref[at, :] = v.astype(ref.dtype)
+        if i % 2:
+            both = pl.ds(pl.multiple_of(shard_of(i) // 2 * (2 * stride), 2 * stride), 2 * stride)
+            for source, target in zip(block_refs + head_refs, block_outs + head_outs):
+                send(source.at[both], target.at[both])
+    for copy in copies:
+        copy.wait()
 
 
 def on_device(
@@ -365,9 +384,8 @@
     plan = Plan(mesh, width, classes, rows)
     n, quads, stride = plan.outer, plan.quads, plan.block_rows
     shape = jax.ShapeDtypeStruct
-    obj, mem = lax.axis_index("obj"), lax.axis_index("mem")
-    outer, inner = mem // 2, mem % 2
-    place = jnp.stack([obj % 2, obj // 2 * 2 + inner, outer, inner]).astype(jnp.int32)
+    mem = lax.axis_index("mem")
+    outer = mem // 2
 
     far_feats = [plan.over_outer(features, k) for k in range(1, n)]
     head_low = head_weight[0].astype(bf16)
@@ -377,6 +395,8 @@
         jnp.arange(classes, dtype=jnp.int32)[None, :] == labels[:, None]
     ).astype(f32)
     weight_low = block_weight.astype(bf16)
+    biases = jnp.concatenate([head_bias, bias_first, bias_second], axis=0)
+    onehot, biases = lax.optimization_barrier((onehot, biases))
     pair = lax.dynamic_slice_in_dim(member_vectors, outer * 2, 2, axis=1).reshape(6, width)
 
     objs = n * rows
@@ -387,10 +407,10 @@
         [
             shape((quads, total, LANES), bf16),
             shape((quads, total, LANES), f32),
-            shape((rows, back), f32),
-        ]
-        + [shape((rows, back), bf16)] * (n - 1),
-        [place, features, *far_feats, onehot, weight_low, pair, head_low, bias_low, far_head],
+            shape((objs // 2, back), f32),
+            shape((objs // 2, back), bf16),
+        ],
+        [features, *far_feats, onehot, weight_low, pair, head_low, bias_low, far_head],
         [
             pltpu.VMEM((2 * objs, width), bf16),
             pltpu.VMEM((2 * objs, width), f32),
@@ -403,16 +423,25 @@
         ],
         name="local",
     )
-    send, keep, back_own, back_far = outs[0], outs[1], outs[2], outs[3:]
+    send, keep, back_keep, back_send = outs
 
     got = plan.over_core(send)
     own, *sends = call(
         functools.partial(core_body, plan),
         [shape((total, LANES), f32)] + [shape((total, LANES), bf16)] * (quads - 1),
-        [place, keep, got],
+        [keep, got],
         name="core_sum",
     )
     got = [plan.over_plane(v, k + 1) for k, v in enumerate(sends)]
+    for bit in plan.bits[:-1]:
+        half = back_keep.shape[0] // 2
+        back_keep, back_send = call(
+            functools.partial(half_body, plan),
+            [shape((half, back), f32), shape((half, back), bf16)],
+            [back_keep, plan.over_outer(back_send, bit)],
+            name="back_half",
+        )
+    got[0], back_send, back_keep = lax.optimization_barrier((got[0], back_send, back_keep))
     send, block, heads = call(
         functools.partial(plane_body, plan),
         [
@@ -420,41 +449,42 @@
             shape((plan.stacked + PAD, LANES), f32),
             shape((2 * stride, LANES), f32),
         ],
-        [place, own, *got],
+        [own, *got],
         name="plane_sum",
     )
     got = [plan.over_outer(send, k) for k in range(1, n)]
+    features_grad, mean_logits = call(
+        functools.partial(back_body, plan),
+        [shape((rows, width), f32), shape((rows, classes), f32)],
+        [back_keep, plan.over_outer(back_send, plan.bits[-1])],
+        name="back_sum",
+    )
+    got, features_grad, mean_logits = lax.optimization_barrier((got, features_grad, mean_logits))
     last = plan.stacked + plan.groups * n + stride + PAD
     same, flip = call(
         functools.partial(outer_body, plan),
         [shape((last, LANES), bf16)] * 2,
-        [place, block, heads, *got],
+        [block, heads, *got],
         name="outer_sum",
     )
     near = [same] + [plan.over_plane(flip if k & 1 else same, k) for k in range(1, quads)]
     far = [plan.over_core(v) for v in near]
 
-    back_got = [plan.over_outer(v, k + 1) for k, v in enumerate(back_far)]
-    features_grad, mean_logits = call(
-        functools.partial(back_body, plan),
-        [shape((rows, width), f32), shape((rows, classes), f32)],
-        [place, back_own, *back_got],
-        name="back_sum",
-    )
-
-    like = lambda v, dtype=f32: shape(v.shape, dtype)
+    like = lambda v, dtype=f32: (v.shape, dtype)
     head_w, head_m, head_v = head_weight[0], head_first[0], head_second[0]
-    (norm, bw, bm, bv, bcopy, vw, vm, vv, hw, hm, hv, hcopy, cw, cm, cv) = call(
-        functools.partial(update_body, plan),
-        [shape((1, LANES), f32)]
+    results = (
+        [((1, LANES), f32)]
         + [like(block_weight)] * 3
         + [like(block_weight, bf16)]
         + [like(member_vectors)] * 3
         + [like(head_w)] * 3
         + [like(head_w, bf16)]
-        + [like(head_bias)] * 3,
+        + [like(head_bias)] * 3
+    )
+    (norm, bw, bm, bv, bcopy, vw, vm, vv, hw, hm, hv, hcopy, cw, cm, cv) = call(
+        functools.partial(update_body, plan),
+        [shape(*r) for r in results],
         [
-            place,
             *near,
             *far,
             block_weight,
@@ -466,12 +496,15 @@
             head_w,
             head_m,
             head_v,
-            head_bias,
-            bias_first,
-            bias_second,
+            biases,
         ],
-        [pltpu.VMEM((plan.items // 2, plan.n_mem, plan.groups, LANES), f32)],
+        [pltpu.VMEM(*r) for r in results]
+        + [
+            pltpu.VMEM((plan.items // 2, plan.n_mem, plan.groups, LANES), f32),
+            pltpu.SemaphoreType.DMA((7 + 8 * plan.quads,)),
+        ],
         name="update",
+        out_spec=pl.BlockSpec(memory_space=pl.ANY),
     )
     return (
         mean_logits,

time: 60.7 us -> 49 us (0.81)
  waiting for transfers between devices: 17.9 us -> 12.5 us
  starting transfers between devices: 26.4 us -> 22.4 us
  Pallas kernels: 11.3 us -> 7.77 us
    ppermute x9 -> x8, waiting for transfers between devices: 10.4 us -> 5.1 us  [over_outer(): return lax.ppermute(v, ALL, self.perm(lambda o, m: (o, m ^ k << 1)))]
    pallas_call x6 -> x7, Pallas kernels: 11.3 us -> 7.77 us  [call(): pl.pallas_call(body, out_shape=outs, in_specs=specs, out_specs=[out_spec]...]
    ppermute x9 -> x8, starting transfers between devices: 16.3 us -> 13.4 us  [over_outer(): return lax.ppermute(v, ALL, self.perm(lambda o, m: (o, m ^ k << 1)))]
    unnamed x26 -> x28, local copies, waits for them, and re-layouts: 0.63 us -> 2.03 us
    convert_element_type x1, other arithmetic: 0.07 us -> 1.32 us  [on_device(): weight_low = block_weight.astype(bf16)]
    ppermute x5, starting transfers between devices: 1.09 us -> 0.08 us  [over_core(): return lax.ppermute(v, ALL, self.perm(lambda o, m: (o ^ 1, m)))]
    dynamic_slice x1, local copies, waits for them, and re-layouts: 0.81 us -> 0.01 us  [on_device(): lax.dynamic_slice_in_dim(member_vectors, outer * 2, 2, axis=1)]
    convert_element_type x1, other arithmetic: 0.81 us -> 0.13 us  [on_device(): onehot = (jnp.arange(classes, dtype=jnp.int32)[None, :] == labels[:, None...]
  transfers between devices with their start and end apart: 21 -> 20, of which waited for: 12 -> 11; matrix products, arithmetic and copies ran while one was open for 6% -> 6% of each run, Pallas kernels for 2% -> 2%
where the time goes in v2:
time: 49 us; the launch traced here: 48.7 us
  starting transfers between devices  22.4 us (46%)
  waiting for transfers between devices  12.5 us (26%)
  Pallas kernels  7.77 us (16%)
  other arithmetic  3.1 us (6%)
  local copies, waits for them, and re-layouts  2.05 us (4%)
  between operations  0.89 us (2%)
    ppermute x8, starting transfers between devices, over_outer(): return lax.ppermute(v, ALL, self.perm(lambda o, m: (o, m ^ k << 1)))  13.4 us
    ppermute x7, starting transfers between devices, over_plane(): lax.ppermute(v, ALL, self.perm(lambda o, m: (o ^ k >> 1 << 1, m ^ k & 1)))  8.91 us
    pallas_call x7, Pallas kernels, call(): pl.pallas_call(body, out_shape=outs, in_specs=specs, out_specs=[out_spec]...  7.77 us
    ppermute x7, waiting for transfers between devices, over_plane(): lax.ppermute(v, ALL, self.perm(lambda o, m: (o ^ k >> 1 << 1, m ^ k & 1)))  5.14 us
    ppermute x8, waiting for transfers between devices, over_outer(): return lax.ppermute(v, ALL, self.perm(lambda o, m: (o, m ^ k << 1)))  5.1 us
    ppermute x5, waiting for transfers between devices, over_core(): return lax.ppermute(v, ALL, self.perm(lambda o, m: (o ^ 1, m)))  2.27 us
    unnamed x28, local copies, waits for them, and re-layouts  2.03 us
    convert_element_type x1, other arithmetic, on_device(): weight_low = block_weight.astype(bf16)  1.32 us
  transfers between devices with their start and end apart: 20, of which 11 were waited for; matrix products, arithmetic and copies ran while one was open for 6% of the time, Pallas kernels for 2%

profile of v2, /device:TPU:0, one launch (start us, length us, event | category | flops | bytes accessed | tf_op | source)
XLA Modules:
  0.0 48.7 jit_solution(1734827873299875309)
XLA Ops:
  0.7 4.1 %collective-permute-start.1 = (bf16[64,512]{1,0:T(8,128)(2,1)}, bf16[64,512]{1,0:T(8,128)(2,1)S(1)}, u32[]{:S(2)}, u32[]{:S(2)}) collective-permute-start(bf16[64,512]{1,0:T(8,128)(2,1)} %refs_0_.1), channel_id=1, source_target_pairs={{0,4},{1,5},{2,6},{3,7},{4,0},{5,1},{6,2},{7,3},{8,12},{9,13},{10,... | collective-permute-start | bytes 196616 | tf_op jit(solution)/shard_map/ppermute | solution.py:85
  4.8 1.6 %collective-permute-start = (bf16[64,512]{1,0:T(8,128)(2,1)}, bf16[64,512]{1,0:T(8,128)(2,1)S(1)}, u32[]{:S(2)}, u32[]{:S(2)}) collective-permute-start(bf16[64,512]{1,0:T(8,128)(2,1)} %refs_0_.1), channel_id=1, source_target_pairs={{0,2},{1,3},{2,0},{3,1},{4,6},{5,7},{6,4},{7,5},{8,10},{9,11},{10,... | collective-permute-start | bytes 196616 | tf_op jit(solution)/shard_map/ppermute | solution.py:85
  6.3 0.0 collective-permute-start.2
  6.3 0.7 %convert_bitcast_fusion = bf16[128]{0:T(256)(128)(2,1)S(1)} fusion(f32[1,128]{1,0:T(1,128)} %param.25), kind=kLoop, calls=%fused_computation.4 | loop fusion | flops 128 | bytes 768 | tf_op jit(solution)/shard_map/broadcast_in_dim | solution.py:392
  7.0 1.0 %bitcast_convert_fusion.refs_7_ = bf16[512,128]{1,0:T(8,128)(2,1)S(1)} fusion(f32[1,512,128]{2,1,0:T(8,128)} %param.22), kind=kLoop, calls=%fused_computation.6 | loop fusion | flops 65536 | bytes 393216 | tf_op jit(solution)/shard_map/convert_element_type | solution.py:391
  8.0 1.8 %collective-permute-start.3 = (bf16[528,128]{1,0:T(8,128)(2,1)S(1)}, bf16[528,128]{1,0:T(8,128)(2,1)S(1)}, u32[]{:S(2)}, u32[]{:S(2)}) collective-permute-start(bf16[528,128]{1,0:T(8,128)(2,1)S(1)} %pad_maximum_fusion), channel_id=1, source_target_pairs={{0,1},{1,0},{2,3},{3,2},{4,5},{5,4},{6,7},{7,6},{8,9},{9,8},{10,11... | collective-permute-start | bytes 405512 | tf_op jit(solution)/shard_map/ppermute | solution.py:82
  9.8 0.7 %copy-done.10 = s32[512]{0:T(512)S(1)} copy-done((s32[512]{0:T(512)S(1)}, s32[512]{0:T(512)}, u32[]{:S(2)}) %copy-start.10) | copy-done | bytes 2072
  10.5 0.1 fusion.refs_4_
  10.6 0.7 %copy-done.6 = f32[3,8,512]{2,1,0:T(8,128)S(1)} copy-done((f32[3,8,512]{2,1,0:T(8,128)S(1)}, f32[3,8,512]{2,1,0:T(8,128)}, u32[]{:S(2)}) %copy-start.6) | copy-done | bytes 49176
  11.3 0.0 copy-start.11
  11.3 0.0 copy-start.12
  11.3 0.0 copy-start.13
  11.3 0.6 %copy-done.11 = f32[1,128]{1,0:T(1,128)S(1)} copy-done((f32[1,128]{1,0:T(1,128)S(1)}, f32[1,128]{1,0:T(1,128)}, u32[]{:S(2)}) %copy-start.11) | copy-done | bytes 536
  11.9 0.0 copy-done.12
  12.0 0.0 copy-done.13
  12.0 1.3 %convert_element_type.13.refs_5_ = bf16[512,512]{1,0:T(8,128)(2,1)S(1)} convert(f32[512,512]{1,0:T(8,128)} %refs_8_.1) | non-fusion elementwise | flops 262144 | bytes 1572864 | tf_op jit(solution)/shard_map/convert_element_type | solution.py:397
  13.3 0.0 collective-permute-done.1.refs_2_
  13.3 0.0 collective-permute-done.refs_1_
  13.3 0.0 collective-permute-done.2.refs_3_
  13.4 0.0 collective-permute-done.3.refs_9_
  13.4 0.0 copy-done.7
  13.4 0.0 copy-start.3
  13.4 0.0 copy-start.8
  13.4 0.0 copy-start.9
  13.4 3.8 %local.1 = (bf16[4,400,128]{2,1,0:T(8,128)(2,1)S(1)}, f32[4,400,128]{2,1,0:T(8,128)S(1)}, f32[128,640]{1,0:T(8,128)S(1)}, bf16[128,640]{1,0:T(8,128)(2,1)S(1)}) custom-call(bf16[64,512]{1,0:T(8,128)(2,1)S(1)} %copy-done.7, bf16[64,512]{1,0:T(8,128)(2,1)S(1)} %collective-permute-done.refs_1_, bf16[64,512]{1,0:T(8,128)(2,1)S(1)} %collective-permute-done.1.refs_2_, ...), custom_call_target="tpu_custom_call" | custom-call | tf_op jit(solution)/shard_map/local/pallas_call | solution.py:45
  17.2 0.1 collective-permute-start.4
  17.3 0.7 %collective-permute-start.6 = (bf16[128,640]{1,0:T(8,128)(2,1)S(1)}, bf16[128,640]{1,0:T(8,128)(2,1)S(1)}, u32[]{:S(2)}, u32[]{:S(2)}) collective-permute-start(bf16[128,640]{1,0:T(8,128)(2,1)S(1)} %get-tuple-element.65), channel_id=1, source_target_pairs={{0,2},{1,3},{2,0},{3,1},{4,6},{5,7},{6,4},{7,5},{8,10},{9,11},{10,... | collective-permute-start | bytes 491528 | tf_op jit(solution)/shard_map/ppermute | solution.py:85
  18.0 1.0 %collective-permute-done.4.got_ref = bf16[4,400,128]{2,1,0:T(8,128)(2,1)S(1)} collective-permute-done((bf16[4,400,128]{2,1,0:T(8,128)(2,1)S(1)}, bf16[4,400,128]{2,1,0:T(8,128)(2,1)S(1)}, u32[]{:S(2)}, u32[]{:S(2)}) %collective-permute-start.4) | collective-permute-done | bytes 409632 | tf_op jit(solution)/shard_map/ppermute | solution.py:79
  19.0 0.1 core_sum.1
  19.1 0.0 copy-start
  19.1 1.5 %collective-permute-start.5 = (bf16[400,128]{1,0:T(8,128)(2,1)S(1)}, bf16[400,128]{1,0:T(8,128)(2,1)S(1)}, u32[]{:S(2)}, u32[]{:S(2)}) collective-permute-start(bf16[400,128]{1,0:T(8,128)(2,1)S(1)} %get-tuple-element.63), channel_id=1, source_target_pairs={{0,1},{1,0},{2,3},{3,2},{4,5},{5,4},{6,7},{7,6},{8,9},{9,8},{10,11... | collective-permute-start | bytes 307208 | tf_op jit(solution)/shard_map/ppermute | solution.py:82
  20.6 1.5 %collective-permute-start.7 = (bf16[400,128]{1,0:T(8,128)(2,1)S(1)}, bf16[400,128]{1,0:T(8,128)(2,1)S(1)}, u32[]{:S(2)}, u32[]{:S(2)}) collective-permute-start(bf16[400,128]{1,0:T(8,128)(2,1)S(1)} %get-tuple-element.69), channel_id=1, source_target_pairs={{0,16},{1,17},{2,18},{3,19},{4,20},{5,21},{6,22},{7,23},{8,24},{9,... | collective-permute-start | bytes 307208 | tf_op jit(solution)/shard_map/ppermute | solution.py:82
  22.1 0.6 %collective-permute-start.8 = (bf16[400,128]{1,0:T(8,128)(2,1)S(1)}, bf16[400,128]{1,0:T(8,128)(2,1)S(1)}, u32[]{:S(2)}, u32[]{:S(2)}) collective-permute-start(bf16[400,128]{1,0:T(8,128)(2,1)S(1)} %get-tuple-element.70), channel_id=1, source_target_pairs={{0,17},{1,16},{2,19},{3,18},{4,21},{5,20},{6,23},{7,22},{8,25},{9,... | collective-permute-start | bytes 307208 | tf_op jit(solution)/shard_map/ppermute | solution.py:82
  22.7 1.2 %collective-permute-done.6.got_ref = bf16[128,640]{1,0:T(8,128)(2,1)S(1)} collective-permute-done((bf16[128,640]{1,0:T(8,128)(2,1)S(1)}, bf16[128,640]{1,0:T(8,128)(2,1)S(1)}, u32[]{:S(2)}, u32[]{:S(2)}) %collective-permute-start.6) | collective-permute-done | bytes 163872 | tf_op jit(solution)/shard_map/ppermute | solution.py:85
  23.9 0.2 collective-permute-done.5.refs_0_
  24.1 2.5 %collective-permute-start.12 = (bf16[64,640]{1,0:T(8,128)(2,1)S(1)}, bf16[64,640]{1,0:T(8,128)(2,1)S(1)}, u32[]{:S(2)}, u32[]{:S(2)}) collective-permute-start(bf16[64,640]{1,0:T(8,128)(2,1)S(1)} %get-tuple-element.73), channel_id=1, source_target_pairs={{0,4},{1,5},{2,6},{3,7},{4,0},{5,1},{6,2},{7,3},{8,12},{9,13},{10,... | collective-permute-start | bytes 245768 | tf_op jit(solution)/shard_map/ppermute | solution.py:85
  26.6 0.0 collective-permute-done.7.refs_1_
  26.6 1.0 %collective-permute-done.8.refs_2_ = bf16[400,128]{1,0:T(8,128)(2,1)S(1)} collective-permute-done((bf16[400,128]{1,0:T(8,128)(2,1)S(1)}, bf16[400,128]{1,0:T(8,128)(2,1)S(1)}, u32[]{:S(2)}, u32[]{:S(2)}) %collective-permute-start.8) | collective-permute-done | bytes 102432 | tf_op jit(solution)/shard_map/ppermute | solution.py:82
  27.7 0.1 plane_sum.1
  27.8 3.7 %collective-permute-start.11 = (bf16[272,128]{1,0:T(8,128)(2,1)S(1)}, bf16[272,128]{1,0:T(8,128)(2,1)S(1)}, u32[]{:S(2)}, u32[]{:S(2)}) collective-permute-start(bf16[272,128]{1,0:T(8,128)(2,1)S(1)} %get-tuple-element.71), channel_id=1, source_target_pairs={{0,6},{1,7},{2,4},{3,5},{4,2},{5,3},{6,0},{7,1},{8,14},{9,15},{10,... | collective-permute-start | bytes 208904 | tf_op jit(solution)/shard_map/ppermute | solution.py:85
  31.4 0.0 collective-permute-start.10
  31.4 0.8 %collective-permute-start.9 = (bf16[272,128]{1,0:T(8,128)(2,1)S(1)}, bf16[272,128]{1,0:T(8,128)(2,1)S(1)}, u32[]{:S(2)}, u32[]{:S(2)}) collective-permute-start(bf16[272,128]{1,0:T(8,128)(2,1)S(1)} %get-tuple-element.71), channel_id=1, source_target_pairs={{0,2},{1,3},{2,0},{3,1},{4,6},{5,7},{6,4},{7,5},{8,10},{9,11},{10,... | collective-permute-start | bytes 208904 | tf_op jit(solution)/shard_map/ppermute | solution.py:85
  32.2 0.0 collective-permute-done.12.got_ref
  32.2 0.7 %back_sum.1 = (f32[64,512]{1,0:T(8,128)}, f32[64,128]{1,0:T(8,128)}) custom-call(f32[64,640]{1,0:T(8,128)S(1)} %get-tuple-element.72.had_ref, bf16[64,640]{1,0:T(8,128)(2,1)S(1)} %collective-permute-done.12.got_ref), custom_call_target="tpu_custom_call" | custom-call | tf_op jit(solution)/shard_map/back_sum/pallas_call | solution.py:45
  32.9 1.0 %collective-permute-done.11.refs_2_ = bf16[272,128]{1,0:T(8,128)(2,1)S(1)} collective-permute-done((bf16[272,128]{1,0:T(8,128)(2,1)S(1)}, bf16[272,128]{1,0:T(8,128)(2,1)S(1)}, u32[]{:S(2)}, u32[]{:S(2)}) %collective-permute-start.11) | collective-permute-done | bytes 69664 | tf_op jit(solution)/shard_map/ppermute | solution.py:85
  33.9 2.8 %collective-permute-done.10.refs_1_ = bf16[272,128]{1,0:T(8,128)(2,1)S(1)} collective-permute-done((bf16[272,128]{1,0:T(8,128)(2,1)S(1)}, bf16[272,128]{1,0:T(8,128)(2,1)S(1)}, u32[]{:S(2)}, u32[]{:S(2)}) %collective-permute-start.10) | collective-permute-done | bytes 69664 | tf_op jit(solution)/shard_map/ppermute | solution.py:85
  36.8 0.0 collective-permute-done.9.refs_0_
  36.8 0.1 outer_sum.1
  36.9 2.3 %collective-permute-start.15 = (bf16[352,128]{1,0:T(8,128)(2,1)S(1)}, bf16[352,128]{1,0:T(8,128)(2,1)S(1)}, u32[]{:S(2)}, u32[]{:S(2)}) collective-permute-start(bf16[352,128]{1,0:T(8,128)(2,1)S(1)} %get-tuple-element.84), channel_id=1, source_target_pairs={{0,17},{1,16},{2,19},{3,18},{4,21},{5,20},{6,23},{7,22},{8,25},{9,... | collective-permute-start | bytes 270344 | tf_op jit(solution)/shard_map/ppermute | solution.py:82
  39.3 0.7 %collective-permute-start.13 = (bf16[352,128]{1,0:T(8,128)(2,1)S(1)}, bf16[352,128]{1,0:T(8,128)(2,1)S(1)}, u32[]{:S(2)}, u32[]{:S(2)}) collective-permute-start(bf16[352,128]{1,0:T(8,128)(2,1)S(1)} %get-tuple-element.84), channel_id=1, source_target_pairs={{0,1},{1,0},{2,3},{3,2},{4,5},{5,4},{6,7},{7,6},{8,9},{9,8},{10,11... | collective-permute-start | bytes 270344 | tf_op jit(solution)/shard_map/ppermute | solution.py:82
  39.9 0.6 %collective-permute-start.14 = (bf16[352,128]{1,0:T(8,128)(2,1)S(1)}, bf16[352,128]{1,0:T(8,128)(2,1)S(1)}, u32[]{:S(2)}, u32[]{:S(2)}) collective-permute-start(bf16[352,128]{1,0:T(8,128)(2,1)S(1)} %get-tuple-element.83.refs_0_), channel_id=1, source_target_pairs={{0,16},{1,17},{2,18},{3,19},{4,20},{5,21},{6,22},{7,23},{8,24},{9,... | collective-permute-start | bytes 270344 | tf_op jit(solution)/shard_map/ppermute | solution.py:82
  40.5 0.0 collective-permute-start.16
  40.5 2.6 %collective-permute-done.15.refs_3_ = bf16[352,128]{1,0:T(8,128)(2,1)S(1)} collective-permute-done((bf16[352,128]{1,0:T(8,128)(2,1)S(1)}, bf16[352,128]{1,0:T(8,128)(2,1)S(1)}, u32[]{:S(2)}, u32[]{:S(2)}) %collective-permute-start.15) | collective-permute-done | bytes 90144 | tf_op jit(solution)/shard_map/ppermute | solution.py:82
  43.1 0.0 collective-permute-start.19
  43.1 0.8 %collective-permute-done.13.refs_1_ = bf16[352,128]{1,0:T(8,128)(2,1)S(1)} collective-permute-done((bf16[352,128]{1,0:T(8,128)(2,1)S(1)}, bf16[352,128]{1,0:T(8,128)(2,1)S(1)}, u32[]{:S(2)}, u32[]{:S(2)}) %collective-permute-start.13) | collective-permute-done | bytes 90144 | tf_op jit(solution)/shard_map/ppermute | solution.py:82
  43.9 0.0 collective-permute-start.17
  43.9 0.5 %collective-permute-done.14.refs_2_ = bf16[352,128]{1,0:T(8,128)(2,1)S(1)} collective-permute-done((bf16[352,128]{1,0:T(8,128)(2,1)S(1)}, bf16[352,128]{1,0:T(8,128)(2,1)S(1)}, u32[]{:S(2)}, u32[]{:S(2)}) %collective-permute-start.14) | collective-permute-done | bytes 90144 | tf_op jit(solution)/shard_map/ppermute | solution.py:82
  44.4 0.0 collective-permute-start.18
  44.4 0.0 collective-permute-done.16.refs_4_
  44.4 0.0 collective-permute-done.19.refs_7_
  44.5 0.8 %collective-permute-done.17.refs_5_ = bf16[352,128]{1,0:T(8,128)(2,1)S(1)} collective-permute-done((bf16[352,128]{1,0:T(8,128)(2,1)S(1)}, bf16[352,128]{1,0:T(8,128)(2,1)S(1)}, u32[]{:S(2)}, u32[]{:S(2)}) %collective-permute-start.17) | collective-permute-done | bytes 90144 | tf_op jit(solution)/shard_map/ppermute | solution.py:79
  45.2 0.5 %collective-permute-done.18.refs_6_ = bf16[352,128]{1,0:T(8,128)(2,1)S(1)} collective-permute-done((bf16[352,128]{1,0:T(8,128)(2,1)S(1)}, bf16[352,128]{1,0:T(8,128)(2,1)S(1)}, u32[]{:S(2)}, u32[]{:S(2)}) %collective-permute-start.18) | collective-permute-done | bytes 90144 | tf_op jit(solution)/shard_map/ppermute | solution.py:79
  45.7 0.0 copy-done.3
  45.8 2.9 %update.1 = (f32[1,128]{1,0:T(1,128)}, f32[512,512]{1,0:T(8,128)}, f32[512,512]{1,0:T(8,128)}, f32[512,512]{1,0:T(8,128)}, bf16[512,512]{1,0:T(8,128)(2,1)}, /*i...) custom-call(bf16[352,128]{1,0:T(8,128)(2,1)S(1)} %get-tuple-element., ...), custom_call_target="tpu_custom_call" | custom-call | tf_op jit(solution)/shard_map/update/pallas_call | solution.py:45
  (20 shorter events, 0.1 us)
Async XLA Ops:
  0.7 12.7 %collective-permute-start.1 = (bf16[64,512]{1,0:T(8,128)(2,1)}, bf16[64,512]{1,0:T(8,128)(2,1)S(1)}, u32[]{:S(2)}, u32[]{:S(2)}) collective-permute-start(bf16[64,512]{1,0:T(8,128)(2,1)} %refs_0_.1), channel_id=1, source_target_pairs={{0,4},{1,5},{2,6},{3,7},{4,0},{5,1},{6,2},{7,3},{8,12},{9,13},{10,... | collective-permute-start | bytes 196616 | tf_op jit(solution)/shard_map/ppermute | solution.py:85
  4.8 8.6 %collective-permute-start = (bf16[64,512]{1,0:T(8,128)(2,1)}, bf16[64,512]{1,0:T(8,128)(2,1)S(1)}, u32[]{:S(2)}, u32[]{:S(2)}) collective-permute-start(bf16[64,512]{1,0:T(8,128)(2,1)} %refs_0_.1), channel_id=1, source_target_pairs={{0,2},{1,3},{2,0},{3,1},{4,6},{5,7},{6,4},{7,5},{8,10},{9,11},{10,... | collective-permute-start | bytes 196616 | tf_op jit(solution)/shard_map/ppermute | solution.py:85
  6.3 7.0 %collective-permute-start.2 = (bf16[64,512]{1,0:T(8,128)(2,1)}, bf16[64,512]{1,0:T(8,128)(2,1)S(1)}, u32[]{:S(2)}, u32[]{:S(2)}) collective-permute-start(bf16[64,512]{1,0:T(8,128)(2,1)} %refs_0_.1), channel_id=1, source_target_pairs={{0,6},{1,7},{2,4},{3,5},{4,2},{5,3},{6,0},{7,1},{8,14},{9,15},{10,... | collective-permute-start | bytes 196616 | tf_op jit(solution)/shard_map/ppermute | solution.py:85
  8.0 5.4 %collective-permute-start.3 = (bf16[528,128]{1,0:T(8,128)(2,1)S(1)}, bf16[528,128]{1,0:T(8,128)(2,1)S(1)}, u32[]{:S(2)}, u32[]{:S(2)}) collective-permute-start(bf16[528,128]{1,0:T(8,128)(2,1)S(1)} %pad_maximum_fusion), channel_id=1, source_target_pairs={{0,1},{1,0},{2,3},{3,2},{4,5},{5,4},{6,7},{7,6},{8,9},{9,8},{10,11... | collective-permute-start | bytes 405512 | tf_op jit(solution)/shard_map/ppermute | solution.py:82
  9.8 0.7 %copy-start.10 = (s32[512]{0:T(512)S(1)}, s32[512]{0:T(512)}, u32[]{:S(2)}) copy-start(s32[512]{0:T(512)} %param.15) | copy-start | bytes 6148
  10.5 0.8 %copy-start.6 = (f32[3,8,512]{2,1,0:T(8,128)S(1)}, f32[3,8,512]{2,1,0:T(8,128)}, u32[]{:S(2)}) copy-start(f32[3,8,512]{2,1,0:T(8,128)} %refs_11_.1) | copy-start | bytes 147460
  11.3 0.7 %copy-start.11 = (f32[1,128]{1,0:T(1,128)S(1)}, f32[1,128]{1,0:T(1,128)}, u32[]{:S(2)}) copy-start(f32[1,128]{1,0:T(1,128)} %param.25) | copy-start | bytes 1540
  11.3 0.7 %copy-start.12 = (f32[1,128]{1,0:T(1,128)S(1)}, f32[1,128]{1,0:T(1,128)}, u32[]{:S(2)}) copy-start(f32[1,128]{1,0:T(1,128)} %param.27) | copy-start | bytes 1540
  11.3 0.7 %copy-start.13 = (f32[1,128]{1,0:T(1,128)S(1)}, f32[1,128]{1,0:T(1,128)}, u32[]{:S(2)}) copy-start(f32[1,128]{1,0:T(1,128)} %param.26) | copy-start | bytes 1540
  12.0 1.4 %copy-start.7 = (bf16[64,512]{1,0:T(8,128)(2,1)S(1)}, bf16[64,512]{1,0:T(8,128)(2,1)}, u32[]{:S(2)}) copy-start(bf16[64,512]{1,0:T(8,128)(2,1)} %refs_0_.1) | copy-start | bytes 196612
  13.4 32.4 %copy-start.3 = (f32[512,512]{1,0:T(8,128)S(1)}, f32[512,512]{1,0:T(8,128)}, u32[]{:S(2)}) copy-start(f32[512,512]{1,0:T(8,128)} %refs_10_.1) | copy-start | bytes 3145732
  13.4 32.4 %copy-start.8 = (f32[3,8,512]{2,1,0:T(8,128)S(1)}, f32[3,8,512]{2,1,0:T(8,128)}, u32[]{:S(2)}) copy-start(f32[3,8,512]{2,1,0:T(8,128)} %refs_12_.1) | copy-start | bytes 147460
  13.4 32.3 %copy-start.9 = (f32[3,8,512]{2,1,0:T(8,128)S(1)}, f32[3,8,512]{2,1,0:T(8,128)}, u32[]{:S(2)}) copy-start(f32[3,8,512]{2,1,0:T(8,128)} %refs_13_.1) | copy-start | bytes 147460
  17.2 1.8 %collective-permute-start.4 = (bf16[4,400,128]{2,1,0:T(8,128)(2,1)S(1)}, bf16[4,400,128]{2,1,0:T(8,128)(2,1)S(1)}, u32[]{:S(2)}, u32[]{:S(2)}) collective-permute-start(bf16[4,400,128]{2,1,0:T(8,128)(2,1)S(1)} %get-tuple-element.61), channel_id=1, source_target_pairs={{0,8},{1,9},{2,10},{3,11},{4,12},{5,13},{6,14},{7,15},{8,0},{9,1},... | collective-permute-start | bytes 1228808 | tf_op jit(solution)/shard_map/ppermute | solution.py:79
  17.3 6.6 %collective-permute-start.6 = (bf16[128,640]{1,0:T(8,128)(2,1)S(1)}, bf16[128,640]{1,0:T(8,128)(2,1)S(1)}, u32[]{:S(2)}, u32[]{:S(2)}) collective-permute-start(bf16[128,640]{1,0:T(8,128)(2,1)S(1)} %get-tuple-element.65), channel_id=1, source_target_pairs={{0,2},{1,3},{2,0},{3,1},{4,6},{5,7},{6,4},{7,5},{8,10},{9,11},{10,... | collective-permute-start | bytes 491528 | tf_op jit(solution)/shard_map/ppermute | solution.py:85
  19.0 26.7 %copy-start.2 = (f32[512,512]{1,0:T(8,128)S(1)}, f32[512,512]{1,0:T(8,128)}, u32[]{:S(2)}) copy-start(f32[512,512]{1,0:T(8,128)} %refs_9_.1) | copy-start | bytes 3145732
  19.0 26.8 %copy-start.5 = (f32[1,512,128]{2,1,0:T(8,128)S(1)}, f32[1,512,128]{2,1,0:T(8,128)}, u32[]{:S(2)}) copy-start(f32[1,512,128]{2,1,0:T(8,128)} %param.24) | copy-start | bytes 786436
  19.1 26.7 %copy-start = (f32[512,512]{1,0:T(8,128)S(1)}, f32[512,512]{1,0:T(8,128)}, u32[]{:S(2)}) copy-start(f32[512,512]{1,0:T(8,128)} %refs_8_.1) | copy-start | bytes 3145732
  19.1 5.0 %collective-permute-start.5 = (bf16[400,128]{1,0:T(8,128)(2,1)S(1)}, bf16[400,128]{1,0:T(8,128)(2,1)S(1)}, u32[]{:S(2)}, u32[]{:S(2)}) collective-permute-start(bf16[400,128]{1,0:T(8,128)(2,1)S(1)} %get-tuple-element.63), channel_id=1, source_target_pairs={{0,1},{1,0},{2,3},{3,2},{4,5},{5,4},{6,7},{7,6},{8,9},{9,8},{10,11... | collective-permute-start | bytes 307208 | tf_op jit(solution)/shard_map/ppermute | solution.py:82
  20.6 6.0 %collective-permute-start.7 = (bf16[400,128]{1,0:T(8,128)(2,1)S(1)}, bf16[400,128]{1,0:T(8,128)(2,1)S(1)}, u32[]{:S(2)}, u32[]{:S(2)}) collective-permute-start(bf16[400,128]{1,0:T(8,128)(2,1)S(1)} %get-tuple-element.69), channel_id=1, source_target_pairs={{0,16},{1,17},{2,18},{3,19},{4,20},{5,21},{6,22},{7,23},{8,24},{9,... | collective-permute-start | bytes 307208 | tf_op jit(solution)/shard_map/ppermute | solution.py:82
  22.1 5.6 %collective-permute-start.8 = (bf16[400,128]{1,0:T(8,128)(2,1)S(1)}, bf16[400,128]{1,0:T(8,128)(2,1)S(1)}, u32[]{:S(2)}, u32[]{:S(2)}) collective-permute-start(bf16[400,128]{1,0:T(8,128)(2,1)S(1)} %get-tuple-element.70), channel_id=1, source_target_pairs={{0,17},{1,16},{2,19},{3,18},{4,21},{5,20},{6,23},{7,22},{8,25},{9,... | collective-permute-start | bytes 307208 | tf_op jit(solution)/shard_map/ppermute | solution.py:82
  24.1 8.1 %collective-permute-start.12 = (bf16[64,640]{1,0:T(8,128)(2,1)S(1)}, bf16[64,640]{1,0:T(8,128)(2,1)S(1)}, u32[]{:S(2)}, u32[]{:S(2)}) collective-permute-start(bf16[64,640]{1,0:T(8,128)(2,1)S(1)} %get-tuple-element.73), channel_id=1, source_target_pairs={{0,4},{1,5},{2,6},{3,7},{4,0},{5,1},{6,2},{7,3},{8,12},{9,13},{10,... | collective-permute-start | bytes 245768 | tf_op jit(solution)/shard_map/ppermute | solution.py:85
  27.8 6.2 %collective-permute-start.11 = (bf16[272,128]{1,0:T(8,128)(2,1)S(1)}, bf16[272,128]{1,0:T(8,128)(2,1)S(1)}, u32[]{:S(2)}, u32[]{:S(2)}) collective-permute-start(bf16[272,128]{1,0:T(8,128)(2,1)S(1)} %get-tuple-element.71), channel_id=1, source_target_pairs={{0,6},{1,7},{2,4},{3,5},{4,2},{5,3},{6,0},{7,1},{8,14},{9,15},{10,... | collective-permute-start | bytes 208904 | tf_op jit(solution)/shard_map/ppermute | solution.py:85
  31.4 5.4 %collective-permute-start.10 = (bf16[272,128]{1,0:T(8,128)(2,1)S(1)}, bf16[272,128]{1,0:T(8,128)(2,1)S(1)}, u32[]{:S(2)}, u32[]{:S(2)}) collective-permute-start(bf16[272,128]{1,0:T(8,128)(2,1)S(1)} %get-tuple-element.71), channel_id=1, source_target_pairs={{0,4},{1,5},{2,6},{3,7},{4,0},{5,1},{6,2},{7,3},{8,12},{9,13},{10,... | collective-permute-start | bytes 208904 | tf_op jit(solution)/shard_map/ppermute | solution.py:85
  31.4 5.4 %collective-permute-start.9 = (bf16[272,128]{1,0:T(8,128)(2,1)S(1)}, bf16[272,128]{1,0:T(8,128)(2,1)S(1)}, u32[]{:S(2)}, u32[]{:S(2)}) collective-permute-start(bf16[272,128]{1,0:T(8,128)(2,1)S(1)} %get-tuple-element.71), channel_id=1, source_target_pairs={{0,2},{1,3},{2,0},{3,1},{4,6},{5,7},{6,4},{7,5},{8,10},{9,11},{10,... | collective-permute-start | bytes 208904 | tf_op jit(solution)/shard_map/ppermute | solution.py:85
  32.2 13.5 %copy-start.4 = (f32[1,512,128]{2,1,0:T(8,128)S(1)}, f32[1,512,128]{2,1,0:T(8,128)}, u32[]{:S(2)}) copy-start(f32[1,512,128]{2,1,0:T(8,128)} %param.23) | copy-start | bytes 786436
  32.9 12.9 %copy-start.1 = (f32[1,512,128]{2,1,0:T(8,128)S(1)}, f32[1,512,128]{2,1,0:T(8,128)}, u32[]{:S(2)}) copy-start(f32[1,512,128]{2,1,0:T(8,128)} %param.22) | copy-start | bytes 786436
  36.9 6.2 %collective-permute-start.15 = (bf16[352,128]{1,0:T(8,128)(2,1)S(1)}, bf16[352,128]{1,0:T(8,128)(2,1)S(1)}, u32[]{:S(2)}, u32[]{:S(2)}) collective-permute-start(bf16[352,128]{1,0:T(8,128)(2,1)S(1)} %get-tuple-element.84), channel_id=1, source_target_pairs={{0,17},{1,16},{2,19},{3,18},{4,21},{5,20},{6,23},{7,22},{8,25},{9,... | collective-permute-start | bytes 270344 | tf_op jit(solution)/shard_map/ppermute | solution.py:82
  39.3 4.7 %collective-permute-start.13 = (bf16[352,128]{1,0:T(8,128)(2,1)S(1)}, bf16[352,128]{1,0:T(8,128)(2,1)S(1)}, u32[]{:S(2)}, u32[]{:S(2)}) collective-permute-start(bf16[352,128]{1,0:T(8,128)(2,1)S(1)} %get-tuple-element.84), channel_id=1, source_target_pairs={{0,1},{1,0},{2,3},{3,2},{4,5},{5,4},{6,7},{7,6},{8,9},{9,8},{10,11... | collective-permute-start | bytes 270344 | tf_op jit(solution)/shard_map/ppermute | solution.py:82
  39.9 4.5 %collective-permute-start.14 = (bf16[352,128]{1,0:T(8,128)(2,1)S(1)}, bf16[352,128]{1,0:T(8,128)(2,1)S(1)}, u32[]{:S(2)}, u32[]{:S(2)}) collective-permute-start(bf16[352,128]{1,0:T(8,128)(2,1)S(1)} %get-tuple-element.83.refs_0_), channel_id=1, source_target_pairs={{0,16},{1,17},{2,18},{3,19},{4,20},{5,21},{6,22},{7,23},{8,24},{9,... | collective-permute-start | bytes 270344 | tf_op jit(solution)/shard_map/ppermute | solution.py:82
  40.5 4.0 %collective-permute-start.16 = (bf16[352,128]{1,0:T(8,128)(2,1)S(1)}, bf16[352,128]{1,0:T(8,128)(2,1)S(1)}, u32[]{:S(2)}, u32[]{:S(2)}) collective-permute-start(bf16[352,128]{1,0:T(8,128)(2,1)S(1)} %get-tuple-element.83.refs_0_), channel_id=1, source_target_pairs={{0,8},{1,9},{2,10},{3,11},{4,12},{5,13},{6,14},{7,15},{8,0},{9,1},... | collective-permute-start | bytes 270344 | tf_op jit(solution)/shard_map/ppermute | solution.py:79
  43.1 1.4 %collective-permute-start.19 = (bf16[352,128]{1,0:T(8,128)(2,1)S(1)}, bf16[352,128]{1,0:T(8,128)(2,1)S(1)}, u32[]{:S(2)}, u32[]{:S(2)}) collective-permute-start(bf16[352,128]{1,0:T(8,128)(2,1)S(1)} %collective-permute-done.15.refs_3_), channel_id=1, source_target_pairs={{0,8},{1,9},{2,10},{3,11},{4,12},{5,13},{6,14},{7,15},{8,0},{9,1},... | collective-permute-start | bytes 270344 | tf_op jit(solution)/shard_map/ppermute | solution.py:79
  43.9 1.3 %collective-permute-start.17 = (bf16[352,128]{1,0:T(8,128)(2,1)S(1)}, bf16[352,128]{1,0:T(8,128)(2,1)S(1)}, u32[]{:S(2)}, u32[]{:S(2)}) collective-permute-start(bf16[352,128]{1,0:T(8,128)(2,1)S(1)} %collective-permute-done.13.refs_1_), channel_id=1, source_target_pairs={{0,8},{1,9},{2,10},{3,11},{4,12},{5,13},{6,14},{7,15},{8,0},{9,1},... | collective-permute-start | bytes 270344 | tf_op jit(solution)/shard_map/ppermute | solution.py:79
  44.4 1.3 %collective-permute-start.18 = (bf16[352,128]{1,0:T(8,128)(2,1)S(1)}, bf16[352,128]{1,0:T(8,128)(2,1)S(1)}, u32[]{:S(2)}, u32[]{:S(2)}) collective-permute-start(bf16[352,128]{1,0:T(8,128)(2,1)S(1)} %collective-permute-done.14.refs_2_), channel_id=1, source_target_pairs={{0,8},{1,9},{2,10},{3,11},{4,12},{5,13},{6,14},{7,15},{8,0},{9,1},... | collective-permute-start | bytes 270344 | tf_op jit(solution)/shard_map/ppermute | solution.py:79

commit v3 on v2

--- a/solution.py
+++ b/solution.py
@@ -30,10 +30,11 @@
 def adamw(weight, grad, first, second, rate, decay):
     first_new = beta_one * first + (1.0 - beta_one) * grad
     second_new = beta_two * second + (1.0 - beta_two) * grad * grad
-    fix_one = 1.0 - beta_one**STEP
-    fix_two = 1.0 - beta_two**STEP
-    step_size = first_new / fix_one / (jnp.sqrt(second_new / fix_two) + epsilon)
-    return (weight - rate * (step_size + decay * weight), first_new, second_new)
+    fix_one = 1.0 / (1.0 - beta_one**STEP)
+    fix_two = 1.0 / (1.0 - beta_two**STEP)
+    root = lax.rsqrt(second_new * fix_two)
+    step_size = first_new * root * (rate * fix_one) / (1.0 + epsilon * root)
+    return (weight * (1.0 - rate * decay) - step_size, first_new, second_new)
 
 
 def dot(a, b, dims=((1,), (0,))):
@@ -85,22 +86,36 @@
         return lax.ppermute(v, ALL, self.perm(lambda o, m: (o, m ^ (k << 1))))
 
 
+def head_body(plan, head_ref, bias_ref, low_ref):
+    low_ref[0 : plan.width, :] = head_ref[...].astype(bf16)
+    low_ref[plan.width :, :] = jnp.broadcast_to(bias_ref[...], (PAD, plan.classes)).astype(bf16)
+
+
+def low_body(plan, weight_ref, bias_ref, first_ref, second_ref, low_ref, biases_ref):
+    low_ref[...] = weight_ref[...].astype(bf16)
+    for i, ref in enumerate((bias_ref, first_ref, second_ref)):
+        biases_ref[i : i + 1, :] = ref[...]
+
+
 def local_body(plan, *refs):
     n = plan.outer
     feats = refs[:n]
-    onehot_ref, weight_ref, vec_ref, own_head, own_bias, far_head = refs[n : n + 6]
-    send_ref, keep_ref = refs[n + 6 : n + 8]
-    back_keep, back_send = refs[n + 8 : n + 10]
+    onehot_ref, weight_ref, vec_ref, own_head, far_head = refs[n : n + 5]
+    send_ref, keep_ref = refs[n + 5 : n + 7]
+    back_keep, back_send = refs[n + 7 : n + 9]
     lifted_ref, mixed_ref, hidden_ref, slope_ref, dmixed_ref, block_ref, heads_ref, items_ref = refs[
-        n + 10 :
+        n + 9 :
     ]
     rows, width, classes = plan.rows, plan.width, plan.classes
     objs = n * rows
     core, quad, outer, inner = place_of()
     tile = 16
 
+    def member(j):
+        return pl.ds(outer * 2 + j, 1)
+
     for j in range(2):
-        scale_r = vec_ref[j : j + 1, :]
+        scale_r = vec_ref[0, member(j), :]
         for k in range(n):
             lifted_ref[j * objs + k * rows : j * objs + (k + 1) * rows, :] = (
                 feats[k][...].astype(f32) * scale_r
@@ -109,27 +124,27 @@
 
     items_ref[...] = jnp.zeros_like(items_ref)
     for j in range(2):
-        scale_s = vec_ref[2 + j : 3 + j, :]
-        shift_b = vec_ref[4 + j : 5 + j, :]
+        scale_s = vec_ref[1, member(j), :]
+        shift_b = vec_ref[2, member(j), :]
 
         def forward(t, carry):
             at = pl.ds(pl.multiple_of(j * objs + t * tile, tile), tile)
             pre = mixed_ref[at, :] * scale_s + shift_b
             square = pre * pre
-            bend = jnp.tanh(gelu_in * (pre + gelu_cube * square * pre))
-            hidden_ref[at, :] = (0.5 * pre * (1.0 + bend)).astype(bf16)
-            slope_ref[at, :] = 0.5 * (1.0 + bend) + (0.5 * gelu_in) * pre * (1.0 - bend * bend) * (
-                1.0 + (3.0 * gelu_cube) * square
+            half = 0.5 + 0.5 * jnp.tanh(pre * (gelu_in + (gelu_in * gelu_cube) * square))
+            hidden_ref[at, :] = (pre * half).astype(bf16)
+            slope_ref[at, :] = half + (half - half * half) * (
+                pre * (2.0 * gelu_in + (6.0 * gelu_in * gelu_cube) * square)
             )
             return carry
 
-        lax.fori_loop(0, objs // tile, forward, 0, unroll=2)
+        lax.fori_loop(0, objs // tile, forward, 0, unroll=min(objs // tile, 16))
 
     logit_sum = None
     for j in range(2):
         mine = inner == j
-        head = jnp.where(mine, own_head[...], far_head[0:width, :])
-        bias = jnp.where(mine, own_bias[0:1, :], far_head[width : width + 1, :]).astype(f32)
+        head = jnp.where(mine, own_head[0:width, :], far_head[0:width, :])
+        bias = jnp.where(mine, own_head[width : width + 1, :], far_head[width : width + 1, :]).astype(f32)
         hidden = hidden_ref[j * objs : (j + 1) * objs, :]
         logits = dot(hidden, head) + bias
         logit_sum = logits if logit_sum is None else logit_sum + logits
@@ -149,7 +164,7 @@
         heads_ref[j] = dot(hidden, dlow, ((0,), (0,)))
         mixed_back = dot(dlow, head, ((1,), (1,)))
         block_ref[0:objs, :] = mixed_back
-        scale_s = vec_ref[2 + j : 3 + j, :]
+        scale_s = vec_ref[1, member(j), :]
 
         def backward(t, carry):
             s_sum, b_sum = carry
@@ -160,7 +175,7 @@
             return s_sum + dpre * mixed_ref[at, :], b_sum + dpre
 
         zero = jnp.zeros((tile, width), f32)
-        s_sum, b_sum = lax.fori_loop(0, objs // tile, backward, (zero, zero), unroll=2)
+        s_sum, b_sum = lax.fori_loop(0, objs // tile, backward, (zero, zero), unroll=min(objs // tile, 16))
         s_grad = jnp.sum(s_sum, axis=0, keepdims=True)
         b_grad = jnp.sum(b_sum, axis=0, keepdims=True)
         for g in range(plan.groups):
@@ -168,7 +183,6 @@
             items_ref[2 + j, g : g + 1, :] = s_grad[:, at]
             items_ref[4 + j, g : g + 1, :] = b_grad[:, at]
 
-    block_ref[0:width, :] = dot(lifted_ref[...], dmixed_ref[...], ((0,), (0,)))
     slope_ref[...] = dot(dmixed_ref[...], weight_ref[...], ((1,), (1,)))
     r_sums = [jnp.zeros((1, width), f32) for _ in range(2)]
     for spot, k in enumerate(plan.halving):
@@ -177,7 +191,7 @@
         for j in range(2):
             lift_back = slope_ref[j * objs + k * rows : j * objs + (k + 1) * rows, :]
             r_sums[j] = r_sums[j] + jnp.sum(lift_back * feat, axis=0, keepdims=True)
-            part = lift_back * vec_ref[j : j + 1, :]
+            part = lift_back * vec_ref[0, member(j), :]
             back = part if back is None else back + part
         out = back_keep if spot < n // 2 else back_send
         at = slice(spot % (n // 2) * rows, (spot % (n // 2) + 1) * rows)
@@ -188,14 +202,17 @@
             items_ref[j, g : g + 1, :] = r_sums[j][:, g * LANES : (g + 1) * LANES]
 
     stride = plan.block_rows
+    half = width // 2
     for out, side in ((keep_ref, core), (send_ref, 1 - core)):
+        part = dot(lifted_ref[:, pl.ds(pl.multiple_of(side * half, half), half)], dmixed_ref[...], ((0,), (0,)))
+        for k in range(plan.quads):
+            for g in range(plan.groups):
+                out[quad ^ k, g * stride : (g + 1) * stride, :] = part[
+                    k * stride : (k + 1) * stride, g * LANES : (g + 1) * LANES
+                ].astype(out.dtype)
         for k in range(plan.quads):
             shard = side * plan.quads + (quad ^ k)
             at = pl.ds(pl.multiple_of(shard * stride, stride), stride)
-            for g in range(plan.groups):
-                out[k, g * stride : (g + 1) * stride, :] = block_ref[
-                    at, g * LANES : (g + 1) * LANES
-                ].astype(out.dtype)
             base = plan.stacked
             for j in range(2):
                 out[k, base : base + stride, :] = heads_ref[j, at, :].astype(out.dtype)
@@ -327,22 +344,6 @@
         return (core ^ side) * plan.quads + (quad ^ k)
 
     for i, chunk in enumerate(chunks):
-        shard = shard_of(i)
-        items = chunk[base : base + groups * n, :].astype(f32)
-        for z in range(n):
-            items_ref[shard // 2, (outer ^ z) * 2 + shard % 2] = items[z * groups : (z + 1) * groups, :]
-    wide = jnp.concatenate([factor] * groups, axis=1)
-    for t in range(3):
-        grad = jnp.concatenate([items_ref[t, :, g, :] for g in range(groups)], axis=1) * wide
-        for ref, v in zip(vec_refs, adamw(vw[t], grad, vm[t], vv[t], 0.5, 0.0)):
-            ref[t] = v
-    grad = items_ref[3, outer * 2 + inner, 0:1, :] * factor
-    for ref, v in zip(bias_refs, adamw(cs[0:1, :], grad, cs[1:2, :], cs[2:3, :], 0.1, 0.0)):
-        ref[...] = v
-    for source, target in zip(vec_refs + bias_refs, vec_outs + bias_outs):
-        send(source, target)
-
-    for i, chunk in enumerate(chunks):
         at = pl.ds(pl.multiple_of(shard_of(i) * stride, stride), stride)
         for g in range(groups):
             lanes = slice(g * LANES, (g + 1) * LANES)
@@ -358,6 +359,22 @@
             both = pl.ds(pl.multiple_of(shard_of(i) // 2 * (2 * stride), 2 * stride), 2 * stride)
             for source, target in zip(block_refs + head_refs, block_outs + head_outs):
                 send(source.at[both], target.at[both])
+    for i, chunk in enumerate(chunks):
+        shard = shard_of(i)
+        items = chunk[base : base + groups * n, :].astype(f32)
+        for z in range(n):
+            items_ref[shard // 2, (outer ^ z) * 2 + shard % 2] = items[z * groups : (z + 1) * groups, :]
+    wide = jnp.concatenate([factor] * groups, axis=1)
+    for t in range(3):
+        grad = jnp.concatenate([items_ref[t, :, g, :] for g in range(groups)], axis=1) * wide
+        for ref, v in zip(vec_refs, adamw(vw[t], grad, vm[t], vv[t], 0.5, 0.0)):
+            ref[t] = v
+    grad = items_ref[3, outer * 2 + inner, 0:1, :] * factor
+    for ref, v in zip(bias_refs, adamw(cs[0:1, :], grad, cs[1:2, :], cs[2:3, :], 0.1, 0.0)):
+        ref[...] = v
+    for source, target in zip(vec_refs + bias_refs, vec_outs + bias_outs):
+        send(source, target)
+
     for copy in copies:
         copy.wait()
 
@@ -384,20 +401,24 @@
     plan = Plan(mesh, width, classes, rows)
     n, quads, stride = plan.outer, plan.quads, plan.block_rows
     shape = jax.ShapeDtypeStruct
-    mem = lax.axis_index("mem")
-    outer = mem // 2
 
     far_feats = [plan.over_outer(features, k) for k in range(1, n)]
-    head_low = head_weight[0].astype(bf16)
-    bias_low = jnp.broadcast_to(head_bias.astype(bf16), (PAD, classes))
-    far_head = plan.over_plane(jnp.concatenate([head_low, bias_low], axis=0), 1)
+    (own_head,) = call(
+        functools.partial(head_body, plan),
+        [shape((width + PAD, classes), bf16)],
+        [head_weight[0], head_bias],
+        name="head_low",
+    )
+    far_head = plan.over_plane(own_head, 1)
+    weight_low, biases = call(
+        functools.partial(low_body, plan),
+        [shape((width, width), bf16), shape((3, classes), f32)],
+        [block_weight, head_bias, bias_first, bias_second],
+        name="weight_low",
+    )
     onehot = (
         jnp.arange(classes, dtype=jnp.int32)[None, :] == labels[:, None]
     ).astype(f32)
-    weight_low = block_weight.astype(bf16)
-    biases = jnp.concatenate([head_bias, bias_first, bias_second], axis=0)
-    onehot, biases = lax.optimization_barrier((onehot, biases))
-    pair = lax.dynamic_slice_in_dim(member_vectors, outer * 2, 2, axis=1).reshape(6, width)
 
     objs = n * rows
     total = plan.stacked + 2 * stride + PAD
@@ -410,7 +431,7 @@
             shape((objs // 2, back), f32),
             shape((objs // 2, back), bf16),
         ],
-        [features, *far_feats, onehot, weight_low, pair, head_low, bias_low, far_head],
+        [features, *far_feats, onehot, weight_low, member_vectors, own_head, far_head],
         [
             pltpu.VMEM((2 * objs, width), bf16),
             pltpu.VMEM((2 * objs, width), f32),

time: 49 us -> 46.6 us (0.951)
  other arithmetic: 3.1 us -> 0.13 us
  waiting for transfers between devices: 12.5 us -> 14.5 us
  Pallas kernels: 7.77 us -> 6.21 us
    convert_element_type x2 -> x0, other arithmetic: 2.29 us -> none  [the longest x1 1.32 us: on_device(): weight_low = block_weight.astype(bf16)]
    ppermute x8, waiting for transfers between devices: 5.1 us -> 7.02 us  [over_outer(): return lax.ppermute(v, ALL, self.perm(lambda o, m: (o, m ^ k << 1)))]
    pallas_call x7 -> x9, Pallas kernels: 7.77 us -> 6.21 us  [call(): pl.pallas_call(body, out_shape=outs, in_specs=specs, out_specs=[out_spec]...]
    broadcast_in_dim x1 -> x0, other arithmetic: 0.66 us -> none  [on_device(): bias_low = jnp.broadcast_to(head_bias.astype(bf16), (PAD, classes))]
    unnamed x28 -> x32, local copies, waits for them, and re-layouts: 2.03 us -> 2.24 us
  transfers between devices with their start and end apart: 20 -> 20, of which waited for: 11 -> 12; matrix products, arithmetic and copies ran while one was open for 6% -> 0% of each run, Pallas kernels for 2% -> 2%
where the time goes in v3:
time: 46.6 us; the launch traced here: 46.4 us
  starting transfers between devices  22.4 us (48%)
  waiting for transfers between devices  14.5 us (31%)
  Pallas kernels  6.21 us (13%)
  local copies, waits for them, and re-layouts  2.24 us (5%)
  between operations  0.86 us (2%)
    ppermute x8, starting transfers between devices, over_outer(): return lax.ppermute(v, ALL, self.perm(lambda o, m: (o, m ^ k << 1)))  13.4 us
    ppermute x7, starting transfers between devices, over_plane(): lax.ppermute(v, ALL, self.perm(lambda o, m: (o ^ k >> 1 << 1, m ^ k & 1)))  8.91 us
    ppermute x8, waiting for transfers between devices, over_outer(): return lax.ppermute(v, ALL, self.perm(lambda o, m: (o, m ^ k << 1)))  7.02 us
    pallas_call x9, Pallas kernels, call(): pl.pallas_call(body, out_shape=outs, in_specs=specs, out_specs=[out_spec]...  6.21 us
    ppermute x7, waiting for transfers between devices, over_plane(): lax.ppermute(v, ALL, self.perm(lambda o, m: (o ^ k >> 1 << 1, m ^ k & 1)))  5.21 us
    ppermute x5, waiting for transfers between devices, over_core(): return lax.ppermute(v, ALL, self.perm(lambda o, m: (o ^ 1, m)))  2.24 us
    unnamed x32, local copies, waits for them, and re-layouts  2.24 us
  transfers between devices with their start and end apart: 20, of which 12 were waited for; matrix products, arithmetic and copies ran while one was open for 0% of the time, Pallas kernels for 2%

profile of v3, /device:TPU:0, one launch (start us, length us, event | category | flops | bytes accessed | tf_op | source)
XLA Modules:
  0.0 46.4 jit_solution(12346370862581154092)
XLA Ops:
  0.7 4.1 %collective-permute-start.1 = (bf16[64,512]{1,0:T(8,128)(2,1)}, bf16[64,512]{1,0:T(8,128)(2,1)S(1)}, u32[]{:S(2)}, u32[]{:S(2)}) collective-permute-start(bf16[64,512]{1,0:T(8,128)(2,1)} %refs_0_.1), channel_id=1, source_target_pairs={{0,4},{1,5},{2,6},{3,7},{4,0},{5,1},{6,2},{7,3},{8,12},{9,13},{10,... | collective-permute-start | bytes 196616 | tf_op jit(solution)/shard_map/ppermute | solution.py:86
  4.8 1.6 %collective-permute-start = (bf16[64,512]{1,0:T(8,128)(2,1)}, bf16[64,512]{1,0:T(8,128)(2,1)S(1)}, u32[]{:S(2)}, u32[]{:S(2)}) collective-permute-start(bf16[64,512]{1,0:T(8,128)(2,1)} %refs_0_.1), channel_id=1, source_target_pairs={{0,2},{1,3},{2,0},{3,1},{4,6},{5,7},{6,4},{7,5},{8,10},{9,11},{10,... | collective-permute-start | bytes 196616 | tf_op jit(solution)/shard_map/ppermute | solution.py:86
  6.3 0.0 collective-permute-start.2
  6.4 0.9 %copy-done.2 = f32[1,512,128]{2,1,0:T(8,128)S(1)} copy-done((f32[1,512,128]{2,1,0:T(8,128)S(1)}, f32[1,512,128]{2,1,0:T(8,128)}, u32[]{:S(2)}) %copy-start.2) | copy-done | bytes 262168
  7.3 0.0 copy-start.13
  7.3 0.0 copy-start.14
  7.3 1.8 %collective-permute-start.3 = (bf16[528,128]{1,0:T(8,128)(2,1)S(1)}, bf16[528,128]{1,0:T(8,128)(2,1)S(1)}, u32[]{:S(2)}, u32[]{:S(2)}) collective-permute-start(bf16[528,128]{1,0:T(8,128)(2,1)S(1)} %head_low.1.refs_7_), channel_id=1, source_target_pairs={{0,1},{1,0},{2,3},{3,2},{4,5},{5,4},{6,7},{7,6},{8,9},{9,8},{10,11... | collective-permute-start | bytes 405512 | tf_op jit(solution)/shard_map/ppermute | solution.py:83
  9.2 0.1 fusion.refs_4_
  9.3 0.0 copy-done.13
  9.3 0.0 copy-done.14
  9.3 0.0 copy-start
  9.3 1.2 %copy-done = f32[512,512]{1,0:T(8,128)S(1)} copy-done((f32[512,512]{1,0:T(8,128)S(1)}, f32[512,512]{1,0:T(8,128)}, u32[]{:S(2)}) %copy-start) | copy-done | bytes 1048600
  10.5 0.1 weight_low.1
  10.6 0.0 collective-permute-done.1.refs_2_
  10.6 0.0 collective-permute-done.refs_1_
  10.6 2.0 %collective-permute-done.2.refs_3_ = bf16[64,512]{1,0:T(8,128)(2,1)S(1)} collective-permute-done((bf16[64,512]{1,0:T(8,128)(2,1)}, bf16[64,512]{1,0:T(8,128)(2,1)S(1)}, u32[]{:S(2)}, u32[]{:S(2)}) %collective-permute-start.2) | collective-permute-done | bytes 65568 | tf_op jit(solution)/shard_map/ppermute | solution.py:86
  12.6 0.0 collective-permute-done.3.refs_8_
  12.6 0.0 copy-done.9
  12.6 0.0 copy-start.5
  12.6 0.0 copy-start.10
  12.7 0.0 copy-start.11
  12.7 2.3 %local.1 = (bf16[4,400,128]{2,1,0:T(8,128)(2,1)S(1)}, f32[4,400,128]{2,1,0:T(8,128)S(1)}, f32[128,640]{1,0:T(8,128)S(1)}, bf16[128,640]{1,0:T(8,128)(2,1)S(1)}) custom-call(bf16[64,512]{1,0:T(8,128)(2,1)S(1)} %copy-done.9, bf16[64,512]{1,0:T(8,128)(2,1)S(1)} %collective-permute-done.refs_1_, bf16[64,512]{1,0:T(8,128)(2,1)S(1)} %collective-permute-done.1.refs_2_, ...), custom_call_target="tpu_custom_call" | custom-call | tf_op jit(solution)/shard_map/local/pallas_call | solution.py:46
  15.0 0.1 collective-permute-start.4
  15.1 0.7 %collective-permute-start.6 = (bf16[128,640]{1,0:T(8,128)(2,1)S(1)}, bf16[128,640]{1,0:T(8,128)(2,1)S(1)}, u32[]{:S(2)}, u32[]{:S(2)}) collective-permute-start(bf16[128,640]{1,0:T(8,128)(2,1)S(1)} %get-tuple-element.65), channel_id=1, source_target_pairs={{0,2},{1,3},{2,0},{3,1},{4,6},{5,7},{6,4},{7,5},{8,10},{9,11},{10,... | collective-permute-start | bytes 491528 | tf_op jit(solution)/shard_map/ppermute | solution.py:86
  15.8 1.0 %collective-permute-done.4.got_ref = bf16[4,400,128]{2,1,0:T(8,128)(2,1)S(1)} collective-permute-done((bf16[4,400,128]{2,1,0:T(8,128)(2,1)S(1)}, bf16[4,400,128]{2,1,0:T(8,128)(2,1)S(1)}, u32[]{:S(2)}, u32[]{:S(2)}) %collective-permute-start.4) | collective-permute-done | bytes 409632 | tf_op jit(solution)/shard_map/ppermute | solution.py:80
  16.8 0.1 core_sum.1
  16.9 0.0 copy-start.1
  16.9 1.6 %collective-permute-start.5 = (bf16[400,128]{1,0:T(8,128)(2,1)S(1)}, bf16[400,128]{1,0:T(8,128)(2,1)S(1)}, u32[]{:S(2)}, u32[]{:S(2)}) collective-permute-start(bf16[400,128]{1,0:T(8,128)(2,1)S(1)} %get-tuple-element.63), channel_id=1, source_target_pairs={{0,1},{1,0},{2,3},{3,2},{4,5},{5,4},{6,7},{7,6},{8,9},{9,8},{10,11... | collective-permute-start | bytes 307208 | tf_op jit(solution)/shard_map/ppermute | solution.py:83
  18.5 1.5 %collective-permute-start.7 = (bf16[400,128]{1,0:T(8,128)(2,1)S(1)}, bf16[400,128]{1,0:T(8,128)(2,1)S(1)}, u32[]{:S(2)}, u32[]{:S(2)}) collective-permute-start(bf16[400,128]{1,0:T(8,128)(2,1)S(1)} %get-tuple-element.69), channel_id=1, source_target_pairs={{0,16},{1,17},{2,18},{3,19},{4,20},{5,21},{6,22},{7,23},{8,24},{9,... | collective-permute-start | bytes 307208 | tf_op jit(solution)/shard_map/ppermute | solution.py:83
  20.0 0.5 %collective-permute-start.8 = (bf16[400,128]{1,0:T(8,128)(2,1)S(1)}, bf16[400,128]{1,0:T(8,128)(2,1)S(1)}, u32[]{:S(2)}, u32[]{:S(2)}) collective-permute-start(bf16[400,128]{1,0:T(8,128)(2,1)S(1)} %get-tuple-element.70), channel_id=1, source_target_pairs={{0,17},{1,16},{2,19},{3,18},{4,21},{5,20},{6,23},{7,22},{8,25},{9,... | collective-permute-start | bytes 307208 | tf_op jit(solution)/shard_map/ppermute | solution.py:83
  20.5 1.2 %collective-permute-done.6.got_ref = bf16[128,640]{1,0:T(8,128)(2,1)S(1)} collective-permute-done((bf16[128,640]{1,0:T(8,128)(2,1)S(1)}, bf16[128,640]{1,0:T(8,128)(2,1)S(1)}, u32[]{:S(2)}, u32[]{:S(2)}) %collective-permute-start.6) | collective-permute-done | bytes 163872 | tf_op jit(solution)/shard_map/ppermute | solution.py:86
  21.7 0.2 collective-permute-done.5.refs_0_
  21.9 2.5 %collective-permute-start.12 = (bf16[64,640]{1,0:T(8,128)(2,1)S(1)}, bf16[64,640]{1,0:T(8,128)(2,1)S(1)}, u32[]{:S(2)}, u32[]{:S(2)}) collective-permute-start(bf16[64,640]{1,0:T(8,128)(2,1)S(1)} %get-tuple-element.73), channel_id=1, source_target_pairs={{0,4},{1,5},{2,6},{3,7},{4,0},{5,1},{6,2},{7,3},{8,12},{9,13},{10,... | collective-permute-start | bytes 245768 | tf_op jit(solution)/shard_map/ppermute | solution.py:86
  24.5 0.0 collective-permute-done.7.refs_1_
  24.5 1.1 %collective-permute-done.8.refs_2_ = bf16[400,128]{1,0:T(8,128)(2,1)S(1)} collective-permute-done((bf16[400,128]{1,0:T(8,128)(2,1)S(1)}, bf16[400,128]{1,0:T(8,128)(2,1)S(1)}, u32[]{:S(2)}, u32[]{:S(2)}) %collective-permute-start.8) | collective-permute-done | bytes 102432 | tf_op jit(solution)/shard_map/ppermute | solution.py:83
  25.6 0.1 plane_sum.1
  25.7 3.7 %collective-permute-start.11 = (bf16[272,128]{1,0:T(8,128)(2,1)S(1)}, bf16[272,128]{1,0:T(8,128)(2,1)S(1)}, u32[]{:S(2)}, u32[]{:S(2)}) collective-permute-start(bf16[272,128]{1,0:T(8,128)(2,1)S(1)} %get-tuple-element.71), channel_id=1, source_target_pairs={{0,6},{1,7},{2,4},{3,5},{4,2},{5,3},{6,0},{7,1},{8,14},{9,15},{10,... | collective-permute-start | bytes 208904 | tf_op jit(solution)/shard_map/ppermute | solution.py:86
  29.3 0.0 collective-permute-start.10
  29.3 0.8 %collective-permute-start.9 = (bf16[272,128]{1,0:T(8,128)(2,1)S(1)}, bf16[272,128]{1,0:T(8,128)(2,1)S(1)}, u32[]{:S(2)}, u32[]{:S(2)}) collective-permute-start(bf16[272,128]{1,0:T(8,128)(2,1)S(1)} %get-tuple-element.71), channel_id=1, source_target_pairs={{0,2},{1,3},{2,0},{3,1},{4,6},{5,7},{6,4},{7,5},{8,10},{9,11},{10,... | collective-permute-start | bytes 208904 | tf_op jit(solution)/shard_map/ppermute | solution.py:86
  30.1 0.0 collective-permute-done.12.got_ref
  30.1 0.7 %back_sum.1 = (f32[64,512]{1,0:T(8,128)}, f32[64,128]{1,0:T(8,128)}) custom-call(f32[64,640]{1,0:T(8,128)S(1)} %get-tuple-element.72.had_ref, bf16[64,640]{1,0:T(8,128)(2,1)S(1)} %collective-permute-done.12.got_ref), custom_call_target="tpu_custom_call" | custom-call | tf_op jit(solution)/shard_map/back_sum/pallas_call | solution.py:46
  30.8 1.0 %collective-permute-done.11.refs_2_ = bf16[272,128]{1,0:T(8,128)(2,1)S(1)} collective-permute-done((bf16[272,128]{1,0:T(8,128)(2,1)S(1)}, bf16[272,128]{1,0:T(8,128)(2,1)S(1)}, u32[]{:S(2)}, u32[]{:S(2)}) %collective-permute-start.11) | collective-permute-done | bytes 69664 | tf_op jit(solution)/shard_map/ppermute | solution.py:86
  31.9 2.8 %collective-permute-done.10.refs_1_ = bf16[272,128]{1,0:T(8,128)(2,1)S(1)} collective-permute-done((bf16[272,128]{1,0:T(8,128)(2,1)S(1)}, bf16[272,128]{1,0:T(8,128)(2,1)S(1)}, u32[]{:S(2)}, u32[]{:S(2)}) %collective-permute-start.10) | collective-permute-done | bytes 69664 | tf_op jit(solution)/shard_map/ppermute | solution.py:86
  34.6 0.0 collective-permute-done.9.refs_0_
  34.6 0.1 outer_sum.1
  34.8 2.4 %collective-permute-start.15 = (bf16[352,128]{1,0:T(8,128)(2,1)S(1)}, bf16[352,128]{1,0:T(8,128)(2,1)S(1)}, u32[]{:S(2)}, u32[]{:S(2)}) collective-permute-start(bf16[352,128]{1,0:T(8,128)(2,1)S(1)} %get-tuple-element.84), channel_id=1, source_target_pairs={{0,17},{1,16},{2,19},{3,18},{4,21},{5,20},{6,23},{7,22},{8,25},{9,... | collective-permute-start | bytes 270344 | tf_op jit(solution)/shard_map/ppermute | solution.py:83
  37.2 0.5 %collective-permute-start.13 = (bf16[352,128]{1,0:T(8,128)(2,1)S(1)}, bf16[352,128]{1,0:T(8,128)(2,1)S(1)}, u32[]{:S(2)}, u32[]{:S(2)}) collective-permute-start(bf16[352,128]{1,0:T(8,128)(2,1)S(1)} %get-tuple-element.84), channel_id=1, source_target_pairs={{0,1},{1,0},{2,3},{3,2},{4,5},{5,4},{6,7},{7,6},{8,9},{9,8},{10,11... | collective-permute-start | bytes 270344 | tf_op jit(solution)/shard_map/ppermute | solution.py:83
  37.7 0.6 %collective-permute-start.14 = (bf16[352,128]{1,0:T(8,128)(2,1)S(1)}, bf16[352,128]{1,0:T(8,128)(2,1)S(1)}, u32[]{:S(2)}, u32[]{:S(2)}) collective-permute-start(bf16[352,128]{1,0:T(8,128)(2,1)S(1)} %get-tuple-element.83.refs_0_), channel_id=1, source_target_pairs={{0,16},{1,17},{2,18},{3,19},{4,20},{5,21},{6,22},{7,23},{8,24},{9,... | collective-permute-start | bytes 270344 | tf_op jit(solution)/shard_map/ppermute | solution.py:83
  38.3 0.0 collective-permute-start.16
  38.3 2.5 %collective-permute-done.15.refs_3_ = bf16[352,128]{1,0:T(8,128)(2,1)S(1)} collective-permute-done((bf16[352,128]{1,0:T(8,128)(2,1)S(1)}, bf16[352,128]{1,0:T(8,128)(2,1)S(1)}, u32[]{:S(2)}, u32[]{:S(2)}) %collective-permute-start.15) | collective-permute-done | bytes 90144 | tf_op jit(solution)/shard_map/ppermute | solution.py:83
  40.9 0.0 collective-permute-start.19
  40.9 0.9 %collective-permute-done.13.refs_1_ = bf16[352,128]{1,0:T(8,128)(2,1)S(1)} collective-permute-done((bf16[352,128]{1,0:T(8,128)(2,1)S(1)}, bf16[352,128]{1,0:T(8,128)(2,1)S(1)}, u32[]{:S(2)}, u32[]{:S(2)}) %collective-permute-start.13) | collective-permute-done | bytes 90144 | tf_op jit(solution)/shard_map/ppermute | solution.py:83
  41.8 0.0 collective-permute-start.17
  41.8 0.5 %collective-permute-done.14.refs_2_ = bf16[352,128]{1,0:T(8,128)(2,1)S(1)} collective-permute-done((bf16[352,128]{1,0:T(8,128)(2,1)S(1)}, bf16[352,128]{1,0:T(8,128)(2,1)S(1)}, u32[]{:S(2)}, u32[]{:S(2)}) %collective-permute-start.14) | collective-permute-done | bytes 90144 | tf_op jit(solution)/shard_map/ppermute | solution.py:83
  42.3 0.0 collective-permute-start.18
  42.3 0.0 collective-permute-done.16.refs_4_
  42.3 0.0 collective-permute-done.19.refs_7_
  42.3 0.8 %collective-permute-done.17.refs_5_ = bf16[352,128]{1,0:T(8,128)(2,1)S(1)} collective-permute-done((bf16[352,128]{1,0:T(8,128)(2,1)S(1)}, bf16[352,128]{1,0:T(8,128)(2,1)S(1)}, u32[]{:S(2)}, u32[]{:S(2)}) %collective-permute-start.17) | collective-permute-done | bytes 90144 | tf_op jit(solution)/shard_map/ppermute | solution.py:80
  43.1 0.5 %collective-permute-done.18.refs_6_ = bf16[352,128]{1,0:T(8,128)(2,1)S(1)} collective-permute-done((bf16[352,128]{1,0:T(8,128)(2,1)S(1)}, bf16[352,128]{1,0:T(8,128)(2,1)S(1)}, u32[]{:S(2)}, u32[]{:S(2)}) %collective-permute-start.18) | collective-permute-done | bytes 90144 | tf_op jit(solution)/shard_map/ppermute | solution.py:80
  43.6 0.0 copy-done.4
  43.6 0.0 copy-done.7
  43.6 0.0 copy-done.1
  43.6 0.0 copy-done.6
  43.6 2.8 %update.1 = (f32[1,128]{1,0:T(1,128)}, f32[512,512]{1,0:T(8,128)}, f32[512,512]{1,0:T(8,128)}, f32[512,512]{1,0:T(8,128)}, bf16[512,512]{1,0:T(8,128)(2,1)}, /*i...) custom-call(bf16[352,128]{1,0:T(8,128)(2,1)S(1)} %get-tuple-element., ...), custom_call_target="tpu_custom_call" | custom-call | tf_op jit(solution)/shard_map/update/pallas_call | solution.py:46
  (18 shorter events, 0.1 us)
Async XLA Ops:
  0.7 5.7 %copy-start.12 = (f32[1,128]{1,0:T(1,128)S(1)}, f32[1,128]{1,0:T(1,128)}, u32[]{:S(2)}) copy-start(f32[1,128]{1,0:T(1,128)} %bias_ref.3) | copy-start | bytes 1540
  0.7 9.9 %collective-permute-start.1 = (bf16[64,512]{1,0:T(8,128)(2,1)}, bf16[64,512]{1,0:T(8,128)(2,1)S(1)}, u32[]{:S(2)}, u32[]{:S(2)}) collective-permute-start(bf16[64,512]{1,0:T(8,128)(2,1)} %refs_0_.1), channel_id=1, source_target_pairs={{0,4},{1,5},{2,6},{3,7},{4,0},{5,1},{6,2},{7,3},{8,12},{9,13},{10,... | collective-permute-start | bytes 196616 | tf_op jit(solution)/shard_map/ppermute | solution.py:86
  4.8 5.8 %collective-permute-start = (bf16[64,512]{1,0:T(8,128)(2,1)}, bf16[64,512]{1,0:T(8,128)(2,1)S(1)}, u32[]{:S(2)}, u32[]{:S(2)}) collective-permute-start(bf16[64,512]{1,0:T(8,128)(2,1)} %refs_0_.1), channel_id=1, source_target_pairs={{0,2},{1,3},{2,0},{3,1},{4,6},{5,7},{6,4},{7,5},{8,10},{9,11},{10,... | collective-permute-start | bytes 196616 | tf_op jit(solution)/shard_map/ppermute | solution.py:86
  6.3 6.3 %collective-permute-start.2 = (bf16[64,512]{1,0:T(8,128)(2,1)}, bf16[64,512]{1,0:T(8,128)(2,1)S(1)}, u32[]{:S(2)}, u32[]{:S(2)}) collective-permute-start(bf16[64,512]{1,0:T(8,128)(2,1)} %refs_0_.1), channel_id=1, source_target_pairs={{0,6},{1,7},{2,4},{3,5},{4,2},{5,3},{6,0},{7,1},{8,14},{9,15},{10,... | collective-permute-start | bytes 196616 | tf_op jit(solution)/shard_map/ppermute | solution.py:86
  6.3 1.0 %copy-start.2 = (f32[1,512,128]{2,1,0:T(8,128)S(1)}, f32[1,512,128]{2,1,0:T(8,128)}, u32[]{:S(2)}) copy-start(f32[1,512,128]{2,1,0:T(8,128)} %param.22) | copy-start | bytes 786436
  7.3 1.9 %copy-start.15 = (s32[512]{0:T(512)S(1)}, s32[512]{0:T(512)}, u32[]{:S(2)}) copy-start(s32[512]{0:T(512)} %param.15) | copy-start | bytes 6148
  7.3 2.0 %copy-start.13 = (f32[1,128]{1,0:T(1,128)S(1)}, f32[1,128]{1,0:T(1,128)}, u32[]{:S(2)}) copy-start(f32[1,128]{1,0:T(1,128)} %first_ref.1) | copy-start | bytes 1540
  7.3 2.0 %copy-start.14 = (f32[1,128]{1,0:T(1,128)S(1)}, f32[1,128]{1,0:T(1,128)}, u32[]{:S(2)}) copy-start(f32[1,128]{1,0:T(1,128)} %second_ref.1) | copy-start | bytes 1540
  7.3 5.3 %collective-permute-start.3 = (bf16[528,128]{1,0:T(8,128)(2,1)S(1)}, bf16[528,128]{1,0:T(8,128)(2,1)S(1)}, u32[]{:S(2)}, u32[]{:S(2)}) collective-permute-start(bf16[528,128]{1,0:T(8,128)(2,1)S(1)} %head_low.1.refs_7_), channel_id=1, source_target_pairs={{0,1},{1,0},{2,3},{3,2},{4,5},{5,4},{6,7},{7,6},{8,9},{9,8},{10,11... | collective-permute-start | bytes 405512 | tf_op jit(solution)/shard_map/ppermute | solution.py:83
  9.3 1.2 %copy-start = (f32[512,512]{1,0:T(8,128)S(1)}, f32[512,512]{1,0:T(8,128)}, u32[]{:S(2)}) copy-start(f32[512,512]{1,0:T(8,128)} %refs_8_.1) | copy-start | bytes 3145732
  10.5 2.1 %copy-start.8 = (f32[3,8,512]{2,1,0:T(8,128)S(1)}, f32[3,8,512]{2,1,0:T(8,128)}, u32[]{:S(2)}) copy-start(f32[3,8,512]{2,1,0:T(8,128)} %refs_11_.1) | copy-start | bytes 147460
  10.5 2.1 %copy-start.9 = (bf16[64,512]{1,0:T(8,128)(2,1)S(1)}, bf16[64,512]{1,0:T(8,128)(2,1)}, u32[]{:S(2)}) copy-start(bf16[64,512]{1,0:T(8,128)(2,1)} %refs_0_.1) | copy-start | bytes 196612
  12.6 30.9 %copy-start.5 = (f32[512,512]{1,0:T(8,128)S(1)}, f32[512,512]{1,0:T(8,128)}, u32[]{:S(2)}) copy-start(f32[512,512]{1,0:T(8,128)} %refs_10_.1) | copy-start | bytes 3145732
  12.6 30.9 %copy-start.10 = (f32[3,8,512]{2,1,0:T(8,128)S(1)}, f32[3,8,512]{2,1,0:T(8,128)}, u32[]{:S(2)}) copy-start(f32[3,8,512]{2,1,0:T(8,128)} %refs_12_.1) | copy-start | bytes 147460
  12.7 30.9 %copy-start.11 = (f32[3,8,512]{2,1,0:T(8,128)S(1)}, f32[3,8,512]{2,1,0:T(8,128)}, u32[]{:S(2)}) copy-start(f32[3,8,512]{2,1,0:T(8,128)} %refs_13_.1) | copy-start | bytes 147460
  15.0 1.8 %collective-permute-start.4 = (bf16[4,400,128]{2,1,0:T(8,128)(2,1)S(1)}, bf16[4,400,128]{2,1,0:T(8,128)(2,1)S(1)}, u32[]{:S(2)}, u32[]{:S(2)}) collective-permute-start(bf16[4,400,128]{2,1,0:T(8,128)(2,1)S(1)} %get-tuple-element.61), channel_id=1, source_target_pairs={{0,8},{1,9},{2,10},{3,11},{4,12},{5,13},{6,14},{7,15},{8,0},{9,1},... | collective-permute-start | bytes 1228808 | tf_op jit(solution)/shard_map/ppermute | solution.py:80
  15.1 6.6 %collective-permute-start.6 = (bf16[128,640]{1,0:T(8,128)(2,1)S(1)}, bf16[128,640]{1,0:T(8,128)(2,1)S(1)}, u32[]{:S(2)}, u32[]{:S(2)}) collective-permute-start(bf16[128,640]{1,0:T(8,128)(2,1)S(1)} %get-tuple-element.65), channel_id=1, source_target_pairs={{0,2},{1,3},{2,0},{3,1},{4,6},{5,7},{6,4},{7,5},{8,10},{9,11},{10,... | collective-permute-start | bytes 491528 | tf_op jit(solution)/shard_map/ppermute | solution.py:86
  16.8 26.8 %copy-start.4 = (f32[512,512]{1,0:T(8,128)S(1)}, f32[512,512]{1,0:T(8,128)}, u32[]{:S(2)}) copy-start(f32[512,512]{1,0:T(8,128)} %refs_9_.1) | copy-start | bytes 3145732
  16.8 26.8 %copy-start.7 = (f32[1,512,128]{2,1,0:T(8,128)S(1)}, f32[1,512,128]{2,1,0:T(8,128)}, u32[]{:S(2)}) copy-start(f32[1,512,128]{2,1,0:T(8,128)} %param.24) | copy-start | bytes 786436
  16.9 26.7 %copy-start.1 = (f32[512,512]{1,0:T(8,128)S(1)}, f32[512,512]{1,0:T(8,128)}, u32[]{:S(2)}) copy-start(f32[512,512]{1,0:T(8,128)} %refs_8_.1) | copy-start | bytes 3145732
  16.9 5.0 %collective-permute-start.5 = (bf16[400,128]{1,0:T(8,128)(2,1)S(1)}, bf16[400,128]{1,0:T(8,128)(2,1)S(1)}, u32[]{:S(2)}, u32[]{:S(2)}) collective-permute-start(bf16[400,128]{1,0:T(8,128)(2,1)S(1)} %get-tuple-element.63), channel_id=1, source_target_pairs={{0,1},{1,0},{2,3},{3,2},{4,5},{5,4},{6,7},{7,6},{8,9},{9,8},{10,11... | collective-permute-start | bytes 307208 | tf_op jit(solution)/shard_map/ppermute | solution.py:83
  18.5 5.9 %collective-permute-start.7 = (bf16[400,128]{1,0:T(8,128)(2,1)S(1)}, bf16[400,128]{1,0:T(8,128)(2,1)S(1)}, u32[]{:S(2)}, u32[]{:S(2)}) collective-permute-start(bf16[400,128]{1,0:T(8,128)(2,1)S(1)} %get-tuple-element.69), channel_id=1, source_target_pairs={{0,16},{1,17},{2,18},{3,19},{4,20},{5,21},{6,22},{7,23},{8,24},{9,... | collective-permute-start | bytes 307208 | tf_op jit(solution)/shard_map/ppermute | solution.py:83
  20.0 5.6 %collective-permute-start.8 = (bf16[400,128]{1,0:T(8,128)(2,1)S(1)}, bf16[400,128]{1,0:T(8,128)(2,1)S(1)}, u32[]{:S(2)}, u32[]{:S(2)}) collective-permute-start(bf16[400,128]{1,0:T(8,128)(2,1)S(1)} %get-tuple-element.70), channel_id=1, source_target_pairs={{0,17},{1,16},{2,19},{3,18},{4,21},{5,20},{6,23},{7,22},{8,25},{9,... | collective-permute-start | bytes 307208 | tf_op jit(solution)/shard_map/ppermute | solution.py:83
  21.9 8.2 %collective-permute-start.12 = (bf16[64,640]{1,0:T(8,128)(2,1)S(1)}, bf16[64,640]{1,0:T(8,128)(2,1)S(1)}, u32[]{:S(2)}, u32[]{:S(2)}) collective-permute-start(bf16[64,640]{1,0:T(8,128)(2,1)S(1)} %get-tuple-element.73), channel_id=1, source_target_pairs={{0,4},{1,5},{2,6},{3,7},{4,0},{5,1},{6,2},{7,3},{8,12},{9,13},{10,... | collective-permute-start | bytes 245768 | tf_op jit(solution)/shard_map/ppermute | solution.py:86
  25.7 6.2 %collective-permute-start.11 = (bf16[272,128]{1,0:T(8,128)(2,1)S(1)}, bf16[272,128]{1,0:T(8,128)(2,1)S(1)}, u32[]{:S(2)}, u32[]{:S(2)}) collective-permute-start(bf16[272,128]{1,0:T(8,128)(2,1)S(1)} %get-tuple-element.71), channel_id=1, source_target_pairs={{0,6},{1,7},{2,4},{3,5},{4,2},{5,3},{6,0},{7,1},{8,14},{9,15},{10,... | collective-permute-start | bytes 208904 | tf_op jit(solution)/shard_map/ppermute | solution.py:86
  29.3 5.3 %collective-permute-start.10 = (bf16[272,128]{1,0:T(8,128)(2,1)S(1)}, bf16[272,128]{1,0:T(8,128)(2,1)S(1)}, u32[]{:S(2)}, u32[]{:S(2)}) collective-permute-start(bf16[272,128]{1,0:T(8,128)(2,1)S(1)} %get-tuple-element.71), channel_id=1, source_target_pairs={{0,4},{1,5},{2,6},{3,7},{4,0},{5,1},{6,2},{7,3},{8,12},{9,13},{10,... | collective-permute-start | bytes 208904 | tf_op jit(solution)/shard_map/ppermute | solution.py:86
  29.3 5.3 %collective-permute-start.9 = (bf16[272,128]{1,0:T(8,128)(2,1)S(1)}, bf16[272,128]{1,0:T(8,128)(2,1)S(1)}, u32[]{:S(2)}, u32[]{:S(2)}) collective-permute-start(bf16[272,128]{1,0:T(8,128)(2,1)S(1)} %get-tuple-element.71), channel_id=1, source_target_pairs={{0,2},{1,3},{2,0},{3,1},{4,6},{5,7},{6,4},{7,5},{8,10},{9,11},{10,... | collective-permute-start | bytes 208904 | tf_op jit(solution)/shard_map/ppermute | solution.py:86
  30.1 13.4 %copy-start.6 = (f32[1,512,128]{2,1,0:T(8,128)S(1)}, f32[1,512,128]{2,1,0:T(8,128)}, u32[]{:S(2)}) copy-start(f32[1,512,128]{2,1,0:T(8,128)} %param.23) | copy-start | bytes 786436
  30.8 12.8 %copy-start.3 = (f32[1,512,128]{2,1,0:T(8,128)S(1)}, f32[1,512,128]{2,1,0:T(8,128)}, u32[]{:S(2)}) copy-start(f32[1,512,128]{2,1,0:T(8,128)} %param.22) | copy-start | bytes 786436
  34.8 6.1 %collective-permute-start.15 = (bf16[352,128]{1,0:T(8,128)(2,1)S(1)}, bf16[352,128]{1,0:T(8,128)(2,1)S(1)}, u32[]{:S(2)}, u32[]{:S(2)}) collective-permute-start(bf16[352,128]{1,0:T(8,128)(2,1)S(1)} %get-tuple-element.84), channel_id=1, source_target_pairs={{0,17},{1,16},{2,19},{3,18},{4,21},{5,20},{6,23},{7,22},{8,25},{9,... | collective-permute-start | bytes 270344 | tf_op jit(solution)/shard_map/ppermute | solution.py:83
  37.2 4.6 %collective-permute-start.13 = (bf16[352,128]{1,0:T(8,128)(2,1)S(1)}, bf16[352,128]{1,0:T(8,128)(2,1)S(1)}, u32[]{:S(2)}, u32[]{:S(2)}) collective-permute-start(bf16[352,128]{1,0:T(8,128)(2,1)S(1)} %get-tuple-element.84), channel_id=1, source_target_pairs={{0,1},{1,0},{2,3},{3,2},{4,5},{5,4},{6,7},{7,6},{8,9},{9,8},{10,11... | collective-permute-start | bytes 270344 | tf_op jit(solution)/shard_map/ppermute | solution.py:83
  37.7 4.5 %collective-permute-start.14 = (bf16[352,128]{1,0:T(8,128)(2,1)S(1)}, bf16[352,128]{1,0:T(8,128)(2,1)S(1)}, u32[]{:S(2)}, u32[]{:S(2)}) collective-permute-start(bf16[352,128]{1,0:T(8,128)(2,1)S(1)} %get-tuple-element.83.refs_0_), channel_id=1, source_target_pairs={{0,16},{1,17},{2,18},{3,19},{4,20},{5,21},{6,22},{7,23},{8,24},{9,... | collective-permute-start | bytes 270344 | tf_op jit(solution)/shard_map/ppermute | solution.py:83
  38.3 4.0 %collective-permute-start.16 = (bf16[352,128]{1,0:T(8,128)(2,1)S(1)}, bf16[352,128]{1,0:T(8,128)(2,1)S(1)}, u32[]{:S(2)}, u32[]{:S(2)}) collective-permute-start(bf16[352,128]{1,0:T(8,128)(2,1)S(1)} %get-tuple-element.83.refs_0_), channel_id=1, source_target_pairs={{0,8},{1,9},{2,10},{3,11},{4,12},{5,13},{6,14},{7,15},{8,0},{9,1},... | collective-permute-start | bytes 270344 | tf_op jit(solution)/shard_map/ppermute | solution.py:80
  40.9 1.4 %collective-permute-start.19 = (bf16[352,128]{1,0:T(8,128)(2,1)S(1)}, bf16[352,128]{1,0:T(8,128)(2,1)S(1)}, u32[]{:S(2)}, u32[]{:S(2)}) collective-permute-start(bf16[352,128]{1,0:T(8,128)(2,1)S(1)} %collective-permute-done.15.refs_3_), channel_id=1, source_target_pairs={{0,8},{1,9},{2,10},{3,11},{4,12},{5,13},{6,14},{7,15},{8,0},{9,1},... | collective-permute-start | bytes 270344 | tf_op jit(solution)/shard_map/ppermute | solution.py:80
  41.8 1.3 %collective-permute-start.17 = (bf16[352,128]{1,0:T(8,128)(2,1)S(1)}, bf16[352,128]{1,0:T(8,128)(2,1)S(1)}, u32[]{:S(2)}, u32[]{:S(2)}) collective-permute-start(bf16[352,128]{1,0:T(8,128)(2,1)S(1)} %collective-permute-done.13.refs_1_), channel_id=1, source_target_pairs={{0,8},{1,9},{2,10},{3,11},{4,12},{5,13},{6,14},{7,15},{8,0},{9,1},... | collective-permute-start | bytes 270344 | tf_op jit(solution)/shard_map/ppermute | solution.py:80
  42.3 1.3 %collective-permute-start.18 = (bf16[352,128]{1,0:T(8,128)(2,1)S(1)}, bf16[352,128]{1,0:T(8,128)(2,1)S(1)}, u32[]{:S(2)}, u32[]{:S(2)}) collective-permute-start(bf16[352,128]{1,0:T(8,128)(2,1)S(1)} %collective-permute-done.14.refs_2_), channel_id=1, source_target_pairs={{0,8},{1,9},{2,10},{3,11},{4,12},{5,13},{6,14},{7,15},{8,0},{9,1},... | collective-permute-start | bytes 270344 | tf_op jit(solution)/shard_map/ppermute | solution.py:80

commit v4 on v3

--- a/solution.py
+++ b/solution.py
@@ -41,14 +41,15 @@
     return lax.dot_general(a, b, (dims, ((), ())), preferred_element_type=f32)
 
 
-def call(body, outs, args, scratch=(), name=None, out_spec=VMEM):
-    specs = [VMEM] * len(args)
+def call(body, outs, args, scratch=(), name=None, out_spec=VMEM, aliases=None, in_hbm=()):
+    specs = [pl.BlockSpec(memory_space=pl.ANY) if i in in_hbm else VMEM for i in range(len(args))]
     return pl.pallas_call(
         body,
         out_shape=outs,
         in_specs=specs,
         out_specs=[out_spec] * len(outs),
         scratch_shapes=list(scratch),
+        input_output_aliases=aliases or {},
         compiler_params=pltpu.CompilerParams(vmem_limit_bytes=40 * MIB),
         name=name,
     )(*args)
@@ -86,9 +87,12 @@
         return lax.ppermute(v, ALL, self.perm(lambda o, m: (o, m ^ (k << 1))))
 
 
-def head_body(plan, head_ref, bias_ref, low_ref):
+def head_body(plan, head_ref, bias_ref, low_ref, held_ref, sem):
+    copy = pltpu.make_async_copy(bias_ref, held_ref, sem)
+    copy.start()
     low_ref[0 : plan.width, :] = head_ref[...].astype(bf16)
-    low_ref[plan.width :, :] = jnp.broadcast_to(bias_ref[...], (PAD, plan.classes)).astype(bf16)
+    copy.wait()
+    low_ref[plan.width :, :] = jnp.broadcast_to(held_ref[...], (PAD, plan.classes)).astype(bf16)
 
 
 def low_body(plan, weight_ref, bias_ref, first_ref, second_ref, low_ref, biases_ref):
@@ -97,38 +101,23 @@
         biases_ref[i : i + 1, :] = ref[...]
 
 
-def local_body(plan, *refs):
-    n = plan.outer
-    feats = refs[:n]
-    onehot_ref, weight_ref, vec_ref, own_head, far_head = refs[n : n + 5]
-    send_ref, keep_ref = refs[n + 5 : n + 7]
-    back_keep, back_send = refs[n + 7 : n + 9]
-    lifted_ref, mixed_ref, hidden_ref, slope_ref, dmixed_ref, block_ref, heads_ref, items_ref = refs[
-        n + 9 :
-    ]
-    rows, width, classes = plan.rows, plan.width, plan.classes
-    objs = n * rows
-    core, quad, outer, inner = place_of()
+def forward_body(plan, pieces, *refs):
+    feats, (weight_ref, vec_ref) = refs[: len(pieces)], refs[len(pieces) : len(pieces) + 2]
+    lifted_ref, mixed_ref, hidden_ref, slope_ref = refs[-4:]
+    rows, objs = plan.rows, plan.outer * plan.rows
+    outer = place_of()[2]
     tile = 16
-
-    def member(j):
-        return pl.ds(outer * 2 + j, 1)
-
     for j in range(2):
-        scale_r = vec_ref[0, member(j), :]
-        for k in range(n):
+        scale_r, scale_s, shift_b = (vec_ref[t, pl.ds(outer * 2 + j, 1), :] for t in range(3))
+        first, last = j * objs + pieces[0] * rows, j * objs + (pieces[-1] + 1) * rows
+        for k, feat in zip(pieces, feats):
             lifted_ref[j * objs + k * rows : j * objs + (k + 1) * rows, :] = (
-                feats[k][...].astype(f32) * scale_r
+                feat[...].astype(f32) * scale_r
             ).astype(bf16)
-    mixed_ref[...] = dot(lifted_ref[...], weight_ref[...])
-
-    items_ref[...] = jnp.zeros_like(items_ref)
-    for j in range(2):
-        scale_s = vec_ref[1, member(j), :]
-        shift_b = vec_ref[2, member(j), :]
+        mixed_ref[first:last, :] = dot(lifted_ref[first:last, :], weight_ref[...])
 
         def forward(t, carry):
-            at = pl.ds(pl.multiple_of(j * objs + t * tile, tile), tile)
+            at = pl.ds(pl.multiple_of(first + t * tile, tile), tile)
             pre = mixed_ref[at, :] * scale_s + shift_b
             square = pre * pre
             half = 0.5 + 0.5 * jnp.tanh(pre * (gelu_in + (gelu_in * gelu_cube) * square))
@@ -138,8 +127,26 @@
             )
             return carry
 
-        lax.fori_loop(0, objs // tile, forward, 0, unroll=min(objs // tile, 16))
-
+        steps = (last - first) // tile
+        lax.fori_loop(0, steps, forward, 0, unroll=min(steps, 16))
+
+
+def local_body(plan, *refs):
+    n = plan.outer
+    feats = refs[:n]
+    onehot_ref, weight_ref, vec_ref, own_head, far_head = refs[n : n + 5]
+    lifted_ref, mixed_ref, hidden_ref, slope_ref = refs[n + 5 : n + 9]
+    send_ref, keep_ref, back_keep, back_send = refs[n + 9 : n + 13]
+    dmixed_ref, block_ref, heads_ref, items_ref = refs[n + 13 :]
+    rows, width, classes = plan.rows, plan.width, plan.classes
+    objs = n * rows
+    core, quad, outer, inner = place_of()
+    tile = 16
+
+    def member(j):
+        return pl.ds(outer * 2 + j, 1)
+
+    items_ref[...] = jnp.zeros_like(items_ref)
     logit_sum = None
     for j in range(2):
         mine = inner == j
@@ -153,8 +160,8 @@
         soft = grown / jnp.sum(grown, axis=-1, keepdims=True)
         hot = jnp.concatenate(
             [
-                onehot_ref[pl.ds(pl.multiple_of(((outer ^ k) * 2 + inner) * rows, rows), rows), :]
-                for k in range(n)
+                onehot_ref[pl.ds(pl.multiple_of(((outer ^ (-p % n)) * 2 + inner) * rows, rows), rows), :]
+                for p in range(n)
             ],
             axis=0,
         )
@@ -183,20 +190,21 @@
             items_ref[2 + j, g : g + 1, :] = s_grad[:, at]
             items_ref[4 + j, g : g + 1, :] = b_grad[:, at]
 
-    slope_ref[...] = dot(dmixed_ref[...], weight_ref[...], ((1,), (1,)))
+    block_ref[...] = dot(dmixed_ref[...], weight_ref[...], ((1,), (1,)))
     r_sums = [jnp.zeros((1, width), f32) for _ in range(2)]
     for spot, k in enumerate(plan.halving):
+        p = -k % n
         feat = feats[k][...].astype(f32)
         back = None
         for j in range(2):
-            lift_back = slope_ref[j * objs + k * rows : j * objs + (k + 1) * rows, :]
+            lift_back = block_ref[j * objs + p * rows : j * objs + (p + 1) * rows, :]
             r_sums[j] = r_sums[j] + jnp.sum(lift_back * feat, axis=0, keepdims=True)
             part = lift_back * vec_ref[0, member(j), :]
             back = part if back is None else back + part
         out = back_keep if spot < n // 2 else back_send
         at = slice(spot % (n // 2) * rows, (spot % (n // 2) + 1) * rows)
         out[at, 0:width] = back.astype(out.dtype)
-        out[at, width : width + classes] = logit_sum[k * rows : (k + 1) * rows, :].astype(out.dtype)
+        out[at, width : width + classes] = logit_sum[p * rows : (p + 1) * rows, :].astype(out.dtype)
     for j in range(2):
         for g in range(plan.groups):
             items_ref[j, g : g + 1, :] = r_sums[j][:, g * LANES : (g + 1) * LANES]
@@ -402,12 +410,14 @@
     n, quads, stride = plan.outer, plan.quads, plan.block_rows
     shape = jax.ShapeDtypeStruct
 
-    far_feats = [plan.over_outer(features, k) for k in range(1, n)]
+    far_feats = [plan.over_outer(features, k) for k in range(n - 1, 0, -1)][::-1]
     (own_head,) = call(
         functools.partial(head_body, plan),
         [shape((width + PAD, classes), bf16)],
         [head_weight[0], head_bias],
+        [pltpu.VMEM(head_bias.shape, f32), pltpu.SemaphoreType.DMA],
         name="head_low",
+        in_hbm=(1,),
     )
     far_head = plan.over_plane(own_head, 1)
     weight_low, biases = call(
@@ -423,6 +433,15 @@
     objs = n * rows
     total = plan.stacked + 2 * stride + PAD
     back = width + classes
+    done = ()
+    for pieces in (range(n),):
+        done = call(
+            functools.partial(forward_body, plan, pieces),
+            [shape((2 * objs, width), dtype) for dtype in (bf16, f32, bf16, f32)],
+            [([features] + far_feats)[-k] for k in pieces] + [weight_low, member_vectors, *done],
+            name="forward",
+            aliases={3 + i: i for i in range(len(done))},
+        )
     outs = call(
         functools.partial(local_body, plan),
         [
@@ -431,14 +450,10 @@
             shape((objs // 2, back), f32),
             shape((objs // 2, back), bf16),
         ],
-        [features, *far_feats, onehot, weight_low, member_vectors, own_head, far_head],
+        [features, *far_feats, onehot, weight_low, member_vectors, own_head, far_head, *done],
         [
             pltpu.VMEM((2 * objs, width), bf16),
             pltpu.VMEM((2 * objs, width), f32),
-            pltpu.VMEM((2 * objs, width), bf16),
-            pltpu.VMEM((2 * objs, width), f32),
-            pltpu.VMEM((2 * objs, width), bf16),
-            pltpu.VMEM((max(width, objs), width), f32),
             pltpu.VMEM((2, width, classes), f32),
             pltpu.VMEM((plan.items, PAD, LANES), f32),
         ],
@@ -462,7 +477,7 @@
             [back_keep, plan.over_outer(back_send, bit)],
             name="back_half",
         )
-    got[0], back_send, back_keep = lax.optimization_barrier((got[0], back_send, back_keep))
+    own, back_send, back_keep = lax.optimization_barrier((own, back_send, back_keep))
     send, block, heads = call(
         functools.partial(plane_body, plan),
         [

time: 46.6 us -> 46.1 us (0.989)
  waiting for transfers between devices: 14.5 us -> 12.9 us
  starting transfers between devices: 22.4 us -> 23.1 us
    ppermute x8, waiting for transfers between devices: 7.02 us -> 5.98 us  [over_outer(): return lax.ppermute(v, ALL, self.perm(lambda o, m: (o, m ^ k << 1)))]
    ppermute x8, starting transfers between devices: 13.4 us -> 14.2 us  [over_outer(): return lax.ppermute(v, ALL, self.perm(lambda o, m: (o, m ^ k << 1)))]
    ppermute x5, waiting for transfers between devices: 2.24 us -> 1.59 us  [over_core(): return lax.ppermute(v, ALL, self.perm(lambda o, m: (o ^ 1, m)))]
    pallas_call x9 -> x10, Pallas kernels: 6.21 us -> 6.6 us  [call(): pl.pallas_call(body, out_shape=outs, in_specs=specs, out_specs=[out_spec]...]
  transfers between devices with their start and end apart: 20 -> 20, of which waited for: 12 -> 12; matrix products, arithmetic and copies ran while one was open for 0% -> 0% of each run, Pallas kernels for 2% -> 4%
where the time goes in v4:
time: 46.1 us; the launch traced here: 45.9 us
  starting transfers between devices  23.1 us (50%)
  waiting for transfers between devices  12.9 us (28%)
  Pallas kernels  6.6 us (14%)
  local copies, waits for them, and re-layouts  2.24 us (5%)
  between operations  0.86 us (2%)
    ppermute x8, starting transfers between devices, over_outer(): return lax.ppermute(v, ALL, self.perm(lambda o, m: (o, m ^ k << 1)))  14.2 us
    ppermute x7, starting transfers between devices, over_plane(): lax.ppermute(v, ALL, self.perm(lambda o, m: (o ^ k >> 1 << 1, m ^ k & 1)))  8.83 us
    pallas_call x10, Pallas kernels, call(): pl.pallas_call(body, out_shape=outs, in_specs=specs, out_specs=[out_spec]...  6.6 us
    ppermute x8, waiting for transfers between devices, over_outer(): return lax.ppermute(v, ALL, self.perm(lambda o, m: (o, m ^ k << 1)))  5.98 us
    ppermute x7, waiting for transfers between devices, over_plane(): lax.ppermute(v, ALL, self.perm(lambda o, m: (o ^ k >> 1 << 1, m ^ k & 1)))  5.33 us
    unnamed x32, local copies, waits for them, and re-layouts  2.24 us
    ppermute x5, waiting for transfers between devices, over_core(): return lax.ppermute(v, ALL, self.perm(lambda o, m: (o ^ 1, m)))  1.59 us
  transfers between devices with their start and end apart: 20, of which 12 were waited for; matrix products, arithmetic and copies ran while one was open for 0% of the time, Pallas kernels for 4%

profile of v4, /device:TPU:0, one launch (start us, length us, event | category | flops | bytes accessed | tf_op | source)
XLA Modules:
  0.0 45.9 jit_solution(13559598688360924063)
XLA Ops:
  0.7 0.0 copy-start.12
  0.7 5.1 %collective-permute-start.2 = (bf16[64,512]{1,0:T(8,128)(2,1)}, bf16[64,512]{1,0:T(8,128)(2,1)S(1)}, u32[]{:S(2)}, u32[]{:S(2)}) collective-permute-start(bf16[64,512]{1,0:T(8,128)(2,1)} %refs_0_.3), channel_id=1, source_target_pairs={{0,6},{1,7},{2,4},{3,5},{4,2},{5,3},{6,0},{7,1},{8,14},{9,15},{10,... | collective-permute-start | bytes 196616 | tf_op jit(solution)/shard_map/ppermute | solution.py:87
  5.8 0.0 collective-permute-start.1
  5.8 0.6 %collective-permute-start = (bf16[64,512]{1,0:T(8,128)(2,1)}, bf16[64,512]{1,0:T(8,128)(2,1)S(1)}, u32[]{:S(2)}, u32[]{:S(2)}) collective-permute-start(bf16[64,512]{1,0:T(8,128)(2,1)} %refs_0_.3), channel_id=1, source_target_pairs={{0,2},{1,3},{2,0},{3,1},{4,6},{5,7},{6,4},{7,5},{8,10},{9,11},{10,... | collective-permute-start | bytes 196616 | tf_op jit(solution)/shard_map/ppermute | solution.py:87
  6.4 0.0 copy-done.12
  6.4 0.9 %copy-done.2 = f32[1,512,128]{2,1,0:T(8,128)S(1)} copy-done((f32[1,512,128]{2,1,0:T(8,128)S(1)}, f32[1,512,128]{2,1,0:T(8,128)}, u32[]{:S(2)}) %copy-start.2) | copy-done | bytes 262168
  7.4 0.0 copy-start.13
  7.4 0.0 copy-start.14
  7.4 1.7 %collective-permute-start.3 = (bf16[528,128]{1,0:T(8,128)(2,1)S(1)}, bf16[528,128]{1,0:T(8,128)(2,1)S(1)}, u32[]{:S(2)}, u32[]{:S(2)}) collective-permute-start(bf16[528,128]{1,0:T(8,128)(2,1)S(1)} %head_low.1.refs_7_), channel_id=1, source_target_pairs={{0,1},{1,0},{2,3},{3,2},{4,5},{5,4},{6,7},{7,6},{8,9},{9,8},{10,11... | collective-permute-start | bytes 405512 | tf_op jit(solution)/shard_map/ppermute | solution.py:84
  9.2 0.0 copy-done.15
  9.2 0.1 fusion.refs_4_
  9.3 0.0 copy-done.13
  9.3 0.0 copy-done.14
  9.3 0.0 copy-start
  9.3 1.2 %copy-done = f32[512,512]{1,0:T(8,128)S(1)} copy-done((f32[512,512]{1,0:T(8,128)S(1)}, f32[512,512]{1,0:T(8,128)}, u32[]{:S(2)}) %copy-start) | copy-done | bytes 1048600
  10.6 0.1 weight_low.1
  10.6 0.0 collective-permute-done.2.refs_1_.refs_3_
  10.6 1.0 %collective-permute-done.1.refs_2_ = bf16[64,512]{1,0:T(8,128)(2,1)S(1)} collective-permute-done((bf16[64,512]{1,0:T(8,128)(2,1)}, bf16[64,512]{1,0:T(8,128)(2,1)S(1)}, u32[]{:S(2)}, u32[]{:S(2)}) %collective-permute-start.1) | collective-permute-done | bytes 65568 | tf_op jit(solution)/shard_map/ppermute | solution.py:87
  11.6 0.0 collective-permute-done.refs_3_.refs_1_
  11.6 0.0 copy-done.6
  11.6 0.9 %forward.1 = (bf16[512,512]{1,0:T(8,128)(2,1)S(1)}, f32[512,512]{1,0:T(8,128)S(1)}, bf16[512,512]{1,0:T(8,128)(2,1)S(1)}, f32[512,512]{1,0:T(8,128)S(1)}) custom-call(bf16[64,512]{1,0:T(8,128)(2,1)S(1)} %copy-done.7, bf16[64,512]{1,0:T(8,128)(2,1)S(1)} %collective-permute-done.2.refs_1_.refs_3_, bf16[64,512]{1,0:T(8,128)(2,1)S(1)} %collective-permute-done.1.refs_2_, ...), custom_call_target="tpu_custom_call" | custom-call | tf_op jit(solution)/shard_map/forward/pallas_call | solution.py:46
  12.5 0.0 collective-permute-done.3.refs_8_
  12.5 0.0 copy-start.10
  12.5 0.0 copy-start.11
  12.5 1.8 %local.1 = (bf16[4,400,128]{2,1,0:T(8,128)(2,1)S(1)}, f32[4,400,128]{2,1,0:T(8,128)S(1)}, f32[128,640]{1,0:T(8,128)S(1)}, bf16[128,640]{1,0:T(8,128)(2,1)S(1)}) custom-call(bf16[64,512]{1,0:T(8,128)(2,1)S(1)} %copy-done.7, bf16[64,512]{1,0:T(8,128)(2,1)S(1)} %collective-permute-done.refs_3_.refs_1_, bf16[64,512]{1,0:T(8,128)(2,1)S(1)} %collective-permute-done.1.refs_2_, ...), custom_call_target="tpu_custom_call" | custom-call | tf_op jit(solution)/shard_map/local/pallas_call | solution.py:46
  14.4 0.1 collective-permute-start.4
  14.4 1.4 %collective-permute-start.5 = (bf16[128,640]{1,0:T(8,128)(2,1)S(1)}, bf16[128,640]{1,0:T(8,128)(2,1)S(1)}, u32[]{:S(2)}, u32[]{:S(2)}) collective-permute-start(bf16[128,640]{1,0:T(8,128)(2,1)S(1)} %get-tuple-element.72), channel_id=1, source_target_pairs={{0,2},{1,3},{2,0},{3,1},{4,6},{5,7},{6,4},{7,5},{8,10},{9,11},{10,... | collective-permute-start | bytes 491528 | tf_op jit(solution)/shard_map/ppermute | solution.py:87
  15.9 0.3 collective-permute-done.4.got_ref
  16.2 0.1 core_sum.1
  16.3 0.0 copy-start.1
  16.3 1.7 %collective-permute-start.6 = (bf16[400,128]{1,0:T(8,128)(2,1)S(1)}, bf16[400,128]{1,0:T(8,128)(2,1)S(1)}, u32[]{:S(2)}, u32[]{:S(2)}) collective-permute-start(bf16[400,128]{1,0:T(8,128)(2,1)S(1)} %get-tuple-element.76), channel_id=1, source_target_pairs={{0,1},{1,0},{2,3},{3,2},{4,5},{5,4},{6,7},{7,6},{8,9},{9,8},{10,11... | collective-permute-start | bytes 307208 | tf_op jit(solution)/shard_map/ppermute | solution.py:84
  18.0 1.5 %collective-permute-start.7 = (bf16[400,128]{1,0:T(8,128)(2,1)S(1)}, bf16[400,128]{1,0:T(8,128)(2,1)S(1)}, u32[]{:S(2)}, u32[]{:S(2)}) collective-permute-start(bf16[400,128]{1,0:T(8,128)(2,1)S(1)} %get-tuple-element.77), channel_id=1, source_target_pairs={{0,16},{1,17},{2,18},{3,19},{4,20},{5,21},{6,22},{7,23},{8,24},{9,... | collective-permute-start | bytes 307208 | tf_op jit(solution)/shard_map/ppermute | solution.py:84
  19.5 0.4 collective-permute-start.8
  19.8 1.2 %collective-permute-done.5.got_ref = bf16[128,640]{1,0:T(8,128)(2,1)S(1)} collective-permute-done((bf16[128,640]{1,0:T(8,128)(2,1)S(1)}, bf16[128,640]{1,0:T(8,128)(2,1)S(1)}, u32[]{:S(2)}, u32[]{:S(2)}) %collective-permute-start.5) | collective-permute-done | bytes 163872 | tf_op jit(solution)/shard_map/ppermute | solution.py:87
  21.1 2.6 %collective-permute-start.12 = (bf16[64,640]{1,0:T(8,128)(2,1)S(1)}, bf16[64,640]{1,0:T(8,128)(2,1)S(1)}, u32[]{:S(2)}, u32[]{:S(2)}) collective-permute-start(bf16[64,640]{1,0:T(8,128)(2,1)S(1)} %get-tuple-element.81), channel_id=1, source_target_pairs={{0,4},{1,5},{2,6},{3,7},{4,0},{5,1},{6,2},{7,3},{8,12},{9,13},{10,... | collective-permute-start | bytes 245768 | tf_op jit(solution)/shard_map/ppermute | solution.py:87
  23.7 0.0 collective-permute-done.6.refs_0_
  23.7 0.0 collective-permute-done.7.refs_1_
  23.7 1.3 %collective-permute-done.8.refs_2_ = bf16[400,128]{1,0:T(8,128)(2,1)S(1)} collective-permute-done((bf16[400,128]{1,0:T(8,128)(2,1)S(1)}, bf16[400,128]{1,0:T(8,128)(2,1)S(1)}, u32[]{:S(2)}, u32[]{:S(2)}) %collective-permute-start.8) | collective-permute-done | bytes 102432 | tf_op jit(solution)/shard_map/ppermute | solution.py:84
  25.1 0.1 plane_sum.1
  25.2 3.7 %collective-permute-start.11 = (bf16[272,128]{1,0:T(8,128)(2,1)S(1)}, bf16[272,128]{1,0:T(8,128)(2,1)S(1)}, u32[]{:S(2)}, u32[]{:S(2)}) collective-permute-start(bf16[272,128]{1,0:T(8,128)(2,1)S(1)} %get-tuple-element.79), channel_id=1, source_target_pairs={{0,6},{1,7},{2,4},{3,5},{4,2},{5,3},{6,0},{7,1},{8,14},{9,15},{10,... | collective-permute-start | bytes 208904 | tf_op jit(solution)/shard_map/ppermute | solution.py:87
  28.8 0.0 collective-permute-start.10
  28.8 0.8 %collective-permute-start.9 = (bf16[272,128]{1,0:T(8,128)(2,1)S(1)}, bf16[272,128]{1,0:T(8,128)(2,1)S(1)}, u32[]{:S(2)}, u32[]{:S(2)}) collective-permute-start(bf16[272,128]{1,0:T(8,128)(2,1)S(1)} %get-tuple-element.79), channel_id=1, source_target_pairs={{0,2},{1,3},{2,0},{3,1},{4,6},{5,7},{6,4},{7,5},{8,10},{9,11},{10,... | collective-permute-start | bytes 208904 | tf_op jit(solution)/shard_map/ppermute | solution.py:87
  29.6 0.6 %collective-permute-done.12.got_ref = bf16[64,640]{1,0:T(8,128)(2,1)S(1)} collective-permute-done((bf16[64,640]{1,0:T(8,128)(2,1)S(1)}, bf16[64,640]{1,0:T(8,128)(2,1)S(1)}, u32[]{:S(2)}, u32[]{:S(2)}) %collective-permute-start.12) | collective-permute-done | bytes 81952 | tf_op jit(solution)/shard_map/ppermute | solution.py:87
  30.3 0.7 %back_sum.1 = (f32[64,512]{1,0:T(8,128)}, f32[64,128]{1,0:T(8,128)}) custom-call(f32[64,640]{1,0:T(8,128)S(1)} %get-tuple-element.80.had_ref, bf16[64,640]{1,0:T(8,128)(2,1)S(1)} %collective-permute-done.12.got_ref), custom_call_target="tpu_custom_call" | custom-call | tf_op jit(solution)/shard_map/back_sum/pallas_call | solution.py:46
  30.9 0.4 collective-permute-done.11.refs_2_
  31.3 2.8 %collective-permute-done.10.refs_1_ = bf16[272,128]{1,0:T(8,128)(2,1)S(1)} collective-permute-done((bf16[272,128]{1,0:T(8,128)(2,1)S(1)}, bf16[272,128]{1,0:T(8,128)(2,1)S(1)}, u32[]{:S(2)}, u32[]{:S(2)}) %collective-permute-start.10) | collective-permute-done | bytes 69664 | tf_op jit(solution)/shard_map/ppermute | solution.py:87
  34.1 0.0 collective-permute-done.9.refs_0_
  34.1 0.1 outer_sum.1
  34.2 2.4 %collective-permute-start.15 = (bf16[352,128]{1,0:T(8,128)(2,1)S(1)}, bf16[352,128]{1,0:T(8,128)(2,1)S(1)}, u32[]{:S(2)}, u32[]{:S(2)}) collective-permute-start(bf16[352,128]{1,0:T(8,128)(2,1)S(1)} %get-tuple-element.92), channel_id=1, source_target_pairs={{0,17},{1,16},{2,19},{3,18},{4,21},{5,20},{6,23},{7,22},{8,25},{9,... | collective-permute-start | bytes 270344 | tf_op jit(solution)/shard_map/ppermute | solution.py:84
  36.6 0.6 %collective-permute-start.13 = (bf16[352,128]{1,0:T(8,128)(2,1)S(1)}, bf16[352,128]{1,0:T(8,128)(2,1)S(1)}, u32[]{:S(2)}, u32[]{:S(2)}) collective-permute-start(bf16[352,128]{1,0:T(8,128)(2,1)S(1)} %get-tuple-element.92), channel_id=1, source_target_pairs={{0,1},{1,0},{2,3},{3,2},{4,5},{5,4},{6,7},{7,6},{8,9},{9,8},{10,11... | collective-permute-start | bytes 270344 | tf_op jit(solution)/shard_map/ppermute | solution.py:84
  37.2 0.6 %collective-permute-start.14 = (bf16[352,128]{1,0:T(8,128)(2,1)S(1)}, bf16[352,128]{1,0:T(8,128)(2,1)S(1)}, u32[]{:S(2)}, u32[]{:S(2)}) collective-permute-start(bf16[352,128]{1,0:T(8,128)(2,1)S(1)} %get-tuple-element.91.refs_0_), channel_id=1, source_target_pairs={{0,16},{1,17},{2,18},{3,19},{4,20},{5,21},{6,22},{7,23},{8,24},{9,... | collective-permute-start | bytes 270344 | tf_op jit(solution)/shard_map/ppermute | solution.py:84
  37.8 0.0 collective-permute-start.16
  37.8 2.5 %collective-permute-done.15.refs_3_ = bf16[352,128]{1,0:T(8,128)(2,1)S(1)} collective-permute-done((bf16[352,128]{1,0:T(8,128)(2,1)S(1)}, bf16[352,128]{1,0:T(8,128)(2,1)S(1)}, u32[]{:S(2)}, u32[]{:S(2)}) %collective-permute-start.15) | collective-permute-done | bytes 90144 | tf_op jit(solution)/shard_map/ppermute | solution.py:84
  40.3 0.0 collective-permute-start.19
  40.3 0.9 %collective-permute-done.13.refs_1_ = bf16[352,128]{1,0:T(8,128)(2,1)S(1)} collective-permute-done((bf16[352,128]{1,0:T(8,128)(2,1)S(1)}, bf16[352,128]{1,0:T(8,128)(2,1)S(1)}, u32[]{:S(2)}, u32[]{:S(2)}) %collective-permute-start.13) | collective-permute-done | bytes 90144 | tf_op jit(solution)/shard_map/ppermute | solution.py:84
  41.2 0.0 collective-permute-start.17
  41.2 0.5 %collective-permute-done.14.refs_2_ = bf16[352,128]{1,0:T(8,128)(2,1)S(1)} collective-permute-done((bf16[352,128]{1,0:T(8,128)(2,1)S(1)}, bf16[352,128]{1,0:T(8,128)(2,1)S(1)}, u32[]{:S(2)}, u32[]{:S(2)}) %collective-permute-start.14) | collective-permute-done | bytes 90144 | tf_op jit(solution)/shard_map/ppermute | solution.py:84
  41.8 0.0 collective-permute-start.18
  41.8 0.0 collective-permute-done.16.refs_4_
  41.8 0.0 collective-permute-done.19.refs_7_
  41.8 0.8 %collective-permute-done.17.refs_5_ = bf16[352,128]{1,0:T(8,128)(2,1)S(1)} collective-permute-done((bf16[352,128]{1,0:T(8,128)(2,1)S(1)}, bf16[352,128]{1,0:T(8,128)(2,1)S(1)}, u32[]{:S(2)}, u32[]{:S(2)}) %collective-permute-start.17) | collective-permute-done | bytes 90144 | tf_op jit(solution)/shard_map/ppermute | solution.py:81
  42.5 0.5 %collective-permute-done.18.refs_6_ = bf16[352,128]{1,0:T(8,128)(2,1)S(1)} collective-permute-done((bf16[352,128]{1,0:T(8,128)(2,1)S(1)}, bf16[352,128]{1,0:T(8,128)(2,1)S(1)}, u32[]{:S(2)}, u32[]{:S(2)}) %collective-permute-start.18) | collective-permute-done | bytes 90144 | tf_op jit(solution)/shard_map/ppermute | solution.py:81
  43.1 0.0 copy-done.10
  43.1 2.8 %update.1 = (f32[1,128]{1,0:T(1,128)}, f32[512,512]{1,0:T(8,128)}, f32[512,512]{1,0:T(8,128)}, f32[512,512]{1,0:T(8,128)}, bf16[512,512]{1,0:T(8,128)(2,1)}, /*i...) custom-call(bf16[352,128]{1,0:T(8,128)(2,1)S(1)} %get-tuple-element., ...), custom_call_target="tpu_custom_call" | custom-call | tf_op jit(solution)/shard_map/update/pallas_call | solution.py:46
  (19 shorter events, 0.1 us)
Async XLA Ops:
  0.7 5.8 %copy-start.12 = (f32[1,128]{1,0:T(1,128)S(1)}, f32[1,128]{1,0:T(1,128)}, u32[]{:S(2)}) copy-start(f32[1,128]{1,0:T(1,128)} %bias_ref.3) | copy-start | bytes 1540
  0.7 10.0 %collective-permute-start.2 = (bf16[64,512]{1,0:T(8,128)(2,1)}, bf16[64,512]{1,0:T(8,128)(2,1)S(1)}, u32[]{:S(2)}, u32[]{:S(2)}) collective-permute-start(bf16[64,512]{1,0:T(8,128)(2,1)} %refs_0_.3), channel_id=1, source_target_pairs={{0,6},{1,7},{2,4},{3,5},{4,2},{5,3},{6,0},{7,1},{8,14},{9,15},{10,... | collective-permute-start | bytes 196616 | tf_op jit(solution)/shard_map/ppermute | solution.py:87
  5.8 5.8 %collective-permute-start.1 = (bf16[64,512]{1,0:T(8,128)(2,1)}, bf16[64,512]{1,0:T(8,128)(2,1)S(1)}, u32[]{:S(2)}, u32[]{:S(2)}) collective-permute-start(bf16[64,512]{1,0:T(8,128)(2,1)} %refs_0_.3), channel_id=1, source_target_pairs={{0,4},{1,5},{2,6},{3,7},{4,0},{5,1},{6,2},{7,3},{8,12},{9,13},{10,... | collective-permute-start | bytes 196616 | tf_op jit(solution)/shard_map/ppermute | solution.py:87
  5.8 5.8 %collective-permute-start = (bf16[64,512]{1,0:T(8,128)(2,1)}, bf16[64,512]{1,0:T(8,128)(2,1)S(1)}, u32[]{:S(2)}, u32[]{:S(2)}) collective-permute-start(bf16[64,512]{1,0:T(8,128)(2,1)} %refs_0_.3), channel_id=1, source_target_pairs={{0,2},{1,3},{2,0},{3,1},{4,6},{5,7},{6,4},{7,5},{8,10},{9,11},{10,... | collective-permute-start | bytes 196616 | tf_op jit(solution)/shard_map/ppermute | solution.py:87
  6.4 1.0 %copy-start.2 = (f32[1,512,128]{2,1,0:T(8,128)S(1)}, f32[1,512,128]{2,1,0:T(8,128)}, u32[]{:S(2)}) copy-start(f32[1,512,128]{2,1,0:T(8,128)} %param.22) | copy-start | bytes 786436
  7.4 1.8 %copy-start.15 = (s32[512]{0:T(512)S(1)}, s32[512]{0:T(512)}, u32[]{:S(2)}) copy-start(s32[512]{0:T(512)} %param.15) | copy-start | bytes 6148
  7.4 1.9 %copy-start.13 = (f32[1,128]{1,0:T(1,128)S(1)}, f32[1,128]{1,0:T(1,128)}, u32[]{:S(2)}) copy-start(f32[1,128]{1,0:T(1,128)} %first_ref.1) | copy-start | bytes 1540
  7.4 1.9 %copy-start.14 = (f32[1,128]{1,0:T(1,128)S(1)}, f32[1,128]{1,0:T(1,128)}, u32[]{:S(2)}) copy-start(f32[1,128]{1,0:T(1,128)} %second_ref.1) | copy-start | bytes 1540
  7.4 5.1 %collective-permute-start.3 = (bf16[528,128]{1,0:T(8,128)(2,1)S(1)}, bf16[528,128]{1,0:T(8,128)(2,1)S(1)}, u32[]{:S(2)}, u32[]{:S(2)}) collective-permute-start(bf16[528,128]{1,0:T(8,128)(2,1)S(1)} %head_low.1.refs_7_), channel_id=1, source_target_pairs={{0,1},{1,0},{2,3},{3,2},{4,5},{5,4},{6,7},{7,6},{8,9},{9,8},{10,11... | collective-permute-start | bytes 405512 | tf_op jit(solution)/shard_map/ppermute | solution.py:84
  9.3 1.2 %copy-start = (f32[512,512]{1,0:T(8,128)S(1)}, f32[512,512]{1,0:T(8,128)}, u32[]{:S(2)}) copy-start(f32[512,512]{1,0:T(8,128)} %refs_8_.1) | copy-start | bytes 3145732
  10.6 1.0 %copy-start.6 = (f32[3,8,512]{2,1,0:T(8,128)S(1)}, f32[3,8,512]{2,1,0:T(8,128)}, u32[]{:S(2)}) copy-start(f32[3,8,512]{2,1,0:T(8,128)} %refs_11_.1) | copy-start | bytes 147460
  10.6 1.0 %copy-start.7 = (bf16[64,512]{1,0:T(8,128)(2,1)S(1)}, bf16[64,512]{1,0:T(8,128)(2,1)}, u32[]{:S(2)}) copy-start(bf16[64,512]{1,0:T(8,128)(2,1)} %refs_0_.3) | copy-start | bytes 196612
  12.5 30.5 %copy-start.5 = (f32[512,512]{1,0:T(8,128)S(1)}, f32[512,512]{1,0:T(8,128)}, u32[]{:S(2)}) copy-start(f32[512,512]{1,0:T(8,128)} %refs_10_.1) | copy-start | bytes 3145732
  12.5 30.5 %copy-start.10 = (f32[3,8,512]{2,1,0:T(8,128)S(1)}, f32[3,8,512]{2,1,0:T(8,128)}, u32[]{:S(2)}) copy-start(f32[3,8,512]{2,1,0:T(8,128)} %refs_12_.1) | copy-start | bytes 147460
  12.5 30.5 %copy-start.11 = (f32[3,8,512]{2,1,0:T(8,128)S(1)}, f32[3,8,512]{2,1,0:T(8,128)}, u32[]{:S(2)}) copy-start(f32[3,8,512]{2,1,0:T(8,128)} %refs_13_.1) | copy-start | bytes 147460
  14.4 1.8 %collective-permute-start.4 = (bf16[4,400,128]{2,1,0:T(8,128)(2,1)S(1)}, bf16[4,400,128]{2,1,0:T(8,128)(2,1)S(1)}, u32[]{:S(2)}, u32[]{:S(2)}) collective-permute-start(bf16[4,400,128]{2,1,0:T(8,128)(2,1)S(1)} %get-tuple-element.69), channel_id=1, source_target_pairs={{0,8},{1,9},{2,10},{3,11},{4,12},{5,13},{6,14},{7,15},{8,0},{9,1},... | collective-permute-start | bytes 1228808 | tf_op jit(solution)/shard_map/ppermute | solution.py:81
  14.4 6.6 %collective-permute-start.5 = (bf16[128,640]{1,0:T(8,128)(2,1)S(1)}, bf16[128,640]{1,0:T(8,128)(2,1)S(1)}, u32[]{:S(2)}, u32[]{:S(2)}) collective-permute-start(bf16[128,640]{1,0:T(8,128)(2,1)S(1)} %get-tuple-element.72), channel_id=1, source_target_pairs={{0,2},{1,3},{2,0},{3,1},{4,6},{5,7},{6,4},{7,5},{8,10},{9,11},{10,... | collective-permute-start | bytes 491528 | tf_op jit(solution)/shard_map/ppermute | solution.py:87
  16.2 26.9 %copy-start.4 = (f32[512,512]{1,0:T(8,128)S(1)}, f32[512,512]{1,0:T(8,128)}, u32[]{:S(2)}) copy-start(f32[512,512]{1,0:T(8,128)} %refs_9_.1) | copy-start | bytes 3145732
  16.2 26.9 %copy-start.9 = (f32[1,512,128]{2,1,0:T(8,128)S(1)}, f32[1,512,128]{2,1,0:T(8,128)}, u32[]{:S(2)}) copy-start(f32[1,512,128]{2,1,0:T(8,128)} %param.24) | copy-start | bytes 786436
  16.3 26.8 %copy-start.1 = (f32[512,512]{1,0:T(8,128)S(1)}, f32[512,512]{1,0:T(8,128)}, u32[]{:S(2)}) copy-start(f32[512,512]{1,0:T(8,128)} %refs_8_.1) | copy-start | bytes 3145732
  16.3 7.4 %collective-permute-start.6 = (bf16[400,128]{1,0:T(8,128)(2,1)S(1)}, bf16[400,128]{1,0:T(8,128)(2,1)S(1)}, u32[]{:S(2)}, u32[]{:S(2)}) collective-permute-start(bf16[400,128]{1,0:T(8,128)(2,1)S(1)} %get-tuple-element.76), channel_id=1, source_target_pairs={{0,1},{1,0},{2,3},{3,2},{4,5},{5,4},{6,7},{7,6},{8,9},{9,8},{10,11... | collective-permute-start | bytes 307208 | tf_op jit(solution)/shard_map/ppermute | solution.py:84
  18.0 5.7 %collective-permute-start.7 = (bf16[400,128]{1,0:T(8,128)(2,1)S(1)}, bf16[400,128]{1,0:T(8,128)(2,1)S(1)}, u32[]{:S(2)}, u32[]{:S(2)}) collective-permute-start(bf16[400,128]{1,0:T(8,128)(2,1)S(1)} %get-tuple-element.77), channel_id=1, source_target_pairs={{0,16},{1,17},{2,18},{3,19},{4,20},{5,21},{6,22},{7,23},{8,24},{9,... | collective-permute-start | bytes 307208 | tf_op jit(solution)/shard_map/ppermute | solution.py:84
  19.5 5.6 %collective-permute-start.8 = (bf16[400,128]{1,0:T(8,128)(2,1)S(1)}, bf16[400,128]{1,0:T(8,128)(2,1)S(1)}, u32[]{:S(2)}, u32[]{:S(2)}) collective-permute-start(bf16[400,128]{1,0:T(8,128)(2,1)S(1)} %get-tuple-element.78), channel_id=1, source_target_pairs={{0,17},{1,16},{2,19},{3,18},{4,21},{5,20},{6,23},{7,22},{8,25},{9,... | collective-permute-start | bytes 307208 | tf_op jit(solution)/shard_map/ppermute | solution.py:84
  21.1 9.1 %collective-permute-start.12 = (bf16[64,640]{1,0:T(8,128)(2,1)S(1)}, bf16[64,640]{1,0:T(8,128)(2,1)S(1)}, u32[]{:S(2)}, u32[]{:S(2)}) collective-permute-start(bf16[64,640]{1,0:T(8,128)(2,1)S(1)} %get-tuple-element.81), channel_id=1, source_target_pairs={{0,4},{1,5},{2,6},{3,7},{4,0},{5,1},{6,2},{7,3},{8,12},{9,13},{10,... | collective-permute-start | bytes 245768 | tf_op jit(solution)/shard_map/ppermute | solution.py:87
  25.2 6.2 %collective-permute-start.11 = (bf16[272,128]{1,0:T(8,128)(2,1)S(1)}, bf16[272,128]{1,0:T(8,128)(2,1)S(1)}, u32[]{:S(2)}, u32[]{:S(2)}) collective-permute-start(bf16[272,128]{1,0:T(8,128)(2,1)S(1)} %get-tuple-element.79), channel_id=1, source_target_pairs={{0,6},{1,7},{2,4},{3,5},{4,2},{5,3},{6,0},{7,1},{8,14},{9,15},{10,... | collective-permute-start | bytes 208904 | tf_op jit(solution)/shard_map/ppermute | solution.py:87
  28.8 5.3 %collective-permute-start.10 = (bf16[272,128]{1,0:T(8,128)(2,1)S(1)}, bf16[272,128]{1,0:T(8,128)(2,1)S(1)}, u32[]{:S(2)}, u32[]{:S(2)}) collective-permute-start(bf16[272,128]{1,0:T(8,128)(2,1)S(1)} %get-tuple-element.79), channel_id=1, source_target_pairs={{0,4},{1,5},{2,6},{3,7},{4,0},{5,1},{6,2},{7,3},{8,12},{9,13},{10,... | collective-permute-start | bytes 208904 | tf_op jit(solution)/shard_map/ppermute | solution.py:87
  28.8 5.3 %collective-permute-start.9 = (bf16[272,128]{1,0:T(8,128)(2,1)S(1)}, bf16[272,128]{1,0:T(8,128)(2,1)S(1)}, u32[]{:S(2)}, u32[]{:S(2)}) collective-permute-start(bf16[272,128]{1,0:T(8,128)(2,1)S(1)} %get-tuple-element.79), channel_id=1, source_target_pairs={{0,2},{1,3},{2,0},{3,1},{4,6},{5,7},{6,4},{7,5},{8,10},{9,11},{10,... | collective-permute-start | bytes 208904 | tf_op jit(solution)/shard_map/ppermute | solution.py:87
  30.2 12.8 %copy-start.8 = (f32[1,512,128]{2,1,0:T(8,128)S(1)}, f32[1,512,128]{2,1,0:T(8,128)}, u32[]{:S(2)}) copy-start(f32[1,512,128]{2,1,0:T(8,128)} %param.23) | copy-start | bytes 786436
  30.9 12.2 %copy-start.3 = (f32[1,512,128]{2,1,0:T(8,128)S(1)}, f32[1,512,128]{2,1,0:T(8,128)}, u32[]{:S(2)}) copy-start(f32[1,512,128]{2,1,0:T(8,128)} %param.22) | copy-start | bytes 786436
  34.2 6.1 %collective-permute-start.15 = (bf16[352,128]{1,0:T(8,128)(2,1)S(1)}, bf16[352,128]{1,0:T(8,128)(2,1)S(1)}, u32[]{:S(2)}, u32[]{:S(2)}) collective-permute-start(bf16[352,128]{1,0:T(8,128)(2,1)S(1)} %get-tuple-element.92), channel_id=1, source_target_pairs={{0,17},{1,16},{2,19},{3,18},{4,21},{5,20},{6,23},{7,22},{8,25},{9,... | collective-permute-start | bytes 270344 | tf_op jit(solution)/shard_map/ppermute | solution.py:84
  36.6 4.6 %collective-permute-start.13 = (bf16[352,128]{1,0:T(8,128)(2,1)S(1)}, bf16[352,128]{1,0:T(8,128)(2,1)S(1)}, u32[]{:S(2)}, u32[]{:S(2)}) collective-permute-start(bf16[352,128]{1,0:T(8,128)(2,1)S(1)} %get-tuple-element.92), channel_id=1, source_target_pairs={{0,1},{1,0},{2,3},{3,2},{4,5},{5,4},{6,7},{7,6},{8,9},{9,8},{10,11... | collective-permute-start | bytes 270344 | tf_op jit(solution)/shard_map/ppermute | solution.py:84
  37.2 4.5 %collective-permute-start.14 = (bf16[352,128]{1,0:T(8,128)(2,1)S(1)}, bf16[352,128]{1,0:T(8,128)(2,1)S(1)}, u32[]{:S(2)}, u32[]{:S(2)}) collective-permute-start(bf16[352,128]{1,0:T(8,128)(2,1)S(1)} %get-tuple-element.91.refs_0_), channel_id=1, source_target_pairs={{0,16},{1,17},{2,18},{3,19},{4,20},{5,21},{6,22},{7,23},{8,24},{9,... | collective-permute-start | bytes 270344 | tf_op jit(solution)/shard_map/ppermute | solution.py:84
  37.8 4.0 %collective-permute-start.16 = (bf16[352,128]{1,0:T(8,128)(2,1)S(1)}, bf16[352,128]{1,0:T(8,128)(2,1)S(1)}, u32[]{:S(2)}, u32[]{:S(2)}) collective-permute-start(bf16[352,128]{1,0:T(8,128)(2,1)S(1)} %get-tuple-element.91.refs_0_), channel_id=1, source_target_pairs={{0,8},{1,9},{2,10},{3,11},{4,12},{5,13},{6,14},{7,15},{8,0},{9,1},... | collective-permute-start | bytes 270344 | tf_op jit(solution)/shard_map/ppermute | solution.py:81
  40.3 1.4 %collective-permute-start.19 = (bf16[352,128]{1,0:T(8,128)(2,1)S(1)}, bf16[352,128]{1,0:T(8,128)(2,1)S(1)}, u32[]{:S(2)}, u32[]{:S(2)}) collective-permute-start(bf16[352,128]{1,0:T(8,128)(2,1)S(1)} %collective-permute-done.15.refs_3_), channel_id=1, source_target_pairs={{0,8},{1,9},{2,10},{3,11},{4,12},{5,13},{6,14},{7,15},{8,0},{9,1},... | collective-permute-start | bytes 270344 | tf_op jit(solution)/shard_map/ppermute | solution.py:81
  41.2 1.3 %collective-permute-start.17 = (bf16[352,128]{1,0:T(8,128)(2,1)S(1)}, bf16[352,128]{1,0:T(8,128)(2,1)S(1)}, u32[]{:S(2)}, u32[]{:S(2)}) collective-permute-start(bf16[352,128]{1,0:T(8,128)(2,1)S(1)} %collective-permute-done.13.refs_1_), channel_id=1, source_target_pairs={{0,8},{1,9},{2,10},{3,11},{4,12},{5,13},{6,14},{7,15},{8,0},{9,1},... | collective-permute-start | bytes 270344 | tf_op jit(solution)/shard_map/ppermute | solution.py:81
  41.8 1.3 %collective-permute-start.18 = (bf16[352,128]{1,0:T(8,128)(2,1)S(1)}, bf16[352,128]{1,0:T(8,128)(2,1)S(1)}, u32[]{:S(2)}, u32[]{:S(2)}) collective-permute-start(bf16[352,128]{1,0:T(8,128)(2,1)S(1)} %collective-permute-done.14.refs_2_), channel_id=1, source_target_pairs={{0,8},{1,9},{2,10},{3,11},{4,12},{5,13},{6,14},{7,15},{8,0},{9,1},... | collective-permute-start | bytes 270344 | tf_op jit(solution)/shard_map/ppermute | solution.py:81

commit v5 on v4

--- a/solution.py
+++ b/solution.py
@@ -95,10 +95,18 @@
     low_ref[plan.width :, :] = jnp.broadcast_to(held_ref[...], (PAD, plan.classes)).astype(bf16)
 
 
-def low_body(plan, weight_ref, bias_ref, first_ref, second_ref, low_ref, biases_ref):
+def low_body(plan, *refs):
+    sources, (low_ref, vectors_ref, same_ref, biases_ref, weight_ref, sems) = refs[:6], refs[6:]
+    targets = [weight_ref, vectors_ref, same_ref] + [biases_ref.at[i : i + 1] for i in range(3)]
+    copies = [
+        pltpu.make_async_copy(source, target, sems.at[i])
+        for i, (source, target) in enumerate(zip(sources, targets))
+    ]
+    for copy in copies:
+        copy.start()
+    for copy in copies:
+        copy.wait()
     low_ref[...] = weight_ref[...].astype(bf16)
-    for i, ref in enumerate((bias_ref, first_ref, second_ref)):
-        biases_ref[i : i + 1, :] = ref[...]
 
 
 def forward_body(plan, pieces, *refs):
@@ -363,7 +371,10 @@
         new = adamw(hw[at, :], grad, hm[at, :], hv[at, :], 0.02, 0.01)
         for ref, v in zip(head_refs, new + (new[0],)):
             ref[at, :] = v.astype(ref.dtype)
-        if i % 2:
+        if i < 2:
+            for source, target in zip(block_refs + head_refs, block_outs + head_outs):
+                send(source.at[at], target.at[at])
+        elif i % 2:
             both = pl.ds(pl.multiple_of(shard_of(i) // 2 * (2 * stride), 2 * stride), 2 * stride)
             for source, target in zip(block_refs + head_refs, block_outs + head_outs):
                 send(source.at[both], target.at[both])
@@ -420,11 +431,21 @@
         in_hbm=(1,),
     )
     far_head = plan.over_plane(own_head, 1)
-    weight_low, biases = call(
+    weight_low, vectors, late, biases = call(
         functools.partial(low_body, plan),
-        [shape((width, width), bf16), shape((3, classes), f32)],
-        [block_weight, head_bias, bias_first, bias_second],
+        [
+            shape((width, width), bf16),
+            shape(member_vectors.shape, f32),
+            shape((rows, width), bf16),
+            shape((3, classes), f32),
+        ],
+        [
+            pltpu.with_memory_space_constraint(v, pltpu.HBM)
+            for v in (block_weight, member_vectors, features, head_bias, bias_first, bias_second)
+        ],
+        [pltpu.VMEM((width, width), f32), pltpu.SemaphoreType.DMA((6,))],
         name="weight_low",
+        in_hbm=range(6),
     )
     onehot = (
         jnp.arange(classes, dtype=jnp.int32)[None, :] == labels[:, None]
@@ -438,7 +459,7 @@
         done = call(
             functools.partial(forward_body, plan, pieces),
             [shape((2 * objs, width), dtype) for dtype in (bf16, f32, bf16, f32)],
-            [([features] + far_feats)[-k] for k in pieces] + [weight_low, member_vectors, *done],
+            [([late] + far_feats)[-k] for k in pieces] + [weight_low, vectors, *done],
             name="forward",
             aliases={3 + i: i for i in range(len(done))},
         )
@@ -450,7 +471,7 @@
             shape((objs // 2, back), f32),
             shape((objs // 2, back), bf16),
         ],
-        [features, *far_feats, onehot, weight_low, member_vectors, own_head, far_head, *done],
+        [features, *far_feats, onehot, weight_low, vectors, own_head, far_head, *done],
         [
             pltpu.VMEM((2 * objs, width), bf16),
             pltpu.VMEM((2 * objs, width), f32),
@@ -537,7 +558,7 @@
         [pltpu.VMEM(*r) for r in results]
         + [
             pltpu.VMEM((plan.items // 2, plan.n_mem, plan.groups, LANES), f32),
-            pltpu.SemaphoreType.DMA((7 + 8 * plan.quads,)),
+            pltpu.SemaphoreType.DMA((15 + 8 * plan.quads,)),
         ],
         name="update",
         out_spec=pl.BlockSpec(memory_space=pl.ANY),

time: 46.1 us -> 46 us (level)
  Pallas kernels: 6.6 us -> 7.84 us
  local copies, waits for them, and re-layouts: 2.24 us -> 1.01 us
    pallas_call x10, Pallas kernels: 6.6 us -> 7.84 us  [call(): pl.pallas_call(body, out_shape=outs, in_specs=specs, out_specs=[out_spec]...]
    unnamed x32 -> x26, local copies, waits for them, and re-layouts: 2.24 us -> 1.01 us
  transfers between devices with their start and end apart: 20 -> 20, of which waited for: 12 -> 12; matrix products, arithmetic and copies ran while one was open for 0% -> 0% of each run, Pallas kernels for 4% -> 7%
where the time goes in v5:
time: 46 us; the launch traced here: 45.8 us
  starting transfers between devices  23.1 us (50%)
  waiting for transfers between devices  12.9 us (28%)
  Pallas kernels  7.84 us (17%)
  local copies, waits for them, and re-layouts  1.01 us (2%)
  between operations  0.86 us (2%)
    ppermute x8, starting transfers between devices, over_outer(): return lax.ppermute(v, ALL, self.perm(lambda o, m: (o, m ^ k << 1)))  14.2 us
    ppermute x7, starting transfers between devices, over_plane(): lax.ppermute(v, ALL, self.perm(lambda o, m: (o ^ k >> 1 << 1, m ^ k & 1)))  8.83 us
    pallas_call x10, Pallas kernels, call(): pl.pallas_call(body, out_shape=outs, in_specs=specs, out_specs=[out_spec]...  7.84 us
    ppermute x8, waiting for transfers between devices, over_outer(): return lax.ppermute(v, ALL, self.perm(lambda o, m: (o, m ^ k << 1)))  5.96 us
    ppermute x7, waiting for transfers between devices, over_plane(): lax.ppermute(v, ALL, self.perm(lambda o, m: (o ^ k >> 1 << 1, m ^ k & 1)))  5.31 us
    ppermute x5, waiting for transfers between devices, over_core(): return lax.ppermute(v, ALL, self.perm(lambda o, m: (o ^ 1, m)))  1.62 us
    unnamed x26, local copies, waits for them, and re-layouts  1.01 us
  transfers between devices with their start and end apart: 20, of which 12 were waited for; matrix products, arithmetic and copies ran while one was open for 0% of the time, Pallas kernels for 7%

profile of v5, /device:TPU:0, one launch (start us, length us, event | category | flops | bytes accessed | tf_op | source)
XLA Modules:
  0.0 45.8 jit_solution(5523041826553473453)
XLA Ops:
  0.7 0.0 copy-start.11
  0.7 5.1 %collective-permute-start.2 = (bf16[64,512]{1,0:T(8,128)(2,1)}, bf16[64,512]{1,0:T(8,128)(2,1)S(1)}, u32[]{:S(2)}, u32[]{:S(2)}) collective-permute-start(bf16[64,512]{1,0:T(8,128)(2,1)} %refs_0_.3), channel_id=1, source_target_pairs={{0,6},{1,7},{2,4},{3,5},{4,2},{5,3},{6,0},{7,1},{8,14},{9,15},{10,... | collective-permute-start | bytes 196616 | tf_op jit(solution)/shard_map/ppermute | solution.py:87
  5.8 0.0 collective-permute-start.1
  5.8 0.6 %collective-permute-start = (bf16[64,512]{1,0:T(8,128)(2,1)}, bf16[64,512]{1,0:T(8,128)(2,1)S(1)}, u32[]{:S(2)}, u32[]{:S(2)}) collective-permute-start(bf16[64,512]{1,0:T(8,128)(2,1)} %refs_0_.3), channel_id=1, source_target_pairs={{0,2},{1,3},{2,0},{3,1},{4,6},{5,7},{6,4},{7,5},{8,10},{9,11},{10,... | collective-permute-start | bytes 196616 | tf_op jit(solution)/shard_map/ppermute | solution.py:87
  6.4 0.0 copy-done.11
  6.4 0.9 %copy-done.1 = f32[1,512,128]{2,1,0:T(8,128)S(1)} copy-done((f32[1,512,128]{2,1,0:T(8,128)S(1)}, f32[1,512,128]{2,1,0:T(8,128)}, u32[]{:S(2)}) %copy-start.1) | copy-done | bytes 262168
  7.4 1.7 %collective-permute-start.3 = (bf16[528,128]{1,0:T(8,128)(2,1)S(1)}, bf16[528,128]{1,0:T(8,128)(2,1)S(1)}, u32[]{:S(2)}, u32[]{:S(2)}) collective-permute-start(bf16[528,128]{1,0:T(8,128)(2,1)S(1)} %head_low.1.refs_7_), channel_id=1, source_target_pairs={{0,1},{1,0},{2,3},{3,2},{4,5},{5,4},{6,7},{7,6},{8,9},{9,8},{10,11... | collective-permute-start | bytes 405512 | tf_op jit(solution)/shard_map/ppermute | solution.py:84
  9.1 0.0 copy-done.12
  9.1 0.1 fusion.refs_4_
  9.3 1.3 %weight_low.1 = (bf16[512,512]{1,0:T(8,128)(2,1)S(1)}, f32[3,8,512]{2,1,0:T(8,128)S(1)}, bf16[64,512]{1,0:T(8,128)(2,1)S(1)}, f32[3,128]{1,0:T(4,128)S(1)}) custom-call(f32[512,512]{1,0:T(8,128)} %refs_8_.1, f32[3,8,512]{2,1,0:T(8,128)} %refs_11_.1, bf16[64,512]{1,0:T(8,128)(2,1)} %refs_0_.3, f32[1,128]{1,0:T(1,128)} %bias_ref.1, f32[1,128]{1,0:T(1,128)} %refs_4_.1, ...), custom_call_target="tpu_custom_call" | custom-call | tf_op jit(solution)/shard_map/weight_low/pallas_call | solution.py:46
  10.6 0.0 collective-permute-done.2.refs_1_.refs_3_
  10.6 0.9 %collective-permute-done.1.refs_2_ = bf16[64,512]{1,0:T(8,128)(2,1)S(1)} collective-permute-done((bf16[64,512]{1,0:T(8,128)(2,1)}, bf16[64,512]{1,0:T(8,128)(2,1)S(1)}, u32[]{:S(2)}, u32[]{:S(2)}) %collective-permute-start.1) | collective-permute-done | bytes 65568 | tf_op jit(solution)/shard_map/ppermute | solution.py:87
  11.6 0.0 collective-permute-done.refs_3_.refs_1_
  11.6 0.9 %forward.1 = (bf16[512,512]{1,0:T(8,128)(2,1)S(1)}, f32[512,512]{1,0:T(8,128)S(1)}, bf16[512,512]{1,0:T(8,128)(2,1)S(1)}, f32[512,512]{1,0:T(8,128)S(1)}) custom-call(bf16[64,512]{1,0:T(8,128)(2,1)S(1)} %get-tuple-element.67.refs_0_, bf16[64,512]{1,0:T(8,128)(2,1)S(1)} %collective-permute-done.2.refs_1_.refs_3_, ...), custom_call_target="tpu_custom_call" | custom-call | tf_op jit(solution)/shard_map/forward/pallas_call | solution.py:46
  12.5 0.0 collective-permute-done.3.refs_8_
  12.5 0.0 copy-done.5
  12.5 0.0 copy-start.4
  12.5 0.0 copy-start.8
  12.5 0.0 copy-start.9
  12.6 0.0 copy-start.10
  12.6 1.8 %local.1 = (bf16[4,400,128]{2,1,0:T(8,128)(2,1)S(1)}, f32[4,400,128]{2,1,0:T(8,128)S(1)}, f32[128,640]{1,0:T(8,128)S(1)}, bf16[128,640]{1,0:T(8,128)(2,1)S(1)}) custom-call(bf16[64,512]{1,0:T(8,128)(2,1)S(1)} %copy-done.5, bf16[64,512]{1,0:T(8,128)(2,1)S(1)} %collective-permute-done.refs_3_.refs_1_, bf16[64,512]{1,0:T(8,128)(2,1)S(1)} %collective-permute-done.1.refs_2_, ...), custom_call_target="tpu_custom_call" | custom-call | tf_op jit(solution)/shard_map/local/pallas_call | solution.py:46
  14.4 0.1 collective-permute-start.4
  14.4 1.4 %collective-permute-start.5 = (bf16[128,640]{1,0:T(8,128)(2,1)S(1)}, bf16[128,640]{1,0:T(8,128)(2,1)S(1)}, u32[]{:S(2)}, u32[]{:S(2)}) collective-permute-start(bf16[128,640]{1,0:T(8,128)(2,1)S(1)} %get-tuple-element.76), channel_id=1, source_target_pairs={{0,2},{1,3},{2,0},{3,1},{4,6},{5,7},{6,4},{7,5},{8,10},{9,11},{10,... | collective-permute-start | bytes 491528 | tf_op jit(solution)/shard_map/ppermute | solution.py:87
  15.8 0.3 collective-permute-done.4.got_ref
  16.2 0.1 core_sum.1
  16.3 0.0 copy-start
  16.3 1.7 %collective-permute-start.6 = (bf16[400,128]{1,0:T(8,128)(2,1)S(1)}, bf16[400,128]{1,0:T(8,128)(2,1)S(1)}, u32[]{:S(2)}, u32[]{:S(2)}) collective-permute-start(bf16[400,128]{1,0:T(8,128)(2,1)S(1)} %get-tuple-element.80), channel_id=1, source_target_pairs={{0,1},{1,0},{2,3},{3,2},{4,5},{5,4},{6,7},{7,6},{8,9},{9,8},{10,11... | collective-permute-start | bytes 307208 | tf_op jit(solution)/shard_map/ppermute | solution.py:84
  18.0 1.5 %collective-permute-start.7 = (bf16[400,128]{1,0:T(8,128)(2,1)S(1)}, bf16[400,128]{1,0:T(8,128)(2,1)S(1)}, u32[]{:S(2)}, u32[]{:S(2)}) collective-permute-start(bf16[400,128]{1,0:T(8,128)(2,1)S(1)} %get-tuple-element.81), channel_id=1, source_target_pairs={{0,16},{1,17},{2,18},{3,19},{4,20},{5,21},{6,22},{7,23},{8,24},{9,... | collective-permute-start | bytes 307208 | tf_op jit(solution)/shard_map/ppermute | solution.py:84
  19.5 0.4 collective-permute-start.8
  19.9 1.2 %collective-permute-done.5.got_ref = bf16[128,640]{1,0:T(8,128)(2,1)S(1)} collective-permute-done((bf16[128,640]{1,0:T(8,128)(2,1)S(1)}, bf16[128,640]{1,0:T(8,128)(2,1)S(1)}, u32[]{:S(2)}, u32[]{:S(2)}) %collective-permute-start.5) | collective-permute-done | bytes 163872 | tf_op jit(solution)/shard_map/ppermute | solution.py:87
  21.1 2.6 %collective-permute-start.12 = (bf16[64,640]{1,0:T(8,128)(2,1)S(1)}, bf16[64,640]{1,0:T(8,128)(2,1)S(1)}, u32[]{:S(2)}, u32[]{:S(2)}) collective-permute-start(bf16[64,640]{1,0:T(8,128)(2,1)S(1)} %get-tuple-element.85), channel_id=1, source_target_pairs={{0,4},{1,5},{2,6},{3,7},{4,0},{5,1},{6,2},{7,3},{8,12},{9,13},{10,... | collective-permute-start | bytes 245768 | tf_op jit(solution)/shard_map/ppermute | solution.py:87
  23.7 0.0 collective-permute-done.6.refs_0_
  23.7 0.0 collective-permute-done.7.refs_1_
  23.7 1.3 %collective-permute-done.8.refs_2_ = bf16[400,128]{1,0:T(8,128)(2,1)S(1)} collective-permute-done((bf16[400,128]{1,0:T(8,128)(2,1)S(1)}, bf16[400,128]{1,0:T(8,128)(2,1)S(1)}, u32[]{:S(2)}, u32[]{:S(2)}) %collective-permute-start.8) | collective-permute-done | bytes 102432 | tf_op jit(solution)/shard_map/ppermute | solution.py:84
  25.0 0.1 plane_sum.1
  25.1 3.7 %collective-permute-start.11 = (bf16[272,128]{1,0:T(8,128)(2,1)S(1)}, bf16[272,128]{1,0:T(8,128)(2,1)S(1)}, u32[]{:S(2)}, u32[]{:S(2)}) collective-permute-start(bf16[272,128]{1,0:T(8,128)(2,1)S(1)} %get-tuple-element.83), channel_id=1, source_target_pairs={{0,6},{1,7},{2,4},{3,5},{4,2},{5,3},{6,0},{7,1},{8,14},{9,15},{10,... | collective-permute-start | bytes 208904 | tf_op jit(solution)/shard_map/ppermute | solution.py:87
  28.8 0.0 collective-permute-start.10
  28.8 0.8 %collective-permute-start.9 = (bf16[272,128]{1,0:T(8,128)(2,1)S(1)}, bf16[272,128]{1,0:T(8,128)(2,1)S(1)}, u32[]{:S(2)}, u32[]{:S(2)}) collective-permute-start(bf16[272,128]{1,0:T(8,128)(2,1)S(1)} %get-tuple-element.83), channel_id=1, source_target_pairs={{0,2},{1,3},{2,0},{3,1},{4,6},{5,7},{6,4},{7,5},{8,10},{9,11},{10,... | collective-permute-start | bytes 208904 | tf_op jit(solution)/shard_map/ppermute | solution.py:87
  29.6 0.6 %collective-permute-done.12.got_ref = bf16[64,640]{1,0:T(8,128)(2,1)S(1)} collective-permute-done((bf16[64,640]{1,0:T(8,128)(2,1)S(1)}, bf16[64,640]{1,0:T(8,128)(2,1)S(1)}, u32[]{:S(2)}, u32[]{:S(2)}) %collective-permute-start.12) | collective-permute-done | bytes 81952 | tf_op jit(solution)/shard_map/ppermute | solution.py:87
  30.2 0.7 %back_sum.1 = (f32[64,512]{1,0:T(8,128)}, f32[64,128]{1,0:T(8,128)}) custom-call(f32[64,640]{1,0:T(8,128)S(1)} %get-tuple-element.84.had_ref, bf16[64,640]{1,0:T(8,128)(2,1)S(1)} %collective-permute-done.12.got_ref), custom_call_target="tpu_custom_call" | custom-call | tf_op jit(solution)/shard_map/back_sum/pallas_call | solution.py:46
  30.9 0.4 collective-permute-done.11.refs_2_
  31.3 2.8 %collective-permute-done.10.refs_1_ = bf16[272,128]{1,0:T(8,128)(2,1)S(1)} collective-permute-done((bf16[272,128]{1,0:T(8,128)(2,1)S(1)}, bf16[272,128]{1,0:T(8,128)(2,1)S(1)}, u32[]{:S(2)}, u32[]{:S(2)}) %collective-permute-start.10) | collective-permute-done | bytes 69664 | tf_op jit(solution)/shard_map/ppermute | solution.py:87
  34.1 0.0 collective-permute-done.9.refs_0_
  34.1 0.1 outer_sum.1
  34.2 2.4 %collective-permute-start.15 = (bf16[352,128]{1,0:T(8,128)(2,1)S(1)}, bf16[352,128]{1,0:T(8,128)(2,1)S(1)}, u32[]{:S(2)}, u32[]{:S(2)}) collective-permute-start(bf16[352,128]{1,0:T(8,128)(2,1)S(1)} %get-tuple-element.96), channel_id=1, source_target_pairs={{0,17},{1,16},{2,19},{3,18},{4,21},{5,20},{6,23},{7,22},{8,25},{9,... | collective-permute-start | bytes 270344 | tf_op jit(solution)/shard_map/ppermute | solution.py:84
  36.6 0.6 %collective-permute-start.13 = (bf16[352,128]{1,0:T(8,128)(2,1)S(1)}, bf16[352,128]{1,0:T(8,128)(2,1)S(1)}, u32[]{:S(2)}, u32[]{:S(2)}) collective-permute-start(bf16[352,128]{1,0:T(8,128)(2,1)S(1)} %get-tuple-element.96), channel_id=1, source_target_pairs={{0,1},{1,0},{2,3},{3,2},{4,5},{5,4},{6,7},{7,6},{8,9},{9,8},{10,11... | collective-permute-start | bytes 270344 | tf_op jit(solution)/shard_map/ppermute | solution.py:84
  37.2 0.6 %collective-permute-start.14 = (bf16[352,128]{1,0:T(8,128)(2,1)S(1)}, bf16[352,128]{1,0:T(8,128)(2,1)S(1)}, u32[]{:S(2)}, u32[]{:S(2)}) collective-permute-start(bf16[352,128]{1,0:T(8,128)(2,1)S(1)} %get-tuple-element.95.refs_0_), channel_id=1, source_target_pairs={{0,16},{1,17},{2,18},{3,19},{4,20},{5,21},{6,22},{7,23},{8,24},{9,... | collective-permute-start | bytes 270344 | tf_op jit(solution)/shard_map/ppermute | solution.py:84
  37.8 0.0 collective-permute-start.16
  37.8 2.5 %collective-permute-done.15.refs_3_ = bf16[352,128]{1,0:T(8,128)(2,1)S(1)} collective-permute-done((bf16[352,128]{1,0:T(8,128)(2,1)S(1)}, bf16[352,128]{1,0:T(8,128)(2,1)S(1)}, u32[]{:S(2)}, u32[]{:S(2)}) %collective-permute-start.15) | collective-permute-done | bytes 90144 | tf_op jit(solution)/shard_map/ppermute | solution.py:84
  40.3 0.0 collective-permute-start.19
  40.3 0.9 %collective-permute-done.13.refs_1_ = bf16[352,128]{1,0:T(8,128)(2,1)S(1)} collective-permute-done((bf16[352,128]{1,0:T(8,128)(2,1)S(1)}, bf16[352,128]{1,0:T(8,128)(2,1)S(1)}, u32[]{:S(2)}, u32[]{:S(2)}) %collective-permute-start.13) | collective-permute-done | bytes 90144 | tf_op jit(solution)/shard_map/ppermute | solution.py:84
  41.2 0.0 collective-permute-start.17
  41.2 0.5 %collective-permute-done.14.refs_2_ = bf16[352,128]{1,0:T(8,128)(2,1)S(1)} collective-permute-done((bf16[352,128]{1,0:T(8,128)(2,1)S(1)}, bf16[352,128]{1,0:T(8,128)(2,1)S(1)}, u32[]{:S(2)}, u32[]{:S(2)}) %collective-permute-start.14) | collective-permute-done | bytes 90144 | tf_op jit(solution)/shard_map/ppermute | solution.py:84
  41.7 0.0 collective-permute-start.18
  41.7 0.0 collective-permute-done.16.refs_4_
  41.7 0.0 collective-permute-done.19.refs_7_
  41.8 0.7 %collective-permute-done.17.refs_5_ = bf16[352,128]{1,0:T(8,128)(2,1)S(1)} collective-permute-done((bf16[352,128]{1,0:T(8,128)(2,1)S(1)}, bf16[352,128]{1,0:T(8,128)(2,1)S(1)}, u32[]{:S(2)}, u32[]{:S(2)}) %collective-permute-start.17) | collective-permute-done | bytes 90144 | tf_op jit(solution)/shard_map/ppermute | solution.py:81
  42.5 0.5 %collective-permute-done.18.refs_6_ = bf16[352,128]{1,0:T(8,128)(2,1)S(1)} collective-permute-done((bf16[352,128]{1,0:T(8,128)(2,1)S(1)}, bf16[352,128]{1,0:T(8,128)(2,1)S(1)}, u32[]{:S(2)}, u32[]{:S(2)}) %collective-permute-start.18) | collective-permute-done | bytes 90144 | tf_op jit(solution)/shard_map/ppermute | solution.py:81
  43.0 0.0 copy-done.4
  43.0 0.0 copy-done.8
  43.0 0.0 copy-done.9
  43.0 0.0 copy-done.10
  43.1 0.0 copy-done.3
  43.1 2.7 %update.1 = (f32[1,128]{1,0:T(1,128)}, f32[512,512]{1,0:T(8,128)}, f32[512,512]{1,0:T(8,128)}, f32[512,512]{1,0:T(8,128)}, bf16[512,512]{1,0:T(8,128)(2,1)}, /*i...) custom-call(bf16[352,128]{1,0:T(8,128)(2,1)S(1)} %get-tuple-element., ...), custom_call_target="tpu_custom_call" | custom-call | tf_op jit(solution)/shard_map/update/pallas_call | solution.py:46
  (13 shorter events, 0.1 us)
Async XLA Ops:
  0.7 5.8 %copy-start.11 = (f32[1,128]{1,0:T(1,128)S(1)}, f32[1,128]{1,0:T(1,128)}, u32[]{:S(2)}) copy-start(f32[1,128]{1,0:T(1,128)} %bias_ref.1) | copy-start | bytes 1540
  0.7 10.0 %collective-permute-start.2 = (bf16[64,512]{1,0:T(8,128)(2,1)}, bf16[64,512]{1,0:T(8,128)(2,1)S(1)}, u32[]{:S(2)}, u32[]{:S(2)}) collective-permute-start(bf16[64,512]{1,0:T(8,128)(2,1)} %refs_0_.3), channel_id=1, source_target_pairs={{0,6},{1,7},{2,4},{3,5},{4,2},{5,3},{6,0},{7,1},{8,14},{9,15},{10,... | collective-permute-start | bytes 196616 | tf_op jit(solution)/shard_map/ppermute | solution.py:87
  5.8 5.8 %collective-permute-start.1 = (bf16[64,512]{1,0:T(8,128)(2,1)}, bf16[64,512]{1,0:T(8,128)(2,1)S(1)}, u32[]{:S(2)}, u32[]{:S(2)}) collective-permute-start(bf16[64,512]{1,0:T(8,128)(2,1)} %refs_0_.3), channel_id=1, source_target_pairs={{0,4},{1,5},{2,6},{3,7},{4,0},{5,1},{6,2},{7,3},{8,12},{9,13},{10,... | collective-permute-start | bytes 196616 | tf_op jit(solution)/shard_map/ppermute | solution.py:87
  5.8 5.8 %collective-permute-start = (bf16[64,512]{1,0:T(8,128)(2,1)}, bf16[64,512]{1,0:T(8,128)(2,1)S(1)}, u32[]{:S(2)}, u32[]{:S(2)}) collective-permute-start(bf16[64,512]{1,0:T(8,128)(2,1)} %refs_0_.3), channel_id=1, source_target_pairs={{0,2},{1,3},{2,0},{3,1},{4,6},{5,7},{6,4},{7,5},{8,10},{9,11},{10,... | collective-permute-start | bytes 196616 | tf_op jit(solution)/shard_map/ppermute | solution.py:87
  6.4 1.0 %copy-start.1 = (f32[1,512,128]{2,1,0:T(8,128)S(1)}, f32[1,512,128]{2,1,0:T(8,128)}, u32[]{:S(2)}) copy-start(f32[1,512,128]{2,1,0:T(8,128)} %param.22) | copy-start | bytes 786436
  7.4 1.8 %copy-start.12 = (s32[512]{0:T(512)S(1)}, s32[512]{0:T(512)}, u32[]{:S(2)}) copy-start(s32[512]{0:T(512)} %param.15) | copy-start | bytes 6148
  7.4 5.1 %collective-permute-start.3 = (bf16[528,128]{1,0:T(8,128)(2,1)S(1)}, bf16[528,128]{1,0:T(8,128)(2,1)S(1)}, u32[]{:S(2)}, u32[]{:S(2)}) collective-permute-start(bf16[528,128]{1,0:T(8,128)(2,1)S(1)} %head_low.1.refs_7_), channel_id=1, source_target_pairs={{0,1},{1,0},{2,3},{3,2},{4,5},{5,4},{6,7},{7,6},{8,9},{9,8},{10,11... | collective-permute-start | bytes 405512 | tf_op jit(solution)/shard_map/ppermute | solution.py:84
  11.6 0.9 %copy-start.5 = (bf16[64,512]{1,0:T(8,128)(2,1)S(1)}, bf16[64,512]{1,0:T(8,128)(2,1)}, u32[]{:S(2)}) copy-start(bf16[64,512]{1,0:T(8,128)(2,1)} %refs_0_.3) | copy-start | bytes 196612
  12.5 30.5 %copy-start.4 = (f32[512,512]{1,0:T(8,128)S(1)}, f32[512,512]{1,0:T(8,128)}, u32[]{:S(2)}) copy-start(f32[512,512]{1,0:T(8,128)} %refs_10_.1) | copy-start | bytes 3145732
  12.5 30.5 %copy-start.8 = (f32[3,8,512]{2,1,0:T(8,128)S(1)}, f32[3,8,512]{2,1,0:T(8,128)}, u32[]{:S(2)}) copy-start(f32[3,8,512]{2,1,0:T(8,128)} %refs_11_.1) | copy-start | bytes 147460
  12.5 30.5 %copy-start.9 = (f32[3,8,512]{2,1,0:T(8,128)S(1)}, f32[3,8,512]{2,1,0:T(8,128)}, u32[]{:S(2)}) copy-start(f32[3,8,512]{2,1,0:T(8,128)} %refs_12_.1) | copy-start | bytes 147460
  12.6 30.5 %copy-start.10 = (f32[3,8,512]{2,1,0:T(8,128)S(1)}, f32[3,8,512]{2,1,0:T(8,128)}, u32[]{:S(2)}) copy-start(f32[3,8,512]{2,1,0:T(8,128)} %refs_13_.1) | copy-start | bytes 147460
  14.4 1.8 %collective-permute-start.4 = (bf16[4,400,128]{2,1,0:T(8,128)(2,1)S(1)}, bf16[4,400,128]{2,1,0:T(8,128)(2,1)S(1)}, u32[]{:S(2)}, u32[]{:S(2)}) collective-permute-start(bf16[4,400,128]{2,1,0:T(8,128)(2,1)S(1)} %get-tuple-element.73), channel_id=1, source_target_pairs={{0,8},{1,9},{2,10},{3,11},{4,12},{5,13},{6,14},{7,15},{8,0},{9,1},... | collective-permute-start | bytes 1228808 | tf_op jit(solution)/shard_map/ppermute | solution.py:81
  14.4 6.6 %collective-permute-start.5 = (bf16[128,640]{1,0:T(8,128)(2,1)S(1)}, bf16[128,640]{1,0:T(8,128)(2,1)S(1)}, u32[]{:S(2)}, u32[]{:S(2)}) collective-permute-start(bf16[128,640]{1,0:T(8,128)(2,1)S(1)} %get-tuple-element.76), channel_id=1, source_target_pairs={{0,2},{1,3},{2,0},{3,1},{4,6},{5,7},{6,4},{7,5},{8,10},{9,11},{10,... | collective-permute-start | bytes 491528 | tf_op jit(solution)/shard_map/ppermute | solution.py:87
  16.2 26.9 %copy-start.3 = (f32[512,512]{1,0:T(8,128)S(1)}, f32[512,512]{1,0:T(8,128)}, u32[]{:S(2)}) copy-start(f32[512,512]{1,0:T(8,128)} %refs_9_.1) | copy-start | bytes 3145732
  16.2 26.9 %copy-start.7 = (f32[1,512,128]{2,1,0:T(8,128)S(1)}, f32[1,512,128]{2,1,0:T(8,128)}, u32[]{:S(2)}) copy-start(f32[1,512,128]{2,1,0:T(8,128)} %param.24) | copy-start | bytes 786436
  16.3 26.8 %copy-start = (f32[512,512]{1,0:T(8,128)S(1)}, f32[512,512]{1,0:T(8,128)}, u32[]{:S(2)}) copy-start(f32[512,512]{1,0:T(8,128)} %refs_8_.1) | copy-start | bytes 3145732
  16.3 7.4 %collective-permute-start.6 = (bf16[400,128]{1,0:T(8,128)(2,1)S(1)}, bf16[400,128]{1,0:T(8,128)(2,1)S(1)}, u32[]{:S(2)}, u32[]{:S(2)}) collective-permute-start(bf16[400,128]{1,0:T(8,128)(2,1)S(1)} %get-tuple-element.80), channel_id=1, source_target_pairs={{0,1},{1,0},{2,3},{3,2},{4,5},{5,4},{6,7},{7,6},{8,9},{9,8},{10,11... | collective-permute-start | bytes 307208 | tf_op jit(solution)/shard_map/ppermute | solution.py:84
  18.0 5.7 %collective-permute-start.7 = (bf16[400,128]{1,0:T(8,128)(2,1)S(1)}, bf16[400,128]{1,0:T(8,128)(2,1)S(1)}, u32[]{:S(2)}, u32[]{:S(2)}) collective-permute-start(bf16[400,128]{1,0:T(8,128)(2,1)S(1)} %get-tuple-element.81), channel_id=1, source_target_pairs={{0,16},{1,17},{2,18},{3,19},{4,20},{5,21},{6,22},{7,23},{8,24},{9,... | collective-permute-start | bytes 307208 | tf_op jit(solution)/shard_map/ppermute | solution.py:84
  19.5 5.6 %collective-permute-start.8 = (bf16[400,128]{1,0:T(8,128)(2,1)S(1)}, bf16[400,128]{1,0:T(8,128)(2,1)S(1)}, u32[]{:S(2)}, u32[]{:S(2)}) collective-permute-start(bf16[400,128]{1,0:T(8,128)(2,1)S(1)} %get-tuple-element.82), channel_id=1, source_target_pairs={{0,17},{1,16},{2,19},{3,18},{4,21},{5,20},{6,23},{7,22},{8,25},{9,... | collective-permute-start | bytes 307208 | tf_op jit(solution)/shard_map/ppermute | solution.py:84
  21.1 9.1 %collective-permute-start.12 = (bf16[64,640]{1,0:T(8,128)(2,1)S(1)}, bf16[64,640]{1,0:T(8,128)(2,1)S(1)}, u32[]{:S(2)}, u32[]{:S(2)}) collective-permute-start(bf16[64,640]{1,0:T(8,128)(2,1)S(1)} %get-tuple-element.85), channel_id=1, source_target_pairs={{0,4},{1,5},{2,6},{3,7},{4,0},{5,1},{6,2},{7,3},{8,12},{9,13},{10,... | collective-permute-start | bytes 245768 | tf_op jit(solution)/shard_map/ppermute | solution.py:87
  25.1 6.2 %collective-permute-start.11 = (bf16[272,128]{1,0:T(8,128)(2,1)S(1)}, bf16[272,128]{1,0:T(8,128)(2,1)S(1)}, u32[]{:S(2)}, u32[]{:S(2)}) collective-permute-start(bf16[272,128]{1,0:T(8,128)(2,1)S(1)} %get-tuple-element.83), channel_id=1, source_target_pairs={{0,6},{1,7},{2,4},{3,5},{4,2},{5,3},{6,0},{7,1},{8,14},{9,15},{10,... | collective-permute-start | bytes 208904 | tf_op jit(solution)/shard_map/ppermute | solution.py:87
  28.8 5.3 %collective-permute-start.10 = (bf16[272,128]{1,0:T(8,128)(2,1)S(1)}, bf16[272,128]{1,0:T(8,128)(2,1)S(1)}, u32[]{:S(2)}, u32[]{:S(2)}) collective-permute-start(bf16[272,128]{1,0:T(8,128)(2,1)S(1)} %get-tuple-element.83), channel_id=1, source_target_pairs={{0,4},{1,5},{2,6},{3,7},{4,0},{5,1},{6,2},{7,3},{8,12},{9,13},{10,... | collective-permute-start | bytes 208904 | tf_op jit(solution)/shard_map/ppermute | solution.py:87
  28.8 5.3 %collective-permute-start.9 = (bf16[272,128]{1,0:T(8,128)(2,1)S(1)}, bf16[272,128]{1,0:T(8,128)(2,1)S(1)}, u32[]{:S(2)}, u32[]{:S(2)}) collective-permute-start(bf16[272,128]{1,0:T(8,128)(2,1)S(1)} %get-tuple-element.83), channel_id=1, source_target_pairs={{0,2},{1,3},{2,0},{3,1},{4,6},{5,7},{6,4},{7,5},{8,10},{9,11},{10,... | collective-permute-start | bytes 208904 | tf_op jit(solution)/shard_map/ppermute | solution.py:87
  30.2 12.8 %copy-start.6 = (f32[1,512,128]{2,1,0:T(8,128)S(1)}, f32[1,512,128]{2,1,0:T(8,128)}, u32[]{:S(2)}) copy-start(f32[1,512,128]{2,1,0:T(8,128)} %param.23) | copy-start | bytes 786436
  30.9 12.2 %copy-start.2 = (f32[1,512,128]{2,1,0:T(8,128)S(1)}, f32[1,512,128]{2,1,0:T(8,128)}, u32[]{:S(2)}) copy-start(f32[1,512,128]{2,1,0:T(8,128)} %param.22) | copy-start | bytes 786436
  34.2 6.1 %collective-permute-start.15 = (bf16[352,128]{1,0:T(8,128)(2,1)S(1)}, bf16[352,128]{1,0:T(8,128)(2,1)S(1)}, u32[]{:S(2)}, u32[]{:S(2)}) collective-permute-start(bf16[352,128]{1,0:T(8,128)(2,1)S(1)} %get-tuple-element.96), channel_id=1, source_target_pairs={{0,17},{1,16},{2,19},{3,18},{4,21},{5,20},{6,23},{7,22},{8,25},{9,... | collective-permute-start | bytes 270344 | tf_op jit(solution)/shard_map/ppermute | solution.py:84
  36.6 4.6 %collective-permute-start.13 = (bf16[352,128]{1,0:T(8,128)(2,1)S(1)}, bf16[352,128]{1,0:T(8,128)(2,1)S(1)}, u32[]{:S(2)}, u32[]{:S(2)}) collective-permute-start(bf16[352,128]{1,0:T(8,128)(2,1)S(1)} %get-tuple-element.96), channel_id=1, source_target_pairs={{0,1},{1,0},{2,3},{3,2},{4,5},{5,4},{6,7},{7,6},{8,9},{9,8},{10,11... | collective-permute-start | bytes 270344 | tf_op jit(solution)/shard_map/ppermute | solution.py:84
  37.2 4.5 %collective-permute-start.14 = (bf16[352,128]{1,0:T(8,128)(2,1)S(1)}, bf16[352,128]{1,0:T(8,128)(2,1)S(1)}, u32[]{:S(2)}, u32[]{:S(2)}) collective-permute-start(bf16[352,128]{1,0:T(8,128)(2,1)S(1)} %get-tuple-element.95.refs_0_), channel_id=1, source_target_pairs={{0,16},{1,17},{2,18},{3,19},{4,20},{5,21},{6,22},{7,23},{8,24},{9,... | collective-permute-start | bytes 270344 | tf_op jit(solution)/shard_map/ppermute | solution.py:84
  37.8 4.0 %collective-permute-start.16 = (bf16[352,128]{1,0:T(8,128)(2,1)S(1)}, bf16[352,128]{1,0:T(8,128)(2,1)S(1)}, u32[]{:S(2)}, u32[]{:S(2)}) collective-permute-start(bf16[352,128]{1,0:T(8,128)(2,1)S(1)} %get-tuple-element.95.refs_0_), channel_id=1, source_target_pairs={{0,8},{1,9},{2,10},{3,11},{4,12},{5,13},{6,14},{7,15},{8,0},{9,1},... | collective-permute-start | bytes 270344 | tf_op jit(solution)/shard_map/ppermute | solution.py:81
  40.3 1.5 %collective-permute-start.19 = (bf16[352,128]{1,0:T(8,128)(2,1)S(1)}, bf16[352,128]{1,0:T(8,128)(2,1)S(1)}, u32[]{:S(2)}, u32[]{:S(2)}) collective-permute-start(bf16[352,128]{1,0:T(8,128)(2,1)S(1)} %collective-permute-done.15.refs_3_), channel_id=1, source_target_pairs={{0,8},{1,9},{2,10},{3,11},{4,12},{5,13},{6,14},{7,15},{8,0},{9,1},... | collective-permute-start | bytes 270344 | tf_op jit(solution)/shard_map/ppermute | solution.py:81
  41.2 1.3 %collective-permute-start.17 = (bf16[352,128]{1,0:T(8,128)(2,1)S(1)}, bf16[352,128]{1,0:T(8,128)(2,1)S(1)}, u32[]{:S(2)}, u32[]{:S(2)}) collective-permute-start(bf16[352,128]{1,0:T(8,128)(2,1)S(1)} %collective-permute-done.13.refs_1_), channel_id=1, source_target_pairs={{0,8},{1,9},{2,10},{3,11},{4,12},{5,13},{6,14},{7,15},{8,0},{9,1},... | collective-permute-start | bytes 270344 | tf_op jit(solution)/shard_map/ppermute | solution.py:81
  41.7 1.3 %collective-permute-start.18 = (bf16[352,128]{1,0:T(8,128)(2,1)S(1)}, bf16[352,128]{1,0:T(8,128)(2,1)S(1)}, u32[]{:S(2)}, u32[]{:S(2)}) collective-permute-start(bf16[352,128]{1,0:T(8,128)(2,1)S(1)} %collective-permute-done.14.refs_2_), channel_id=1, source_target_pairs={{0,8},{1,9},{2,10},{3,11},{4,12},{5,13},{6,14},{7,15},{8,0},{9,1},... | collective-permute-start | bytes 270344 | tf_op jit(solution)/shard_map/ppermute | solution.py:81

commit v6 on v4

--- a/solution.py
+++ b/solution.py
@@ -229,9 +229,9 @@
 
 
 def core_body(plan, keep_ref, got_ref, own_ref, *send_refs):
-    own_ref[...] = keep_ref[0] + got_ref[0].astype(f32)
+    own_ref[...] = keep_ref[0].astype(f32) + got_ref[0].astype(f32)
     for k in range(1, plan.quads):
-        send_refs[k - 1][...] = (keep_ref[k] + got_ref[k].astype(f32)).astype(bf16)
+        send_refs[k - 1][...] = (keep_ref[k].astype(f32) + got_ref[k].astype(f32)).astype(bf16)
 
 
 def place_of():
@@ -363,7 +363,10 @@
         new = adamw(hw[at, :], grad, hm[at, :], hv[at, :], 0.02, 0.01)
         for ref, v in zip(head_refs, new + (new[0],)):
             ref[at, :] = v.astype(ref.dtype)
-        if i % 2:
+        if i < 2:
+            for source, target in zip(block_refs + head_refs, block_outs + head_outs):
+                send(source.at[at], target.at[at])
+        elif i % 2:
             both = pl.ds(pl.multiple_of(shard_of(i) // 2 * (2 * stride), 2 * stride), 2 * stride)
             for source, target in zip(block_refs + head_refs, block_outs + head_outs):
                 send(source.at[both], target.at[both])
@@ -446,7 +449,7 @@
         functools.partial(local_body, plan),
         [
             shape((quads, total, LANES), bf16),
-            shape((quads, total, LANES), f32),
+            shape((quads, total, LANES), bf16),
             shape((objs // 2, back), f32),
             shape((objs // 2, back), bf16),
         ],
@@ -537,7 +540,7 @@
         [pltpu.VMEM(*r) for r in results]
         + [
             pltpu.VMEM((plan.items // 2, plan.n_mem, plan.groups, LANES), f32),
-            pltpu.SemaphoreType.DMA((7 + 8 * plan.quads,)),
+            pltpu.SemaphoreType.DMA((15 + 8 * plan.quads,)),
         ],
         name="update",
         out_spec=pl.BlockSpec(memory_space=pl.ANY),

time: 46.1 us -> 46 us (level)
  no operation moved by 1% of the time
where the time goes in v6:
time: 46 us; the launch traced here: 45.8 us
  starting transfers between devices  23.1 us (50%)
  waiting for transfers between devices  12.9 us (28%)
  Pallas kernels  6.56 us (14%)
  local copies, waits for them, and re-layouts  2.24 us (5%)
  between operations  0.86 us (2%)
    ppermute x8, starting transfers between devices, over_outer(): return lax.ppermute(v, ALL, self.perm(lambda o, m: (o, m ^ k << 1)))  14.2 us
    ppermute x7, starting transfers between devices, over_plane(): lax.ppermute(v, ALL, self.perm(lambda o, m: (o ^ k >> 1 << 1, m ^ k & 1)))  8.83 us
    pallas_call x10, Pallas kernels, call(): pl.pallas_call(body, out_shape=outs, in_specs=specs, out_specs=[out_spec]...  6.56 us
    ppermute x8, waiting for transfers between devices, over_outer(): return lax.ppermute(v, ALL, self.perm(lambda o, m: (o, m ^ k << 1)))  6 us
    ppermute x7, waiting for transfers between devices, over_plane(): lax.ppermute(v, ALL, self.perm(lambda o, m: (o ^ k >> 1 << 1, m ^ k & 1)))  5.31 us
    unnamed x32, local copies, waits for them, and re-layouts  2.24 us
    ppermute x5, waiting for transfers between devices, over_core(): return lax.ppermute(v, ALL, self.perm(lambda o, m: (o ^ 1, m)))  1.59 us
  transfers between devices with their start and end apart: 20, of which 12 were waited for; matrix products, arithmetic and copies ran while one was open for 0% of the time, Pallas kernels for 4%

profile of v6, /device:TPU:0, one launch (start us, length us, event | category | flops | bytes accessed | tf_op | source)
XLA Modules:
  0.0 45.8 jit_solution(12448658126304277478)
XLA Ops:
  0.7 5.1 %collective-permute-start.2 = (bf16[64,512]{1,0:T(8,128)(2,1)}, bf16[64,512]{1,0:T(8,128)(2,1)S(1)}, u32[]{:S(2)}, u32[]{:S(2)}) collective-permute-start(bf16[64,512]{1,0:T(8,128)(2,1)} %refs_0_.3), channel_id=1, source_target_pairs={{0,6},{1,7},{2,4},{3,5},{4,2},{5,3},{6,0},{7,1},{8,14},{9,15},{10,... | collective-permute-start | bytes 196616 | tf_op jit(solution)/shard_map/ppermute | solution.py:87
  5.8 0.0 collective-permute-start.1
  5.8 0.6 %collective-permute-start = (bf16[64,512]{1,0:T(8,128)(2,1)}, bf16[64,512]{1,0:T(8,128)(2,1)S(1)}, u32[]{:S(2)}, u32[]{:S(2)}) collective-permute-start(bf16[64,512]{1,0:T(8,128)(2,1)} %refs_0_.3), channel_id=1, source_target_pairs={{0,2},{1,3},{2,0},{3,1},{4,6},{5,7},{6,4},{7,5},{8,10},{9,11},{10,... | collective-permute-start | bytes 196616 | tf_op jit(solution)/shard_map/ppermute | solution.py:87
  6.4 0.9 %copy-done.2 = f32[1,512,128]{2,1,0:T(8,128)S(1)} copy-done((f32[1,512,128]{2,1,0:T(8,128)S(1)}, f32[1,512,128]{2,1,0:T(8,128)}, u32[]{:S(2)}) %copy-start.2) | copy-done | bytes 262168
  7.4 0.0 copy-start.13
  7.4 0.0 copy-start.14
  7.4 1.7 %collective-permute-start.3 = (bf16[528,128]{1,0:T(8,128)(2,1)S(1)}, bf16[528,128]{1,0:T(8,128)(2,1)S(1)}, u32[]{:S(2)}, u32[]{:S(2)}) collective-permute-start(bf16[528,128]{1,0:T(8,128)(2,1)S(1)} %head_low.1.refs_7_), channel_id=1, source_target_pairs={{0,1},{1,0},{2,3},{3,2},{4,5},{5,4},{6,7},{7,6},{8,9},{9,8},{10,11... | collective-permute-start | bytes 405512 | tf_op jit(solution)/shard_map/ppermute | solution.py:84
  9.2 0.0 copy-done.15
  9.2 0.1 fusion.refs_4_
  9.3 0.0 copy-start
  9.3 1.2 %copy-done = f32[512,512]{1,0:T(8,128)S(1)} copy-done((f32[512,512]{1,0:T(8,128)S(1)}, f32[512,512]{1,0:T(8,128)}, u32[]{:S(2)}) %copy-start) | copy-done | bytes 1048600
  10.6 0.1 weight_low.1
  10.6 0.0 collective-permute-done.2.refs_1_.refs_3_
  10.6 1.0 %collective-permute-done.1.refs_2_ = bf16[64,512]{1,0:T(8,128)(2,1)S(1)} collective-permute-done((bf16[64,512]{1,0:T(8,128)(2,1)}, bf16[64,512]{1,0:T(8,128)(2,1)S(1)}, u32[]{:S(2)}, u32[]{:S(2)}) %collective-permute-start.1) | collective-permute-done | bytes 65568 | tf_op jit(solution)/shard_map/ppermute | solution.py:87
  11.6 0.0 collective-permute-done.refs_3_.refs_1_
  11.6 0.0 copy-done.7
  11.6 0.9 %forward.1 = (bf16[512,512]{1,0:T(8,128)(2,1)S(1)}, f32[512,512]{1,0:T(8,128)S(1)}, bf16[512,512]{1,0:T(8,128)(2,1)S(1)}, f32[512,512]{1,0:T(8,128)S(1)}) custom-call(bf16[64,512]{1,0:T(8,128)(2,1)S(1)} %copy-done.7, bf16[64,512]{1,0:T(8,128)(2,1)S(1)} %collective-permute-done.2.refs_1_.refs_3_, bf16[64,512]{1,0:T(8,128)(2,1)S(1)} %collective-permute-done.1.refs_2_, ...), custom_call_target="tpu_custom_call" | custom-call | tf_op jit(solution)/shard_map/forward/pallas_call | solution.py:46
  12.5 0.0 collective-permute-done.3.refs_8_
  12.5 0.0 copy-start.8
  12.5 0.0 copy-start.9
  12.5 1.8 %local.1 = (bf16[4,400,128]{2,1,0:T(8,128)(2,1)S(1)}, bf16[4,400,128]{2,1,0:T(8,128)(2,1)S(1)}, f32[128,640]{1,0:T(8,128)S(1)}, bf16[128,640]{1,0:T(8,128)(2,1)S(1)}) custom-call(bf16[64,512]{1,0:T(8,128)(2,1)S(1)} %copy-done.7, bf16[64,512]{1,0:T(8,128)(2,1)S(1)} %collective-permute-done.refs_3_.refs_1_, ...), custom_call_target="tpu_custom_call" | custom-call | tf_op jit(solution)/shard_map/local/pallas_call | solution.py:46
  14.4 0.1 collective-permute-start.4
  14.4 1.4 %collective-permute-start.5 = (bf16[128,640]{1,0:T(8,128)(2,1)S(1)}, bf16[128,640]{1,0:T(8,128)(2,1)S(1)}, u32[]{:S(2)}, u32[]{:S(2)}) collective-permute-start(bf16[128,640]{1,0:T(8,128)(2,1)S(1)} %get-tuple-element.72), channel_id=1, source_target_pairs={{0,2},{1,3},{2,0},{3,1},{4,6},{5,7},{6,4},{7,5},{8,10},{9,11},{10,... | collective-permute-start | bytes 491528 | tf_op jit(solution)/shard_map/ppermute | solution.py:87
  15.9 0.3 collective-permute-done.4.got_ref
  16.2 0.1 core_sum.1
  16.3 0.0 copy-start.1
  16.3 1.7 %collective-permute-start.6 = (bf16[400,128]{1,0:T(8,128)(2,1)S(1)}, bf16[400,128]{1,0:T(8,128)(2,1)S(1)}, u32[]{:S(2)}, u32[]{:S(2)}) collective-permute-start(bf16[400,128]{1,0:T(8,128)(2,1)S(1)} %get-tuple-element.76), channel_id=1, source_target_pairs={{0,1},{1,0},{2,3},{3,2},{4,5},{5,4},{6,7},{7,6},{8,9},{9,8},{10,11... | collective-permute-start | bytes 307208 | tf_op jit(solution)/shard_map/ppermute | solution.py:84
  18.0 1.5 %collective-permute-start.7 = (bf16[400,128]{1,0:T(8,128)(2,1)S(1)}, bf16[400,128]{1,0:T(8,128)(2,1)S(1)}, u32[]{:S(2)}, u32[]{:S(2)}) collective-permute-start(bf16[400,128]{1,0:T(8,128)(2,1)S(1)} %get-tuple-element.77), channel_id=1, source_target_pairs={{0,16},{1,17},{2,18},{3,19},{4,20},{5,21},{6,22},{7,23},{8,24},{9,... | collective-permute-start | bytes 307208 | tf_op jit(solution)/shard_map/ppermute | solution.py:84
  19.5 0.4 collective-permute-start.8
  19.8 1.2 %collective-permute-done.5.got_ref = bf16[128,640]{1,0:T(8,128)(2,1)S(1)} collective-permute-done((bf16[128,640]{1,0:T(8,128)(2,1)S(1)}, bf16[128,640]{1,0:T(8,128)(2,1)S(1)}, u32[]{:S(2)}, u32[]{:S(2)}) %collective-permute-start.5) | collective-permute-done | bytes 163872 | tf_op jit(solution)/shard_map/ppermute | solution.py:87
  21.1 2.6 %collective-permute-start.12 = (bf16[64,640]{1,0:T(8,128)(2,1)S(1)}, bf16[64,640]{1,0:T(8,128)(2,1)S(1)}, u32[]{:S(2)}, u32[]{:S(2)}) collective-permute-start(bf16[64,640]{1,0:T(8,128)(2,1)S(1)} %get-tuple-element.81), channel_id=1, source_target_pairs={{0,4},{1,5},{2,6},{3,7},{4,0},{5,1},{6,2},{7,3},{8,12},{9,13},{10,... | collective-permute-start | bytes 245768 | tf_op jit(solution)/shard_map/ppermute | solution.py:87
  23.7 0.0 collective-permute-done.6.refs_0_
  23.7 0.0 collective-permute-done.7.refs_1_
  23.7 1.3 %collective-permute-done.8.refs_2_ = bf16[400,128]{1,0:T(8,128)(2,1)S(1)} collective-permute-done((bf16[400,128]{1,0:T(8,128)(2,1)S(1)}, bf16[400,128]{1,0:T(8,128)(2,1)S(1)}, u32[]{:S(2)}, u32[]{:S(2)}) %collective-permute-start.8) | collective-permute-done | bytes 102432 | tf_op jit(solution)/shard_map/ppermute | solution.py:84
  25.0 0.1 plane_sum.1
  25.2 3.7 %collective-permute-start.11 = (bf16[272,128]{1,0:T(8,128)(2,1)S(1)}, bf16[272,128]{1,0:T(8,128)(2,1)S(1)}, u32[]{:S(2)}, u32[]{:S(2)}) collective-permute-start(bf16[272,128]{1,0:T(8,128)(2,1)S(1)} %get-tuple-element.79), channel_id=1, source_target_pairs={{0,6},{1,7},{2,4},{3,5},{4,2},{5,3},{6,0},{7,1},{8,14},{9,15},{10,... | collective-permute-start | bytes 208904 | tf_op jit(solution)/shard_map/ppermute | solution.py:87
  28.8 0.0 collective-permute-start.10
  28.8 0.8 %collective-permute-start.9 = (bf16[272,128]{1,0:T(8,128)(2,1)S(1)}, bf16[272,128]{1,0:T(8,128)(2,1)S(1)}, u32[]{:S(2)}, u32[]{:S(2)}) collective-permute-start(bf16[272,128]{1,0:T(8,128)(2,1)S(1)} %get-tuple-element.79), channel_id=1, source_target_pairs={{0,2},{1,3},{2,0},{3,1},{4,6},{5,7},{6,4},{7,5},{8,10},{9,11},{10,... | collective-permute-start | bytes 208904 | tf_op jit(solution)/shard_map/ppermute | solution.py:87
  29.6 0.6 %collective-permute-done.12.got_ref = bf16[64,640]{1,0:T(8,128)(2,1)S(1)} collective-permute-done((bf16[64,640]{1,0:T(8,128)(2,1)S(1)}, bf16[64,640]{1,0:T(8,128)(2,1)S(1)}, u32[]{:S(2)}, u32[]{:S(2)}) %collective-permute-start.12) | collective-permute-done | bytes 81952 | tf_op jit(solution)/shard_map/ppermute | solution.py:87
  30.3 0.7 %back_sum.1 = (f32[64,512]{1,0:T(8,128)}, f32[64,128]{1,0:T(8,128)}) custom-call(f32[64,640]{1,0:T(8,128)S(1)} %get-tuple-element.80.had_ref, bf16[64,640]{1,0:T(8,128)(2,1)S(1)} %collective-permute-done.12.got_ref), custom_call_target="tpu_custom_call" | custom-call | tf_op jit(solution)/shard_map/back_sum/pallas_call | solution.py:46
  30.9 0.4 collective-permute-done.11.refs_2_
  31.3 2.8 %collective-permute-done.10.refs_1_ = bf16[272,128]{1,0:T(8,128)(2,1)S(1)} collective-permute-done((bf16[272,128]{1,0:T(8,128)(2,1)S(1)}, bf16[272,128]{1,0:T(8,128)(2,1)S(1)}, u32[]{:S(2)}, u32[]{:S(2)}) %collective-permute-start.10) | collective-permute-done | bytes 69664 | tf_op jit(solution)/shard_map/ppermute | solution.py:87
  34.1 0.0 collective-permute-done.9.refs_0_
  34.1 0.1 outer_sum.1
  34.2 2.4 %collective-permute-start.15 = (bf16[352,128]{1,0:T(8,128)(2,1)S(1)}, bf16[352,128]{1,0:T(8,128)(2,1)S(1)}, u32[]{:S(2)}, u32[]{:S(2)}) collective-permute-start(bf16[352,128]{1,0:T(8,128)(2,1)S(1)} %get-tuple-element.92), channel_id=1, source_target_pairs={{0,17},{1,16},{2,19},{3,18},{4,21},{5,20},{6,23},{7,22},{8,25},{9,... | collective-permute-start | bytes 270344 | tf_op jit(solution)/shard_map/ppermute | solution.py:84
  36.7 0.6 %collective-permute-start.13 = (bf16[352,128]{1,0:T(8,128)(2,1)S(1)}, bf16[352,128]{1,0:T(8,128)(2,1)S(1)}, u32[]{:S(2)}, u32[]{:S(2)}) collective-permute-start(bf16[352,128]{1,0:T(8,128)(2,1)S(1)} %get-tuple-element.92), channel_id=1, source_target_pairs={{0,1},{1,0},{2,3},{3,2},{4,5},{5,4},{6,7},{7,6},{8,9},{9,8},{10,11... | collective-permute-start | bytes 270344 | tf_op jit(solution)/shard_map/ppermute | solution.py:84
  37.2 0.6 %collective-permute-start.14 = (bf16[352,128]{1,0:T(8,128)(2,1)S(1)}, bf16[352,128]{1,0:T(8,128)(2,1)S(1)}, u32[]{:S(2)}, u32[]{:S(2)}) collective-permute-start(bf16[352,128]{1,0:T(8,128)(2,1)S(1)} %get-tuple-element.91.refs_0_), channel_id=1, source_target_pairs={{0,16},{1,17},{2,18},{3,19},{4,20},{5,21},{6,22},{7,23},{8,24},{9,... | collective-permute-start | bytes 270344 | tf_op jit(solution)/shard_map/ppermute | solution.py:84
  37.8 0.0 collective-permute-start.16
  37.8 2.5 %collective-permute-done.15.refs_3_ = bf16[352,128]{1,0:T(8,128)(2,1)S(1)} collective-permute-done((bf16[352,128]{1,0:T(8,128)(2,1)S(1)}, bf16[352,128]{1,0:T(8,128)(2,1)S(1)}, u32[]{:S(2)}, u32[]{:S(2)}) %collective-permute-start.15) | collective-permute-done | bytes 90144 | tf_op jit(solution)/shard_map/ppermute | solution.py:84
  40.3 0.0 collective-permute-start.19
  40.3 0.9 %collective-permute-done.13.refs_1_ = bf16[352,128]{1,0:T(8,128)(2,1)S(1)} collective-permute-done((bf16[352,128]{1,0:T(8,128)(2,1)S(1)}, bf16[352,128]{1,0:T(8,128)(2,1)S(1)}, u32[]{:S(2)}, u32[]{:S(2)}) %collective-permute-start.13) | collective-permute-done | bytes 90144 | tf_op jit(solution)/shard_map/ppermute | solution.py:84
  41.2 0.0 collective-permute-start.17
  41.2 0.5 %collective-permute-done.14.refs_2_ = bf16[352,128]{1,0:T(8,128)(2,1)S(1)} collective-permute-done((bf16[352,128]{1,0:T(8,128)(2,1)S(1)}, bf16[352,128]{1,0:T(8,128)(2,1)S(1)}, u32[]{:S(2)}, u32[]{:S(2)}) %collective-permute-start.14) | collective-permute-done | bytes 90144 | tf_op jit(solution)/shard_map/ppermute | solution.py:84
  41.8 0.0 collective-permute-start.18
  41.8 0.0 collective-permute-done.16.refs_4_
  41.8 0.0 collective-permute-done.19.refs_7_
  41.8 0.8 %collective-permute-done.17.refs_5_ = bf16[352,128]{1,0:T(8,128)(2,1)S(1)} collective-permute-done((bf16[352,128]{1,0:T(8,128)(2,1)S(1)}, bf16[352,128]{1,0:T(8,128)(2,1)S(1)}, u32[]{:S(2)}, u32[]{:S(2)}) %collective-permute-start.17) | collective-permute-done | bytes 90144 | tf_op jit(solution)/shard_map/ppermute | solution.py:81
  42.5 0.5 %collective-permute-done.18.refs_6_ = bf16[352,128]{1,0:T(8,128)(2,1)S(1)} collective-permute-done((bf16[352,128]{1,0:T(8,128)(2,1)S(1)}, bf16[352,128]{1,0:T(8,128)(2,1)S(1)}, u32[]{:S(2)}, u32[]{:S(2)}) %collective-permute-start.18) | collective-permute-done | bytes 90144 | tf_op jit(solution)/shard_map/ppermute | solution.py:81
  43.1 0.0 copy-done.9
  43.1 0.0 copy-done.4
  43.1 0.0 copy-done.1
  43.1 0.0 copy-done.3
  43.1 0.0 copy-done.10
  43.1 2.7 %update.1 = (f32[1,128]{1,0:T(1,128)}, f32[512,512]{1,0:T(8,128)}, f32[512,512]{1,0:T(8,128)}, f32[512,512]{1,0:T(8,128)}, bf16[512,512]{1,0:T(8,128)(2,1)}, /*i...) custom-call(bf16[352,128]{1,0:T(8,128)(2,1)S(1)} %get-tuple-element., ...), custom_call_target="tpu_custom_call" | custom-call | tf_op jit(solution)/shard_map/update/pallas_call | solution.py:46
  (19 shorter events, 0.1 us)
Async XLA Ops:
  0.7 5.8 %copy-start.12 = (f32[1,128]{1,0:T(1,128)S(1)}, f32[1,128]{1,0:T(1,128)}, u32[]{:S(2)}) copy-start(f32[1,128]{1,0:T(1,128)} %bias_ref.3) | copy-start | bytes 1540
  0.7 10.0 %collective-permute-start.2 = (bf16[64,512]{1,0:T(8,128)(2,1)}, bf16[64,512]{1,0:T(8,128)(2,1)S(1)}, u32[]{:S(2)}, u32[]{:S(2)}) collective-permute-start(bf16[64,512]{1,0:T(8,128)(2,1)} %refs_0_.3), channel_id=1, source_target_pairs={{0,6},{1,7},{2,4},{3,5},{4,2},{5,3},{6,0},{7,1},{8,14},{9,15},{10,... | collective-permute-start | bytes 196616 | tf_op jit(solution)/shard_map/ppermute | solution.py:87
  5.8 5.8 %collective-permute-start.1 = (bf16[64,512]{1,0:T(8,128)(2,1)}, bf16[64,512]{1,0:T(8,128)(2,1)S(1)}, u32[]{:S(2)}, u32[]{:S(2)}) collective-permute-start(bf16[64,512]{1,0:T(8,128)(2,1)} %refs_0_.3), channel_id=1, source_target_pairs={{0,4},{1,5},{2,6},{3,7},{4,0},{5,1},{6,2},{7,3},{8,12},{9,13},{10,... | collective-permute-start | bytes 196616 | tf_op jit(solution)/shard_map/ppermute | solution.py:87
  5.8 5.8 %collective-permute-start = (bf16[64,512]{1,0:T(8,128)(2,1)}, bf16[64,512]{1,0:T(8,128)(2,1)S(1)}, u32[]{:S(2)}, u32[]{:S(2)}) collective-permute-start(bf16[64,512]{1,0:T(8,128)(2,1)} %refs_0_.3), channel_id=1, source_target_pairs={{0,2},{1,3},{2,0},{3,1},{4,6},{5,7},{6,4},{7,5},{8,10},{9,11},{10,... | collective-permute-start | bytes 196616 | tf_op jit(solution)/shard_map/ppermute | solution.py:87
  6.4 1.0 %copy-start.2 = (f32[1,512,128]{2,1,0:T(8,128)S(1)}, f32[1,512,128]{2,1,0:T(8,128)}, u32[]{:S(2)}) copy-start(f32[1,512,128]{2,1,0:T(8,128)} %param.22) | copy-start | bytes 786436
  7.4 1.8 %copy-start.15 = (s32[512]{0:T(512)S(1)}, s32[512]{0:T(512)}, u32[]{:S(2)}) copy-start(s32[512]{0:T(512)} %param.15) | copy-start | bytes 6148
  7.4 1.9 %copy-start.13 = (f32[1,128]{1,0:T(1,128)S(1)}, f32[1,128]{1,0:T(1,128)}, u32[]{:S(2)}) copy-start(f32[1,128]{1,0:T(1,128)} %first_ref.1) | copy-start | bytes 1540
  7.4 1.9 %copy-start.14 = (f32[1,128]{1,0:T(1,128)S(1)}, f32[1,128]{1,0:T(1,128)}, u32[]{:S(2)}) copy-start(f32[1,128]{1,0:T(1,128)} %second_ref.1) | copy-start | bytes 1540
  7.4 5.1 %collective-permute-start.3 = (bf16[528,128]{1,0:T(8,128)(2,1)S(1)}, bf16[528,128]{1,0:T(8,128)(2,1)S(1)}, u32[]{:S(2)}, u32[]{:S(2)}) collective-permute-start(bf16[528,128]{1,0:T(8,128)(2,1)S(1)} %head_low.1.refs_7_), channel_id=1, source_target_pairs={{0,1},{1,0},{2,3},{3,2},{4,5},{5,4},{6,7},{7,6},{8,9},{9,8},{10,11... | collective-permute-start | bytes 405512 | tf_op jit(solution)/shard_map/ppermute | solution.py:84
  9.3 1.2 %copy-start = (f32[512,512]{1,0:T(8,128)S(1)}, f32[512,512]{1,0:T(8,128)}, u32[]{:S(2)}) copy-start(f32[512,512]{1,0:T(8,128)} %refs_8_.1) | copy-start | bytes 3145732
  10.6 1.0 %copy-start.6 = (f32[3,8,512]{2,1,0:T(8,128)S(1)}, f32[3,8,512]{2,1,0:T(8,128)}, u32[]{:S(2)}) copy-start(f32[3,8,512]{2,1,0:T(8,128)} %refs_11_.1) | copy-start | bytes 147460
  10.6 1.0 %copy-start.7 = (bf16[64,512]{1,0:T(8,128)(2,1)S(1)}, bf16[64,512]{1,0:T(8,128)(2,1)}, u32[]{:S(2)}) copy-start(bf16[64,512]{1,0:T(8,128)(2,1)} %refs_0_.3) | copy-start | bytes 196612
  12.5 30.5 %copy-start.5 = (f32[512,512]{1,0:T(8,128)S(1)}, f32[512,512]{1,0:T(8,128)}, u32[]{:S(2)}) copy-start(f32[512,512]{1,0:T(8,128)} %refs_10_.1) | copy-start | bytes 3145732
  12.5 30.5 %copy-start.8 = (f32[1,512,128]{2,1,0:T(8,128)S(1)}, f32[1,512,128]{2,1,0:T(8,128)}, u32[]{:S(2)}) copy-start(f32[1,512,128]{2,1,0:T(8,128)} %param.23) | copy-start | bytes 786436
  12.5 30.5 %copy-start.9 = (f32[1,512,128]{2,1,0:T(8,128)S(1)}, f32[1,512,128]{2,1,0:T(8,128)}, u32[]{:S(2)}) copy-start(f32[1,512,128]{2,1,0:T(8,128)} %param.24) | copy-start | bytes 786436
  14.4 1.8 %collective-permute-start.4 = (bf16[4,400,128]{2,1,0:T(8,128)(2,1)S(1)}, bf16[4,400,128]{2,1,0:T(8,128)(2,1)S(1)}, u32[]{:S(2)}, u32[]{:S(2)}) collective-permute-start(bf16[4,400,128]{2,1,0:T(8,128)(2,1)S(1)} %get-tuple-element.69), channel_id=1, source_target_pairs={{0,8},{1,9},{2,10},{3,11},{4,12},{5,13},{6,14},{7,15},{8,0},{9,1},... | collective-permute-start | bytes 1228808 | tf_op jit(solution)/shard_map/ppermute | solution.py:81
  14.4 6.6 %collective-permute-start.5 = (bf16[128,640]{1,0:T(8,128)(2,1)S(1)}, bf16[128,640]{1,0:T(8,128)(2,1)S(1)}, u32[]{:S(2)}, u32[]{:S(2)}) collective-permute-start(bf16[128,640]{1,0:T(8,128)(2,1)S(1)} %get-tuple-element.72), channel_id=1, source_target_pairs={{0,2},{1,3},{2,0},{3,1},{4,6},{5,7},{6,4},{7,5},{8,10},{9,11},{10,... | collective-permute-start | bytes 491528 | tf_op jit(solution)/shard_map/ppermute | solution.py:87
  16.2 26.9 %copy-start.4 = (f32[512,512]{1,0:T(8,128)S(1)}, f32[512,512]{1,0:T(8,128)}, u32[]{:S(2)}) copy-start(f32[512,512]{1,0:T(8,128)} %refs_9_.1) | copy-start | bytes 3145732
  16.3 26.8 %copy-start.1 = (f32[512,512]{1,0:T(8,128)S(1)}, f32[512,512]{1,0:T(8,128)}, u32[]{:S(2)}) copy-start(f32[512,512]{1,0:T(8,128)} %refs_8_.1) | copy-start | bytes 3145732
  16.3 7.4 %collective-permute-start.6 = (bf16[400,128]{1,0:T(8,128)(2,1)S(1)}, bf16[400,128]{1,0:T(8,128)(2,1)S(1)}, u32[]{:S(2)}, u32[]{:S(2)}) collective-permute-start(bf16[400,128]{1,0:T(8,128)(2,1)S(1)} %get-tuple-element.76), channel_id=1, source_target_pairs={{0,1},{1,0},{2,3},{3,2},{4,5},{5,4},{6,7},{7,6},{8,9},{9,8},{10,11... | collective-permute-start | bytes 307208 | tf_op jit(solution)/shard_map/ppermute | solution.py:84
  18.0 5.7 %collective-permute-start.7 = (bf16[400,128]{1,0:T(8,128)(2,1)S(1)}, bf16[400,128]{1,0:T(8,128)(2,1)S(1)}, u32[]{:S(2)}, u32[]{:S(2)}) collective-permute-start(bf16[400,128]{1,0:T(8,128)(2,1)S(1)} %get-tuple-element.77), channel_id=1, source_target_pairs={{0,16},{1,17},{2,18},{3,19},{4,20},{5,21},{6,22},{7,23},{8,24},{9,... | collective-permute-start | bytes 307208 | tf_op jit(solution)/shard_map/ppermute | solution.py:84
  19.5 5.6 %collective-permute-start.8 = (bf16[400,128]{1,0:T(8,128)(2,1)S(1)}, bf16[400,128]{1,0:T(8,128)(2,1)S(1)}, u32[]{:S(2)}, u32[]{:S(2)}) collective-permute-start(bf16[400,128]{1,0:T(8,128)(2,1)S(1)} %get-tuple-element.78), channel_id=1, source_target_pairs={{0,17},{1,16},{2,19},{3,18},{4,21},{5,20},{6,23},{7,22},{8,25},{9,... | collective-permute-start | bytes 307208 | tf_op jit(solution)/shard_map/ppermute | solution.py:84
  21.1 9.1 %collective-permute-start.12 = (bf16[64,640]{1,0:T(8,128)(2,1)S(1)}, bf16[64,640]{1,0:T(8,128)(2,1)S(1)}, u32[]{:S(2)}, u32[]{:S(2)}) collective-permute-start(bf16[64,640]{1,0:T(8,128)(2,1)S(1)} %get-tuple-element.81), channel_id=1, source_target_pairs={{0,4},{1,5},{2,6},{3,7},{4,0},{5,1},{6,2},{7,3},{8,12},{9,13},{10,... | collective-permute-start | bytes 245768 | tf_op jit(solution)/shard_map/ppermute | solution.py:87
  25.2 6.2 %collective-permute-start.11 = (bf16[272,128]{1,0:T(8,128)(2,1)S(1)}, bf16[272,128]{1,0:T(8,128)(2,1)S(1)}, u32[]{:S(2)}, u32[]{:S(2)}) collective-permute-start(bf16[272,128]{1,0:T(8,128)(2,1)S(1)} %get-tuple-element.79), channel_id=1, source_target_pairs={{0,6},{1,7},{2,4},{3,5},{4,2},{5,3},{6,0},{7,1},{8,14},{9,15},{10,... | collective-permute-start | bytes 208904 | tf_op jit(solution)/shard_map/ppermute | solution.py:87
  28.8 5.3 %collective-permute-start.10 = (bf16[272,128]{1,0:T(8,128)(2,1)S(1)}, bf16[272,128]{1,0:T(8,128)(2,1)S(1)}, u32[]{:S(2)}, u32[]{:S(2)}) collective-permute-start(bf16[272,128]{1,0:T(8,128)(2,1)S(1)} %get-tuple-element.79), channel_id=1, source_target_pairs={{0,4},{1,5},{2,6},{3,7},{4,0},{5,1},{6,2},{7,3},{8,12},{9,13},{10,... | collective-permute-start | bytes 208904 | tf_op jit(solution)/shard_map/ppermute | solution.py:87
  28.8 5.3 %collective-permute-start.9 = (bf16[272,128]{1,0:T(8,128)(2,1)S(1)}, bf16[272,128]{1,0:T(8,128)(2,1)S(1)}, u32[]{:S(2)}, u32[]{:S(2)}) collective-permute-start(bf16[272,128]{1,0:T(8,128)(2,1)S(1)} %get-tuple-element.79), channel_id=1, source_target_pairs={{0,2},{1,3},{2,0},{3,1},{4,6},{5,7},{6,4},{7,5},{8,10},{9,11},{10,... | collective-permute-start | bytes 208904 | tf_op jit(solution)/shard_map/ppermute | solution.py:87
  30.9 12.1 %copy-start.3 = (f32[1,512,128]{2,1,0:T(8,128)S(1)}, f32[1,512,128]{2,1,0:T(8,128)}, u32[]{:S(2)}) copy-start(f32[1,512,128]{2,1,0:T(8,128)} %param.22) | copy-start | bytes 786436
  34.1 9.0 %copy-start.10 = (f32[3,8,512]{2,1,0:T(8,128)S(1)}, f32[3,8,512]{2,1,0:T(8,128)}, u32[]{:S(2)}) copy-start(f32[3,8,512]{2,1,0:T(8,128)} %refs_12_.1) | copy-start | bytes 147460
  34.1 9.0 %copy-start.11 = (f32[3,8,512]{2,1,0:T(8,128)S(1)}, f32[3,8,512]{2,1,0:T(8,128)}, u32[]{:S(2)}) copy-start(f32[3,8,512]{2,1,0:T(8,128)} %refs_13_.1) | copy-start | bytes 147460
  34.2 6.1 %collective-permute-start.15 = (bf16[352,128]{1,0:T(8,128)(2,1)S(1)}, bf16[352,128]{1,0:T(8,128)(2,1)S(1)}, u32[]{:S(2)}, u32[]{:S(2)}) collective-permute-start(bf16[352,128]{1,0:T(8,128)(2,1)S(1)} %get-tuple-element.92), channel_id=1, source_target_pairs={{0,17},{1,16},{2,19},{3,18},{4,21},{5,20},{6,23},{7,22},{8,25},{9,... | collective-permute-start | bytes 270344 | tf_op jit(solution)/shard_map/ppermute | solution.py:84
  36.7 4.6 %collective-permute-start.13 = (bf16[352,128]{1,0:T(8,128)(2,1)S(1)}, bf16[352,128]{1,0:T(8,128)(2,1)S(1)}, u32[]{:S(2)}, u32[]{:S(2)}) collective-permute-start(bf16[352,128]{1,0:T(8,128)(2,1)S(1)} %get-tuple-element.92), channel_id=1, source_target_pairs={{0,1},{1,0},{2,3},{3,2},{4,5},{5,4},{6,7},{7,6},{8,9},{9,8},{10,11... | collective-permute-start | bytes 270344 | tf_op jit(solution)/shard_map/ppermute | solution.py:84
  37.2 4.5 %collective-permute-start.14 = (bf16[352,128]{1,0:T(8,128)(2,1)S(1)}, bf16[352,128]{1,0:T(8,128)(2,1)S(1)}, u32[]{:S(2)}, u32[]{:S(2)}) collective-permute-start(bf16[352,128]{1,0:T(8,128)(2,1)S(1)} %get-tuple-element.91.refs_0_), channel_id=1, source_target_pairs={{0,16},{1,17},{2,18},{3,19},{4,20},{5,21},{6,22},{7,23},{8,24},{9,... | collective-permute-start | bytes 270344 | tf_op jit(solution)/shard_map/ppermute | solution.py:84
  37.8 4.0 %collective-permute-start.16 = (bf16[352,128]{1,0:T(8,128)(2,1)S(1)}, bf16[352,128]{1,0:T(8,128)(2,1)S(1)}, u32[]{:S(2)}, u32[]{:S(2)}) collective-permute-start(bf16[352,128]{1,0:T(8,128)(2,1)S(1)} %get-tuple-element.91.refs_0_), channel_id=1, source_target_pairs={{0,8},{1,9},{2,10},{3,11},{4,12},{5,13},{6,14},{7,15},{8,0},{9,1},... | collective-permute-start | bytes 270344 | tf_op jit(solution)/shard_map/ppermute | solution.py:81
  40.3 1.4 %collective-permute-start.19 = (bf16[352,128]{1,0:T(8,128)(2,1)S(1)}, bf16[352,128]{1,0:T(8,128)(2,1)S(1)}, u32[]{:S(2)}, u32[]{:S(2)}) collective-permute-start(bf16[352,128]{1,0:T(8,128)(2,1)S(1)} %collective-permute-done.15.refs_3_), channel_id=1, source_target_pairs={{0,8},{1,9},{2,10},{3,11},{4,12},{5,13},{6,14},{7,15},{8,0},{9,1},... | collective-permute-start | bytes 270344 | tf_op jit(solution)/shard_map/ppermute | solution.py:81
  41.2 1.3 %collective-permute-start.17 = (bf16[352,128]{1,0:T(8,128)(2,1)S(1)}, bf16[352,128]{1,0:T(8,128)(2,1)S(1)}, u32[]{:S(2)}, u32[]{:S(2)}) collective-permute-start(bf16[352,128]{1,0:T(8,128)(2,1)S(1)} %collective-permute-done.13.refs_1_), channel_id=1, source_target_pairs={{0,8},{1,9},{2,10},{3,11},{4,12},{5,13},{6,14},{7,15},{8,0},{9,1},... | collective-permute-start | bytes 270344 | tf_op jit(solution)/shard_map/ppermute | solution.py:81
  41.8 1.3 %collective-permute-start.18 = (bf16[352,128]{1,0:T(8,128)(2,1)S(1)}, bf16[352,128]{1,0:T(8,128)(2,1)S(1)}, u32[]{:S(2)}, u32[]{:S(2)}) collective-permute-start(bf16[352,128]{1,0:T(8,128)(2,1)S(1)} %collective-permute-done.14.refs_2_), channel_id=1, source_target_pairs={{0,8},{1,9},{2,10},{3,11},{4,12},{5,13},{6,14},{7,15},{8,0},{9,1},... | collective-permute-start | bytes 270344 | tf_op jit(solution)/shard_map/ppermute | solution.py:81

commit v7 on v4

--- a/solution.py
+++ b/solution.py
@@ -231,7 +231,7 @@
 def core_body(plan, keep_ref, got_ref, own_ref, *send_refs):
     own_ref[...] = keep_ref[0] + got_ref[0].astype(f32)
     for k in range(1, plan.quads):
-        send_refs[k - 1][...] = (keep_ref[k] + got_ref[k].astype(f32)).astype(bf16)
+        send_refs[-k][...] = (keep_ref[k] + got_ref[k].astype(f32)).astype(bf16)
 
 
 def place_of():
@@ -468,7 +468,7 @@
         [keep, got],
         name="core_sum",
     )
-    got = [plan.over_plane(v, k + 1) for k, v in enumerate(sends)]
+    got = [plan.over_plane(v, quads - 1 - k) for k, v in enumerate(sends)]
     for bit in plan.bits[:-1]:
         half = back_keep.shape[0] // 2
         back_keep, back_send = call(

time: 46.1 us -> 46.1 us (level)
  transfers between devices with their start and end apart: 20 -> 20, of which waited for: 12 -> 11; matrix products, arithmetic and copies ran while one was open for 0% -> 0% of each run, Pallas kernels for 4% -> 4%
where the time goes in v7:
time: 46.1 us; the launch traced here: 45.9 us
  starting transfers between devices  23.5 us (51%)
  waiting for transfers between devices  12.6 us (27%)
  Pallas kernels  6.6 us (14%)
  local copies, waits for them, and re-layouts  2.24 us (5%)
  between operations  0.86 us (2%)
    ppermute x8, starting transfers between devices, over_outer(): return lax.ppermute(v, ALL, self.perm(lambda o, m: (o, m ^ k << 1)))  14.2 us
    ppermute x7, starting transfers between devices, over_plane(): lax.ppermute(v, ALL, self.perm(lambda o, m: (o ^ k >> 1 << 1, m ^ k & 1)))  8.83 us
    pallas_call x10, Pallas kernels, call(): pl.pallas_call(body, out_shape=outs, in_specs=specs, out_specs=[out_spec]...  6.6 us
    ppermute x8, waiting for transfers between devices, over_outer(): return lax.ppermute(v, ALL, self.perm(lambda o, m: (o, m ^ k << 1)))  6.39 us
    ppermute x7, waiting for transfers between devices, over_plane(): lax.ppermute(v, ALL, self.perm(lambda o, m: (o ^ k >> 1 << 1, m ^ k & 1)))  4.92 us
    unnamed x32, local copies, waits for them, and re-layouts  2.24 us
    ppermute x5, waiting for transfers between devices, over_core(): return lax.ppermute(v, ALL, self.perm(lambda o, m: (o ^ 1, m)))  1.27 us
  transfers between devices with their start and end apart: 20, of which 11 were waited for; matrix products, arithmetic and copies ran while one was open for 0% of the time, Pallas kernels for 4%

profile of v7, /device:TPU:0, one launch (start us, length us, event | category | flops | bytes accessed | tf_op | source)
XLA Modules:
  0.0 45.9 jit_solution(3850829903997285727)
XLA Ops:
  0.7 0.0 copy-start.12
  0.7 5.1 %collective-permute-start.2 = (bf16[64,512]{1,0:T(8,128)(2,1)}, bf16[64,512]{1,0:T(8,128)(2,1)S(1)}, u32[]{:S(2)}, u32[]{:S(2)}) collective-permute-start(bf16[64,512]{1,0:T(8,128)(2,1)} %refs_0_.3), channel_id=1, source_target_pairs={{0,6},{1,7},{2,4},{3,5},{4,2},{5,3},{6,0},{7,1},{8,14},{9,15},{10,... | collective-permute-start | bytes 196616 | tf_op jit(solution)/shard_map/ppermute | solution.py:87
  5.8 0.0 collective-permute-start.1
  5.8 0.6 %collective-permute-start = (bf16[64,512]{1,0:T(8,128)(2,1)}, bf16[64,512]{1,0:T(8,128)(2,1)S(1)}, u32[]{:S(2)}, u32[]{:S(2)}) collective-permute-start(bf16[64,512]{1,0:T(8,128)(2,1)} %refs_0_.3), channel_id=1, source_target_pairs={{0,2},{1,3},{2,0},{3,1},{4,6},{5,7},{6,4},{7,5},{8,10},{9,11},{10,... | collective-permute-start | bytes 196616 | tf_op jit(solution)/shard_map/ppermute | solution.py:87
  6.4 0.0 copy-done.12
  6.4 0.9 %copy-done.2 = f32[1,512,128]{2,1,0:T(8,128)S(1)} copy-done((f32[1,512,128]{2,1,0:T(8,128)S(1)}, f32[1,512,128]{2,1,0:T(8,128)}, u32[]{:S(2)}) %copy-start.2) | copy-done | bytes 262168
  7.4 0.0 copy-start.13
  7.4 0.0 copy-start.14
  7.4 1.7 %collective-permute-start.3 = (bf16[528,128]{1,0:T(8,128)(2,1)S(1)}, bf16[528,128]{1,0:T(8,128)(2,1)S(1)}, u32[]{:S(2)}, u32[]{:S(2)}) collective-permute-start(bf16[528,128]{1,0:T(8,128)(2,1)S(1)} %head_low.1.refs_7_), channel_id=1, source_target_pairs={{0,1},{1,0},{2,3},{3,2},{4,5},{5,4},{6,7},{7,6},{8,9},{9,8},{10,11... | collective-permute-start | bytes 405512 | tf_op jit(solution)/shard_map/ppermute | solution.py:84
  9.2 0.0 copy-done.15
  9.2 0.1 fusion.refs_4_
  9.3 0.0 copy-done.13
  9.3 0.0 copy-done.14
  9.3 0.0 copy-start
  9.3 1.2 %copy-done = f32[512,512]{1,0:T(8,128)S(1)} copy-done((f32[512,512]{1,0:T(8,128)S(1)}, f32[512,512]{1,0:T(8,128)}, u32[]{:S(2)}) %copy-start) | copy-done | bytes 1048600
  10.6 0.1 weight_low.1
  10.6 0.0 collective-permute-done.2.refs_1_.refs_3_
  10.6 1.0 %collective-permute-done.1.refs_2_ = bf16[64,512]{1,0:T(8,128)(2,1)S(1)} collective-permute-done((bf16[64,512]{1,0:T(8,128)(2,1)}, bf16[64,512]{1,0:T(8,128)(2,1)S(1)}, u32[]{:S(2)}, u32[]{:S(2)}) %collective-permute-start.1) | collective-permute-done | bytes 65568 | tf_op jit(solution)/shard_map/ppermute | solution.py:87
  11.6 0.0 collective-permute-done.refs_3_.refs_1_
  11.6 0.0 copy-done.6
  11.6 0.0 copy-done.7
  11.6 0.9 %forward.1 = (bf16[512,512]{1,0:T(8,128)(2,1)S(1)}, f32[512,512]{1,0:T(8,128)S(1)}, bf16[512,512]{1,0:T(8,128)(2,1)S(1)}, f32[512,512]{1,0:T(8,128)S(1)}) custom-call(bf16[64,512]{1,0:T(8,128)(2,1)S(1)} %copy-done.7, bf16[64,512]{1,0:T(8,128)(2,1)S(1)} %collective-permute-done.2.refs_1_.refs_3_, bf16[64,512]{1,0:T(8,128)(2,1)S(1)} %collective-permute-done.1.refs_2_, ...), custom_call_target="tpu_custom_call" | custom-call | tf_op jit(solution)/shard_map/forward/pallas_call | solution.py:46
  12.5 0.0 collective-permute-done.3.refs_8_
  12.5 0.0 copy-start.10
  12.5 0.0 copy-start.11
  12.5 1.8 %local.1 = (bf16[4,400,128]{2,1,0:T(8,128)(2,1)S(1)}, f32[4,400,128]{2,1,0:T(8,128)S(1)}, f32[128,640]{1,0:T(8,128)S(1)}, bf16[128,640]{1,0:T(8,128)(2,1)S(1)}) custom-call(bf16[64,512]{1,0:T(8,128)(2,1)S(1)} %copy-done.7, bf16[64,512]{1,0:T(8,128)(2,1)S(1)} %collective-permute-done.refs_3_.refs_1_, bf16[64,512]{1,0:T(8,128)(2,1)S(1)} %collective-permute-done.1.refs_2_, ...), custom_call_target="tpu_custom_call" | custom-call | tf_op jit(solution)/shard_map/local/pallas_call | solution.py:46
  14.4 0.1 collective-permute-start.4
  14.4 1.4 %collective-permute-start.5 = (bf16[128,640]{1,0:T(8,128)(2,1)S(1)}, bf16[128,640]{1,0:T(8,128)(2,1)S(1)}, u32[]{:S(2)}, u32[]{:S(2)}) collective-permute-start(bf16[128,640]{1,0:T(8,128)(2,1)S(1)} %get-tuple-element.72), channel_id=1, source_target_pairs={{0,2},{1,3},{2,0},{3,1},{4,6},{5,7},{6,4},{7,5},{8,10},{9,11},{10,... | collective-permute-start | bytes 491528 | tf_op jit(solution)/shard_map/ppermute | solution.py:87
  15.9 0.3 collective-permute-done.4.got_ref
  16.2 0.1 core_sum.1
  16.3 0.0 copy-start.1
  16.3 2.6 %collective-permute-start.6 = (bf16[400,128]{1,0:T(8,128)(2,1)S(1)}, bf16[400,128]{1,0:T(8,128)(2,1)S(1)}, u32[]{:S(2)}, u32[]{:S(2)}) collective-permute-start(bf16[400,128]{1,0:T(8,128)(2,1)S(1)} %get-tuple-element.76), channel_id=1, source_target_pairs={{0,17},{1,16},{2,19},{3,18},{4,21},{5,20},{6,23},{7,22},{8,25},{9,... | collective-permute-start | bytes 307208 | tf_op jit(solution)/shard_map/ppermute | solution.py:84
  18.9 0.5 %collective-permute-start.7 = (bf16[400,128]{1,0:T(8,128)(2,1)S(1)}, bf16[400,128]{1,0:T(8,128)(2,1)S(1)}, u32[]{:S(2)}, u32[]{:S(2)}) collective-permute-start(bf16[400,128]{1,0:T(8,128)(2,1)S(1)} %get-tuple-element.77), channel_id=1, source_target_pairs={{0,16},{1,17},{2,18},{3,19},{4,20},{5,21},{6,22},{7,23},{8,24},{9,... | collective-permute-start | bytes 307208 | tf_op jit(solution)/shard_map/ppermute | solution.py:84
  19.5 0.4 collective-permute-start.8
  19.9 1.2 %collective-permute-done.5.got_ref = bf16[128,640]{1,0:T(8,128)(2,1)S(1)} collective-permute-done((bf16[128,640]{1,0:T(8,128)(2,1)S(1)}, bf16[128,640]{1,0:T(8,128)(2,1)S(1)}, u32[]{:S(2)}, u32[]{:S(2)}) %collective-permute-start.5) | collective-permute-done | bytes 163872 | tf_op jit(solution)/shard_map/ppermute | solution.py:87
  21.1 2.6 %collective-permute-start.12 = (bf16[64,640]{1,0:T(8,128)(2,1)S(1)}, bf16[64,640]{1,0:T(8,128)(2,1)S(1)}, u32[]{:S(2)}, u32[]{:S(2)}) collective-permute-start(bf16[64,640]{1,0:T(8,128)(2,1)S(1)} %get-tuple-element.81), channel_id=1, source_target_pairs={{0,4},{1,5},{2,6},{3,7},{4,0},{5,1},{6,2},{7,3},{8,12},{9,13},{10,... | collective-permute-start | bytes 245768 | tf_op jit(solution)/shard_map/ppermute | solution.py:87
  23.7 0.0 collective-permute-done.6.refs_0_
  23.7 0.9 %collective-permute-done.7.refs_1_ = bf16[400,128]{1,0:T(8,128)(2,1)S(1)} collective-permute-done((bf16[400,128]{1,0:T(8,128)(2,1)S(1)}, bf16[400,128]{1,0:T(8,128)(2,1)S(1)}, u32[]{:S(2)}, u32[]{:S(2)}) %collective-permute-start.7) | collective-permute-done | bytes 102432 | tf_op jit(solution)/shard_map/ppermute | solution.py:84
  24.5 0.0 collective-permute-done.8.refs_2_
  24.6 0.1 plane_sum.1
  24.7 3.7 %collective-permute-start.11 = (bf16[272,128]{1,0:T(8,128)(2,1)S(1)}, bf16[272,128]{1,0:T(8,128)(2,1)S(1)}, u32[]{:S(2)}, u32[]{:S(2)}) collective-permute-start(bf16[272,128]{1,0:T(8,128)(2,1)S(1)} %get-tuple-element.79), channel_id=1, source_target_pairs={{0,6},{1,7},{2,4},{3,5},{4,2},{5,3},{6,0},{7,1},{8,14},{9,15},{10,... | collective-permute-start | bytes 208904 | tf_op jit(solution)/shard_map/ppermute | solution.py:87
  28.3 0.0 collective-permute-start.10
  28.3 0.8 %collective-permute-start.9 = (bf16[272,128]{1,0:T(8,128)(2,1)S(1)}, bf16[272,128]{1,0:T(8,128)(2,1)S(1)}, u32[]{:S(2)}, u32[]{:S(2)}) collective-permute-start(bf16[272,128]{1,0:T(8,128)(2,1)S(1)} %get-tuple-element.79), channel_id=1, source_target_pairs={{0,2},{1,3},{2,0},{3,1},{4,6},{5,7},{6,4},{7,5},{8,10},{9,11},{10,... | collective-permute-start | bytes 208904 | tf_op jit(solution)/shard_map/ppermute | solution.py:87
  29.1 0.0 collective-permute-done.12.got_ref
  29.1 0.7 %back_sum.1 = (f32[64,512]{1,0:T(8,128)}, f32[64,128]{1,0:T(8,128)}) custom-call(f32[64,640]{1,0:T(8,128)S(1)} %get-tuple-element.80.had_ref, bf16[64,640]{1,0:T(8,128)(2,1)S(1)} %collective-permute-done.12.got_ref), custom_call_target="tpu_custom_call" | custom-call | tf_op jit(solution)/shard_map/back_sum/pallas_call | solution.py:46
  29.8 1.7 %collective-permute-done.11.refs_2_ = bf16[272,128]{1,0:T(8,128)(2,1)S(1)} collective-permute-done((bf16[272,128]{1,0:T(8,128)(2,1)S(1)}, bf16[272,128]{1,0:T(8,128)(2,1)S(1)}, u32[]{:S(2)}, u32[]{:S(2)}) %collective-permute-start.11) | collective-permute-done | bytes 69664 | tf_op jit(solution)/shard_map/ppermute | solution.py:87
  31.5 2.5 %collective-permute-done.10.refs_1_ = bf16[272,128]{1,0:T(8,128)(2,1)S(1)} collective-permute-done((bf16[272,128]{1,0:T(8,128)(2,1)S(1)}, bf16[272,128]{1,0:T(8,128)(2,1)S(1)}, u32[]{:S(2)}, u32[]{:S(2)}) %collective-permute-start.10) | collective-permute-done | bytes 69664 | tf_op jit(solution)/shard_map/ppermute | solution.py:87
  34.0 0.0 collective-permute-done.9.refs_0_
  34.0 0.1 outer_sum.1
  34.1 2.6 %collective-permute-start.15 = (bf16[352,128]{1,0:T(8,128)(2,1)S(1)}, bf16[352,128]{1,0:T(8,128)(2,1)S(1)}, u32[]{:S(2)}, u32[]{:S(2)}) collective-permute-start(bf16[352,128]{1,0:T(8,128)(2,1)S(1)} %get-tuple-element.92), channel_id=1, source_target_pairs={{0,17},{1,16},{2,19},{3,18},{4,21},{5,20},{6,23},{7,22},{8,25},{9,... | collective-permute-start | bytes 270344 | tf_op jit(solution)/shard_map/ppermute | solution.py:84
  36.8 0.4 collective-permute-start.13
  37.2 0.5 %collective-permute-start.14 = (bf16[352,128]{1,0:T(8,128)(2,1)S(1)}, bf16[352,128]{1,0:T(8,128)(2,1)S(1)}, u32[]{:S(2)}, u32[]{:S(2)}) collective-permute-start(bf16[352,128]{1,0:T(8,128)(2,1)S(1)} %get-tuple-element.91.refs_0_), channel_id=1, source_target_pairs={{0,16},{1,17},{2,18},{3,19},{4,20},{5,21},{6,22},{7,23},{8,24},{9,... | collective-permute-start | bytes 270344 | tf_op jit(solution)/shard_map/ppermute | solution.py:84
  37.7 0.0 collective-permute-start.16
  37.7 2.0 %collective-permute-done.15.refs_3_ = bf16[352,128]{1,0:T(8,128)(2,1)S(1)} collective-permute-done((bf16[352,128]{1,0:T(8,128)(2,1)S(1)}, bf16[352,128]{1,0:T(8,128)(2,1)S(1)}, u32[]{:S(2)}, u32[]{:S(2)}) %collective-permute-start.15) | collective-permute-done | bytes 90144 | tf_op jit(solution)/shard_map/ppermute | solution.py:84
  39.7 0.0 collective-permute-start.19
  39.7 1.9 %collective-permute-done.13.refs_1_ = bf16[352,128]{1,0:T(8,128)(2,1)S(1)} collective-permute-done((bf16[352,128]{1,0:T(8,128)(2,1)S(1)}, bf16[352,128]{1,0:T(8,128)(2,1)S(1)}, u32[]{:S(2)}, u32[]{:S(2)}) %collective-permute-start.13) | collective-permute-done | bytes 90144 | tf_op jit(solution)/shard_map/ppermute | solution.py:84
  41.6 0.0 collective-permute-start.17
  41.6 0.2 collective-permute-done.14.refs_2_
  41.8 0.3 collective-permute-start.18
  42.1 0.0 collective-permute-done.16.refs_4_
  42.1 0.0 collective-permute-done.19.refs_7_
  42.1 0.8 %collective-permute-done.17.refs_5_ = bf16[352,128]{1,0:T(8,128)(2,1)S(1)} collective-permute-done((bf16[352,128]{1,0:T(8,128)(2,1)S(1)}, bf16[352,128]{1,0:T(8,128)(2,1)S(1)}, u32[]{:S(2)}, u32[]{:S(2)}) %collective-permute-start.17) | collective-permute-done | bytes 90144 | tf_op jit(solution)/shard_map/ppermute | solution.py:81
  42.9 0.2 collective-permute-done.18.refs_6_
  43.1 2.8 %update.1 = (f32[1,128]{1,0:T(1,128)}, f32[512,512]{1,0:T(8,128)}, f32[512,512]{1,0:T(8,128)}, f32[512,512]{1,0:T(8,128)}, bf16[512,512]{1,0:T(8,128)(2,1)}, /*i...) custom-call(bf16[352,128]{1,0:T(8,128)(2,1)S(1)} %get-tuple-element., ...), custom_call_target="tpu_custom_call" | custom-call | tf_op jit(solution)/shard_map/update/pallas_call | solution.py:46
  (19 shorter events, 0.1 us)
Async XLA Ops:
  0.7 5.8 %copy-start.12 = (f32[1,128]{1,0:T(1,128)S(1)}, f32[1,128]{1,0:T(1,128)}, u32[]{:S(2)}) copy-start(f32[1,128]{1,0:T(1,128)} %bias_ref.3) | copy-start | bytes 1540
  0.7 10.0 %collective-permute-start.2 = (bf16[64,512]{1,0:T(8,128)(2,1)}, bf16[64,512]{1,0:T(8,128)(2,1)S(1)}, u32[]{:S(2)}, u32[]{:S(2)}) collective-permute-start(bf16[64,512]{1,0:T(8,128)(2,1)} %refs_0_.3), channel_id=1, source_target_pairs={{0,6},{1,7},{2,4},{3,5},{4,2},{5,3},{6,0},{7,1},{8,14},{9,15},{10,... | collective-permute-start | bytes 196616 | tf_op jit(solution)/shard_map/ppermute | solution.py:87
  5.8 5.8 %collective-permute-start.1 = (bf16[64,512]{1,0:T(8,128)(2,1)}, bf16[64,512]{1,0:T(8,128)(2,1)S(1)}, u32[]{:S(2)}, u32[]{:S(2)}) collective-permute-start(bf16[64,512]{1,0:T(8,128)(2,1)} %refs_0_.3), channel_id=1, source_target_pairs={{0,4},{1,5},{2,6},{3,7},{4,0},{5,1},{6,2},{7,3},{8,12},{9,13},{10,... | collective-permute-start | bytes 196616 | tf_op jit(solution)/shard_map/ppermute | solution.py:87
  5.8 5.8 %collective-permute-start = (bf16[64,512]{1,0:T(8,128)(2,1)}, bf16[64,512]{1,0:T(8,128)(2,1)S(1)}, u32[]{:S(2)}, u32[]{:S(2)}) collective-permute-start(bf16[64,512]{1,0:T(8,128)(2,1)} %refs_0_.3), channel_id=1, source_target_pairs={{0,2},{1,3},{2,0},{3,1},{4,6},{5,7},{6,4},{7,5},{8,10},{9,11},{10,... | collective-permute-start | bytes 196616 | tf_op jit(solution)/shard_map/ppermute | solution.py:87
  6.4 1.0 %copy-start.2 = (f32[1,512,128]{2,1,0:T(8,128)S(1)}, f32[1,512,128]{2,1,0:T(8,128)}, u32[]{:S(2)}) copy-start(f32[1,512,128]{2,1,0:T(8,128)} %param.22) | copy-start | bytes 786436
  7.4 1.8 %copy-start.15 = (s32[512]{0:T(512)S(1)}, s32[512]{0:T(512)}, u32[]{:S(2)}) copy-start(s32[512]{0:T(512)} %param.15) | copy-start | bytes 6148
  7.4 1.9 %copy-start.13 = (f32[1,128]{1,0:T(1,128)S(1)}, f32[1,128]{1,0:T(1,128)}, u32[]{:S(2)}) copy-start(f32[1,128]{1,0:T(1,128)} %first_ref.1) | copy-start | bytes 1540
  7.4 1.9 %copy-start.14 = (f32[1,128]{1,0:T(1,128)S(1)}, f32[1,128]{1,0:T(1,128)}, u32[]{:S(2)}) copy-start(f32[1,128]{1,0:T(1,128)} %second_ref.1) | copy-start | bytes 1540
  7.4 5.1 %collective-permute-start.3 = (bf16[528,128]{1,0:T(8,128)(2,1)S(1)}, bf16[528,128]{1,0:T(8,128)(2,1)S(1)}, u32[]{:S(2)}, u32[]{:S(2)}) collective-permute-start(bf16[528,128]{1,0:T(8,128)(2,1)S(1)} %head_low.1.refs_7_), channel_id=1, source_target_pairs={{0,1},{1,0},{2,3},{3,2},{4,5},{5,4},{6,7},{7,6},{8,9},{9,8},{10,11... | collective-permute-start | bytes 405512 | tf_op jit(solution)/shard_map/ppermute | solution.py:84
  9.3 1.2 %copy-start = (f32[512,512]{1,0:T(8,128)S(1)}, f32[512,512]{1,0:T(8,128)}, u32[]{:S(2)}) copy-start(f32[512,512]{1,0:T(8,128)} %refs_8_.1) | copy-start | bytes 3145732
  10.6 1.0 %copy-start.6 = (f32[3,8,512]{2,1,0:T(8,128)S(1)}, f32[3,8,512]{2,1,0:T(8,128)}, u32[]{:S(2)}) copy-start(f32[3,8,512]{2,1,0:T(8,128)} %refs_11_.1) | copy-start | bytes 147460
  10.6 1.0 %copy-start.7 = (bf16[64,512]{1,0:T(8,128)(2,1)S(1)}, bf16[64,512]{1,0:T(8,128)(2,1)}, u32[]{:S(2)}) copy-start(bf16[64,512]{1,0:T(8,128)(2,1)} %refs_0_.3) | copy-start | bytes 196612
  12.5 30.5 %copy-start.5 = (f32[512,512]{1,0:T(8,128)S(1)}, f32[512,512]{1,0:T(8,128)}, u32[]{:S(2)}) copy-start(f32[512,512]{1,0:T(8,128)} %refs_10_.1) | copy-start | bytes 3145732
  12.5 30.5 %copy-start.10 = (f32[3,8,512]{2,1,0:T(8,128)S(1)}, f32[3,8,512]{2,1,0:T(8,128)}, u32[]{:S(2)}) copy-start(f32[3,8,512]{2,1,0:T(8,128)} %refs_12_.1) | copy-start | bytes 147460
  12.5 30.5 %copy-start.11 = (f32[3,8,512]{2,1,0:T(8,128)S(1)}, f32[3,8,512]{2,1,0:T(8,128)}, u32[]{:S(2)}) copy-start(f32[3,8,512]{2,1,0:T(8,128)} %refs_13_.1) | copy-start | bytes 147460
  14.4 1.8 %collective-permute-start.4 = (bf16[4,400,128]{2,1,0:T(8,128)(2,1)S(1)}, bf16[4,400,128]{2,1,0:T(8,128)(2,1)S(1)}, u32[]{:S(2)}, u32[]{:S(2)}) collective-permute-start(bf16[4,400,128]{2,1,0:T(8,128)(2,1)S(1)} %get-tuple-element.69), channel_id=1, source_target_pairs={{0,8},{1,9},{2,10},{3,11},{4,12},{5,13},{6,14},{7,15},{8,0},{9,1},... | collective-permute-start | bytes 1228808 | tf_op jit(solution)/shard_map/ppermute | solution.py:81
  14.4 6.6 %collective-permute-start.5 = (bf16[128,640]{1,0:T(8,128)(2,1)S(1)}, bf16[128,640]{1,0:T(8,128)(2,1)S(1)}, u32[]{:S(2)}, u32[]{:S(2)}) collective-permute-start(bf16[128,640]{1,0:T(8,128)(2,1)S(1)} %get-tuple-element.72), channel_id=1, source_target_pairs={{0,2},{1,3},{2,0},{3,1},{4,6},{5,7},{6,4},{7,5},{8,10},{9,11},{10,... | collective-permute-start | bytes 491528 | tf_op jit(solution)/shard_map/ppermute | solution.py:87
  16.2 26.9 %copy-start.4 = (f32[512,512]{1,0:T(8,128)S(1)}, f32[512,512]{1,0:T(8,128)}, u32[]{:S(2)}) copy-start(f32[512,512]{1,0:T(8,128)} %refs_9_.1) | copy-start | bytes 3145732
  16.2 26.9 %copy-start.9 = (f32[1,512,128]{2,1,0:T(8,128)S(1)}, f32[1,512,128]{2,1,0:T(8,128)}, u32[]{:S(2)}) copy-start(f32[1,512,128]{2,1,0:T(8,128)} %param.24) | copy-start | bytes 786436
  16.3 26.8 %copy-start.1 = (f32[512,512]{1,0:T(8,128)S(1)}, f32[512,512]{1,0:T(8,128)}, u32[]{:S(2)}) copy-start(f32[512,512]{1,0:T(8,128)} %refs_8_.1) | copy-start | bytes 3145732
  16.3 7.4 %collective-permute-start.6 = (bf16[400,128]{1,0:T(8,128)(2,1)S(1)}, bf16[400,128]{1,0:T(8,128)(2,1)S(1)}, u32[]{:S(2)}, u32[]{:S(2)}) collective-permute-start(bf16[400,128]{1,0:T(8,128)(2,1)S(1)} %get-tuple-element.76), channel_id=1, source_target_pairs={{0,17},{1,16},{2,19},{3,18},{4,21},{5,20},{6,23},{7,22},{8,25},{9,... | collective-permute-start | bytes 307208 | tf_op jit(solution)/shard_map/ppermute | solution.py:84
  18.9 5.6 %collective-permute-start.7 = (bf16[400,128]{1,0:T(8,128)(2,1)S(1)}, bf16[400,128]{1,0:T(8,128)(2,1)S(1)}, u32[]{:S(2)}, u32[]{:S(2)}) collective-permute-start(bf16[400,128]{1,0:T(8,128)(2,1)S(1)} %get-tuple-element.77), channel_id=1, source_target_pairs={{0,16},{1,17},{2,18},{3,19},{4,20},{5,21},{6,22},{7,23},{8,24},{9,... | collective-permute-start | bytes 307208 | tf_op jit(solution)/shard_map/ppermute | solution.py:84
  19.5 5.1 %collective-permute-start.8 = (bf16[400,128]{1,0:T(8,128)(2,1)S(1)}, bf16[400,128]{1,0:T(8,128)(2,1)S(1)}, u32[]{:S(2)}, u32[]{:S(2)}) collective-permute-start(bf16[400,128]{1,0:T(8,128)(2,1)S(1)} %get-tuple-element.78), channel_id=1, source_target_pairs={{0,1},{1,0},{2,3},{3,2},{4,5},{5,4},{6,7},{7,6},{8,9},{9,8},{10,11... | collective-permute-start | bytes 307208 | tf_op jit(solution)/shard_map/ppermute | solution.py:84
  21.1 8.0 %collective-permute-start.12 = (bf16[64,640]{1,0:T(8,128)(2,1)S(1)}, bf16[64,640]{1,0:T(8,128)(2,1)S(1)}, u32[]{:S(2)}, u32[]{:S(2)}) collective-permute-start(bf16[64,640]{1,0:T(8,128)(2,1)S(1)} %get-tuple-element.81), channel_id=1, source_target_pairs={{0,4},{1,5},{2,6},{3,7},{4,0},{5,1},{6,2},{7,3},{8,12},{9,13},{10,... | collective-permute-start | bytes 245768 | tf_op jit(solution)/shard_map/ppermute | solution.py:87
  24.7 6.8 %collective-permute-start.11 = (bf16[272,128]{1,0:T(8,128)(2,1)S(1)}, bf16[272,128]{1,0:T(8,128)(2,1)S(1)}, u32[]{:S(2)}, u32[]{:S(2)}) collective-permute-start(bf16[272,128]{1,0:T(8,128)(2,1)S(1)} %get-tuple-element.79), channel_id=1, source_target_pairs={{0,6},{1,7},{2,4},{3,5},{4,2},{5,3},{6,0},{7,1},{8,14},{9,15},{10,... | collective-permute-start | bytes 208904 | tf_op jit(solution)/shard_map/ppermute | solution.py:87
  28.3 5.7 %collective-permute-start.10 = (bf16[272,128]{1,0:T(8,128)(2,1)S(1)}, bf16[272,128]{1,0:T(8,128)(2,1)S(1)}, u32[]{:S(2)}, u32[]{:S(2)}) collective-permute-start(bf16[272,128]{1,0:T(8,128)(2,1)S(1)} %get-tuple-element.79), channel_id=1, source_target_pairs={{0,4},{1,5},{2,6},{3,7},{4,0},{5,1},{6,2},{7,3},{8,12},{9,13},{10,... | collective-permute-start | bytes 208904 | tf_op jit(solution)/shard_map/ppermute | solution.py:87
  28.3 5.7 %collective-permute-start.9 = (bf16[272,128]{1,0:T(8,128)(2,1)S(1)}, bf16[272,128]{1,0:T(8,128)(2,1)S(1)}, u32[]{:S(2)}, u32[]{:S(2)}) collective-permute-start(bf16[272,128]{1,0:T(8,128)(2,1)S(1)} %get-tuple-element.79), channel_id=1, source_target_pairs={{0,2},{1,3},{2,0},{3,1},{4,6},{5,7},{6,4},{7,5},{8,10},{9,11},{10,... | collective-permute-start | bytes 208904 | tf_op jit(solution)/shard_map/ppermute | solution.py:87
  29.1 14.0 %copy-start.8 = (f32[1,512,128]{2,1,0:T(8,128)S(1)}, f32[1,512,128]{2,1,0:T(8,128)}, u32[]{:S(2)}) copy-start(f32[1,512,128]{2,1,0:T(8,128)} %param.23) | copy-start | bytes 786436
  29.8 13.3 %copy-start.3 = (f32[1,512,128]{2,1,0:T(8,128)S(1)}, f32[1,512,128]{2,1,0:T(8,128)}, u32[]{:S(2)}) copy-start(f32[1,512,128]{2,1,0:T(8,128)} %param.22) | copy-start | bytes 786436
  34.1 5.6 %collective-permute-start.15 = (bf16[352,128]{1,0:T(8,128)(2,1)S(1)}, bf16[352,128]{1,0:T(8,128)(2,1)S(1)}, u32[]{:S(2)}, u32[]{:S(2)}) collective-permute-start(bf16[352,128]{1,0:T(8,128)(2,1)S(1)} %get-tuple-element.92), channel_id=1, source_target_pairs={{0,17},{1,16},{2,19},{3,18},{4,21},{5,20},{6,23},{7,22},{8,25},{9,... | collective-permute-start | bytes 270344 | tf_op jit(solution)/shard_map/ppermute | solution.py:84
  36.8 4.8 %collective-permute-start.13 = (bf16[352,128]{1,0:T(8,128)(2,1)S(1)}, bf16[352,128]{1,0:T(8,128)(2,1)S(1)}, u32[]{:S(2)}, u32[]{:S(2)}) collective-permute-start(bf16[352,128]{1,0:T(8,128)(2,1)S(1)} %get-tuple-element.92), channel_id=1, source_target_pairs={{0,1},{1,0},{2,3},{3,2},{4,5},{5,4},{6,7},{7,6},{8,9},{9,8},{10,11... | collective-permute-start | bytes 270344 | tf_op jit(solution)/shard_map/ppermute | solution.py:84
  37.2 4.6 %collective-permute-start.14 = (bf16[352,128]{1,0:T(8,128)(2,1)S(1)}, bf16[352,128]{1,0:T(8,128)(2,1)S(1)}, u32[]{:S(2)}, u32[]{:S(2)}) collective-permute-start(bf16[352,128]{1,0:T(8,128)(2,1)S(1)} %get-tuple-element.91.refs_0_), channel_id=1, source_target_pairs={{0,16},{1,17},{2,18},{3,19},{4,20},{5,21},{6,22},{7,23},{8,24},{9,... | collective-permute-start | bytes 270344 | tf_op jit(solution)/shard_map/ppermute | solution.py:84
  37.7 4.4 %collective-permute-start.16 = (bf16[352,128]{1,0:T(8,128)(2,1)S(1)}, bf16[352,128]{1,0:T(8,128)(2,1)S(1)}, u32[]{:S(2)}, u32[]{:S(2)}) collective-permute-start(bf16[352,128]{1,0:T(8,128)(2,1)S(1)} %get-tuple-element.91.refs_0_), channel_id=1, source_target_pairs={{0,8},{1,9},{2,10},{3,11},{4,12},{5,13},{6,14},{7,15},{8,0},{9,1},... | collective-permute-start | bytes 270344 | tf_op jit(solution)/shard_map/ppermute | solution.py:81
  39.7 2.4 %collective-permute-start.19 = (bf16[352,128]{1,0:T(8,128)(2,1)S(1)}, bf16[352,128]{1,0:T(8,128)(2,1)S(1)}, u32[]{:S(2)}, u32[]{:S(2)}) collective-permute-start(bf16[352,128]{1,0:T(8,128)(2,1)S(1)} %collective-permute-done.15.refs_3_), channel_id=1, source_target_pairs={{0,8},{1,9},{2,10},{3,11},{4,12},{5,13},{6,14},{7,15},{8,0},{9,1},... | collective-permute-start | bytes 270344 | tf_op jit(solution)/shard_map/ppermute | solution.py:81
  41.6 1.3 %collective-permute-start.17 = (bf16[352,128]{1,0:T(8,128)(2,1)S(1)}, bf16[352,128]{1,0:T(8,128)(2,1)S(1)}, u32[]{:S(2)}, u32[]{:S(2)}) collective-permute-start(bf16[352,128]{1,0:T(8,128)(2,1)S(1)} %collective-permute-done.13.refs_1_), channel_id=1, source_target_pairs={{0,8},{1,9},{2,10},{3,11},{4,12},{5,13},{6,14},{7,15},{8,0},{9,1},... | collective-permute-start | bytes 270344 | tf_op jit(solution)/shard_map/ppermute | solution.py:81
  41.8 1.3 %collective-permute-start.18 = (bf16[352,128]{1,0:T(8,128)(2,1)S(1)}, bf16[352,128]{1,0:T(8,128)(2,1)S(1)}, u32[]{:S(2)}, u32[]{:S(2)}) collective-permute-start(bf16[352,128]{1,0:T(8,128)(2,1)S(1)} %collective-permute-done.14.refs_2_), channel_id=1, source_target_pairs={{0,8},{1,9},{2,10},{3,11},{4,12},{5,13},{6,14},{7,15},{8,0},{9,1},... | collective-permute-start | bytes 270344 | tf_op jit(solution)/shard_map/ppermute | solution.py:81
